TPU v7x, 32 devices: a whole 2x2x4 slice. The times are simulated.
32 devices in a mesh: wa: 8 (over z, x), col: 4 (over y, core).
Axes of the slice: x: 2, y: 2, z: 4, core: 2. Of those that a mesh axis runs over, the one named last changes fastest.
Arguments:
- tokens: bfloat16 [4, 8, 512, 768], P('col', None, 'wa'), may hold values from -6 to 6
- tap: bfloat16 [4, 8, 512, 768], P('col', None, 'wa'), may hold values from -6 to 6
- ln1_gain: bfloat16 [768], P(('wa', 'col')), may hold values from 0.5 to 1.5
- ln1_bias: bfloat16 [768], P(('wa', 'col')), may hold values from -3 to 3
- qkv_weight: bfloat16 [768, 2304], P(('wa', 'col')), may hold values from -0.21875 to 0.21875
- query_bias: bfloat16 [768], P(('wa', 'col')), may hold values from -3 to 3
- value_bias: bfloat16 [768], P(('wa', 'col')), may hold values from -3 to 3
- out_weight: bfloat16 [768, 768], P(('wa', 'col')), may hold values from -0.875 to 0.875
- out_bias: bfloat16 [768], P(('wa', 'col')), may hold values from -3 to 3
- ln2_gain: bfloat16 [768], P(('wa', 'col')), may hold values from 0.5 to 1.5
- ln2_bias: bfloat16 [768], P(('wa', 'col')), may hold values from -3 to 3
- fc1_weight: bfloat16 [768, 3072], P(('wa', 'col')), may hold values from -0.21875 to 0.21875
- fc1_bias: bfloat16 [3072], P(('wa', 'col')), may hold values from -3 to 3
- fc2_weight: bfloat16 [3072, 768], P(('wa', 'col')), may hold values from -0.109375 to 0.109375
- fc2_bias: bfloat16 [768], P(('wa', 'col')), may hold values from -3 to 3
- block_up: bfloat16 [768, 1024], P(('wa', 'col')), may hold values from -0.21875 to 0.21875
- tap_up: bfloat16 [768, 1024], P(('wa', 'col')), may hold values from -0.21875 to 0.21875
- conv1_weight: bfloat16 [27, 128, 256], P(None, 'col'), may hold values from -0.078125 to 0.078125
- conv2_weight: bfloat16 [27, 128, 128], P(None, 'col'), may hold values from -0.109375 to 0.109375
- skip_weight: bfloat16 [128, 256], P('col'), may hold values from -0.375 to 0.375
- cotangent: bfloat16 [4, 8, 128, 4096], P(None, 'wa', 'col'), may hold values from -6 to 6
Outputs:
- section_out: bfloat16 [4, 8, 128, 4096], P(None, 'wa', 'col')
- input_grad: float32 [4, 8, 512, 768], P('col', None, 'wa')
- tap_grad: float32 [4, 8, 512, 768], P('col', None, 'wa')
- grad_ln1_gain: float32 [768], P(('wa', 'col'))
- grad_ln1_bias: float32 [768], P(('wa', 'col'))
- grad_qkv_weight: float32 [768, 2304], P(('wa', 'col'))
- grad_query_bias: float32 [768], P(('wa', 'col'))
- grad_value_bias: float32 [768], P(('wa', 'col'))
- grad_out_weight: float32 [768, 768], P(('wa', 'col'))
- grad_out_bias: float32 [768], P(('wa', 'col'))
- grad_ln2_gain: float32 [768], P(('wa', 'col'))
- grad_ln2_bias: float32 [768], P(('wa', 'col'))
- grad_fc1_weight: float32 [768, 3072], P(('wa', 'col'))
- grad_fc1_bias: float32 [3072], P(('wa', 'col'))
- grad_fc2_weight: float32 [3072, 768], P(('wa', 'col'))
- grad_fc2_bias: float32 [768], P(('wa', 'col'))
- grad_block_up: float32 [768, 1024], P(('wa', 'col'))
- grad_tap_up: float32 [768, 1024], P(('wa', 'col'))
- grad_conv1_weight: float32 [27, 128, 256], P(None, 'col')
- grad_conv2_weight: float32 [27, 128, 128], P(None, 'col')
- grad_skip_weight: float32 [128, 256], P('col')
All inputs are finite; a program needn't handle non-finite values.
Results may differ from a plain program's by a relative error of at most 0.028.
Values may be sent and summed in bfloat16 or wider, within the bound.
No kernel may reach another device: no remote copies, remote signals or barrier semaphores. Data moves between devices by JAX's collectives and lax.ppermute only.
A program may use at most 320 MiB of HBM per device.

v0:
```python
import jax
import jax.numpy as jnp
from jax import lax
from jax.experimental import pallas as pl
from jax.experimental.pallas import tpu as pltpu
from jax.sharding import Mesh, PartitionSpec as P

D = 768
HEADS = 12
HEAD_DIM = 64
MLP = 3072
DEC = 128
GRID = 8
PATCHES = 512
SIDE = 16
VOX = 4096
PLANE = SIDE * SIDE
BF = jnp.bfloat16
F32 = jnp.float32
VMEM_BYTES = 56 * 2**20
COST = 3 * 10**10


def cut_axis(devices, label):
    places = [getattr(item, "coords", None) for item in devices]
    if len(devices) == 1 or any(place is None for place in places):
        return [(label, len(devices), False)]
    full = [tuple(item.coords) + (item.core_on_chip,) for item in devices]
    found = []
    for axis in range(4):
        values = [place[axis] for place in full]
        if len(set(values)) > 1:
            stride = next(k for k in range(len(values)) if values[k] != values[0])
            found.append((stride, len(set(values)), axis))
    found.sort(reverse=True)
    step = 1
    for stride, size, _ in reversed(found):
        if stride != step:
            return [(label, len(devices), False)]
        step *= size
    if step != len(devices):
        return [(label, len(devices), False)]
    return [(label + "xyzc"[axis], size, axis == 3) for _, size, axis in found]


class Axes:
    def __init__(self, mesh):
        grid = mesh.devices
        wa = cut_axis(list(grid[:, 0]), "wa")
        col = cut_axis(list(grid[0, :]), "col")
        parts = wa + col
        self.sizes = {name: size for name, size, _ in parts}
        self.names = tuple(self.sizes)
        self.wa = tuple(name for name, _, _ in wa)
        self.col = tuple(name for name, _, _ in col)
        self.wa_count, self.col_count = grid.shape
        self.mesh = Mesh(grid.reshape(tuple(self.sizes.values())), self.names)
        core = [name for name, _, is_core in parts if is_core]
        links = [name for name, _, is_core in parts if not is_core]
        links.sort(key=lambda name: -self.sizes[name])
        self.core = core[0] if core else None
        self.links_a = tuple(links)
        if len(links) > 2:
            links = links[:-2] + [links[-1], links[-2]]
        self.links_b = tuple(links)

    def inside(self, names):
        return [n for n in self.links_a if n in names] + [n for n in (self.core,) if n in names]


def swap(value, axis):
    return lax.ppermute(value, axis, [(0, 1), (1, 0)])


def turn(value, axis, size, step):
    return lax.ppermute(value, axis, [(k, (k + step) % size) for k in range(size)])


def gather_axis(value, axis, size):
    place = lax.axis_index(axis)
    if size == 2:
        mine, other = value[None], swap(value, axis)[None]
        return jnp.where(
            place == 0,
            jnp.concatenate([mine, other]),
            jnp.concatenate([other, mine]),
        )
    got = [turn(value, axis, size, step) for step in range(1, size)]
    out = jnp.zeros((size,) + value.shape, value.dtype)
    out = lax.dynamic_update_index_in_dim(out, value, place, 0)
    for step in range(1, size):
        out = lax.dynamic_update_index_in_dim(out, got[step - 1], (place - step) % size, 0)
    return out


def keep_order(first, second, place, axis):
    return jnp.where(
        place == 0,
        jnp.concatenate([first, second], axis),
        jnp.concatenate([second, first], axis),
    )


def column_half(value, place):
    half = value.shape[-1] // 2
    return lax.dynamic_slice_in_dim(value, place * half, half, value.ndim - 1)


def gather_dims(value, order, names):
    dims, inner = [], value.ndim
    for name in order:
        value = gather_axis(value, name, lax.axis_size(name))
        dims.insert(0, name)
    kept = [name for name in names if name in dims]
    return value.transpose([dims.index(n) for n in kept] + [len(dims) + k for k in range(inner)])


class RowGather:
    def __init__(self, value, links, axes):
        self.axes, self.left, self.dims = axes, list(links), []
        place = lax.axis_index(axes.core)
        mine, other = column_half(value, place), column_half(value, 1 - place)
        self.value = keep_order(mine[None], swap(other, axes.core)[None], place, 0)

    def link(self):
        name = self.left.pop(0)
        self.value = gather_axis(self.value, name, lax.axis_size(name))
        self.dims.insert(0, name)

    def rows(self):
        axes, value = self.axes, self.value
        kept = [name for name in axes.names if name in self.dims]
        count = len(kept)
        value = value.transpose([self.dims.index(n) for n in kept] + [count, count + 1, count + 2])
        value = jnp.moveaxis(value, count, axes.names.index(axes.core))
        return value.reshape(-1, value.shape[-1])

    def finish(self, half):
        place = lax.axis_index(self.axes.core)
        return keep_order(half, swap(half, self.axes.core), place, 1)


def wait_for(value, *others):
    return lax.optimization_barrier((value, *others))[0]


def corner(value):
    return value.reshape(-1, value.shape[-1])[:16, :128]


def scatter_axis(value, axis, dim):
    size, place = lax.axis_size(axis), lax.axis_index(axis)
    got = [
        turn(lax.dynamic_index_in_dim(value, (place + step) % size, dim, False), axis, size, step)
        for step in range(1, size)
    ]
    total = lax.dynamic_index_in_dim(value, place, dim, False).astype(F32)
    for item in got:
        total = total + item.astype(F32)
    return total


def scatter_dims(value, order, names):
    dims = [name for name in names if name in order]
    for name in order:
        dim = dims.index(name)
        dims.pop(dim)
        value = scatter_axis(value.astype(BF), name, dim)
    return value


class RowSum:
    def __init__(self, keep, send, links, axes):
        self.axes, self.left = axes, list(reversed(links))
        self.dims = list(axes.names)
        got = swap(send, axes.core)
        self.value = (keep.astype(F32) + got.astype(F32)).astype(BF)
        columns = keep.shape[1]
        self.value = self.value.reshape([lax.axis_size(n) for n in self.dims] + [-1, columns])

    def link(self):
        name = self.left.pop(0)
        dim = self.dims.index(name)
        self.dims.pop(dim)
        self.value = scatter_axis(self.value, name, dim)
        if self.left:
            self.value = self.value.astype(BF)

    def finish(self):
        axes = self.axes
        place = lax.axis_index(axes.core)
        mine = lax.dynamic_index_in_dim(self.value, place, 0, False)
        other = lax.dynamic_index_in_dim(self.value, 1 - place, 0, False).astype(BF)
        return keep_order(mine, swap(other, axes.core).astype(F32), place, 1)


def swap_blocks(value, axes):
    return lax.all_to_all(value, axes, 0, 0, tiled=True)


def product(left, right):
    return jnp.dot(left, right, preferred_element_type=F32)


def product_rows(left, right):
    return lax.dot_general(left, right, (((0,), (0,)), ((), ())), preferred_element_type=F32)


def product_back(left, right):
    return lax.dot_general(left, right, (((1,), (1,)), ((), ())), preferred_element_type=F32)


def row_norm(values, epsilon):
    center = values - jnp.mean(values, axis=-1, keepdims=True)
    factor = lax.rsqrt(jnp.mean(center * center, axis=-1, keepdims=True) + epsilon)
    return (center * factor, factor)


def row_norm_back(upstream, normed, factor):
    middle = upstream - jnp.mean(upstream, axis=-1, keepdims=True)
    return factor * (middle - normed * jnp.mean(upstream * normed, axis=-1, keepdims=True))


def unit_matrix(size):
    here = lax.broadcasted_iota(jnp.int32, (size, size), 0)
    there = lax.broadcasted_iota(jnp.int32, (size, size), 1)
    return (here == there).astype(F32).astype(BF)


def turned(value, unit):
    return product_back(unit, value).astype(BF)


def head_masks():
    lane = lax.broadcasted_iota(jnp.int32, (PATCHES, 2 * HEAD_DIM), 1)
    return [(lane < HEAD_DIM).astype(F32).astype(BF), (lane >= HEAD_DIM).astype(F32).astype(BF)]


def low_lanes(shape):
    return lax.broadcasted_iota(jnp.int32, shape, 1) < HEAD_DIM


def attention_kernel(
    rows_ref, weight_ref,
    input_one_ref, qkv_ref, probs_ref, attn_ref, first_ref, input_two_ref, vectors_ref,
):
    rows = rows_ref[...].astype(F32)
    unit = unit_matrix(2 * HEAD_DIM)
    vectors_ref[...] = product_back(unit, weight_ref[:, 4 * D : 4 * D + DEC])[:16]
    gain_one, bias_one, query_bias, value_bias, out_shift, gain_two, bias_two = (
        vectors_ref[k : k + 1] for k in range(7)
    )
    normed, _ = row_norm(rows, 1e-06)
    input_one_ref[...] = (normed * gain_one + bias_one).astype(BF)
    for block, bias in enumerate((query_bias, None, value_bias)):
        columns = slice(block * D, (block + 1) * D)
        value = product(input_one_ref[...], weight_ref[:, columns])
        qkv_ref[:, columns] = (value if bias is None else value + bias).astype(BF)
    masks, wide_unit = head_masks(), unit_matrix(PATCHES)

    def pair_step(pair, _):
        at = pl.multiple_of(pair * 2 * HEAD_DIM, 2 * HEAD_DIM)
        columns = pl.ds(at, 2 * HEAD_DIM)
        queries = qkv_ref[:, columns]
        keys = qkv_ref[:, pl.ds(at + D, 2 * HEAD_DIM)]
        values = turned(qkv_ref[:, pl.ds(at + 2 * D, 2 * HEAD_DIM)], unit)
        mixed = []
        for head in range(2):
            scores = product_back(keys * masks[head], queries) * 0.125
            expo = jnp.exp(scores - jnp.max(scores, axis=0, keepdims=True))
            probs = (expo * (1.0 / jnp.sum(expo, axis=0, keepdims=True))).astype(BF)
            probs_ref[2 * pair + head] = probs
            part = product(values[head * HEAD_DIM : (head + 1) * HEAD_DIM], probs)
            mixed.append(part.astype(BF))
        attn_ref[:, columns] = product_back(wide_unit, jnp.concatenate(mixed)).astype(BF)

    lax.fori_loop(0, HEADS // 2, pair_step, None, unroll=PAIRS)
    first = rows + product(attn_ref[...], weight_ref[:, 3 * D : 4 * D]) + out_shift
    first_ref[...] = first
    normed, _ = row_norm(first, 1e-06)
    input_two_ref[...] = (normed * gain_two + bias_two).astype(BF)


CHUNK = 512


def mlp_kernel(
    input_ref, first_ref, fc1_ref, fc2_ref, fc1_shift_ref, fc2_shift_ref,
    active_ref, slope_ref, out_ref,
):
    total = first_ref[...] + fc2_shift_ref[...]
    for at in range(0, MLP, CHUNK):
        columns = slice(at, at + CHUNK)
        hidden = product(input_ref[...], fc1_ref[:, columns]) + fc1_shift_ref[:, columns]
        below = 0.5 * (1.0 + lax.erf(hidden * 0.7071067811865476))
        slope = below + hidden * (0.3989422804014327 * jnp.exp(-0.5 * hidden * hidden))
        slope_ref[:, columns] = slope.astype(BF)
        active_ref[:, columns] = (hidden * below).astype(BF)
        total = total + product(active_ref[:, columns], fc2_ref[columns])
    out_ref[...] = total.astype(BF)


def cut_columns(ref, place):
    half = ref.shape[1] // 2
    keep = pl.ds(pl.multiple_of(place * half, DEC), half)
    send = pl.ds(pl.multiple_of((1 - place) * half, DEC), half)
    return (keep, send)


def up_back_kernel(
    grad_block_ref, grad_tap_ref, block_ref, tap_ref, up_ref,
    grad_up_ref, grad_rows_ref, grad_second_ref, grad_mlp_ref, sums_ref,
):
    unit = unit_matrix(PLANE)
    for source, (grad_ref, rows_ref) in enumerate(
        ((grad_block_ref, block_ref), (grad_tap_ref, tap_ref))
    ):
        columns = slice(source * 8 * DEC, (source + 1) * 8 * DEC)
        for at in range(0, D, PLANE):
            rows = slice(at, at + PLANE)
            left = turned(rows_ref[:, rows], unit)
            grad_up_ref[rows, columns] = product(left, grad_ref[...]).astype(BF)
        back = product_back(grad_ref[...], up_ref[:, columns])
        if source == 0:
            grad_second_ref[...] = back
            grad_mlp_ref[...] = back.astype(BF)
            sums_ref[...] = column_sum(back.astype(BF).astype(F32))
        else:
            grad_rows_ref[...] = back.astype(BF)


def fc2_back_kernel(
    place_ref, grad_mlp_ref, active_ref, slope_ref, fc2_ref,
    keep_ref, send_ref, grad_hidden_ref, sums_ref,
):
    unit = unit_matrix(PLANE)
    keep, send = cut_columns(grad_mlp_ref, place_ref[0])
    for at in range(0, MLP, PLANE):
        rows = slice(at, at + PLANE)
        left = turned(active_ref[:, rows], unit)
        send_ref[rows] = product(left, grad_mlp_ref[:, send]).astype(BF)
        keep_ref[rows] = product(left, grad_mlp_ref[:, keep]).astype(BF)
    for at in range(0, MLP, CHUNK):
        rows = slice(at, at + CHUNK)
        grad = product_back(grad_mlp_ref[...], fc2_ref[rows]) * slope_ref[:, rows].astype(F32)
        grad = grad.astype(BF)
        grad_hidden_ref[:, rows] = grad
        sums_ref[:, rows] = column_sum(grad.astype(F32))


def fc1_back_kernel(
    place_ref, grad_hidden_ref, input_ref, first_ref, grad_second_ref, fc1_ref, weight_ref,
    vectors_ref,
    keep_ref, send_ref, grad_first_ref, grad_attn_ref, grad_mixed_ref, sums_ref,
):
    unit = unit_matrix(PLANE)
    keep, send = cut_columns(grad_hidden_ref, place_ref[0])
    for at in range(0, D, PLANE):
        rows = slice(at, at + PLANE)
        left = turned(input_ref[:, rows], unit)
        send_ref[rows] = product(left, grad_hidden_ref[:, send]).astype(BF)
        keep_ref[rows] = product(left, grad_hidden_ref[:, keep]).astype(BF)
    grad = product_back(grad_hidden_ref[...], fc1_ref[...])
    normed, factor = row_norm(first_ref[...], 1e-06)
    sums_ref[0:1] = column_sum(grad * normed)
    sums_ref[1:2] = column_sum(grad)
    grad = grad_second_ref[...] + row_norm_back(grad * vectors_ref[5:6], normed, factor)
    grad_first_ref[...] = grad
    grad = grad.astype(BF)
    grad_attn_ref[...] = grad
    sums_ref[2:3] = column_sum(grad.astype(F32))
    grad_mixed_ref[...] = product_back(grad, weight_ref[:, 3 * D : 4 * D]).astype(BF)


def attention_back_kernel(
    place_ref, grad_mixed_ref, grad_attn_ref, grad_first_ref, qkv_ref, probs_ref, attn_ref,
    input_ref, rows_ref, weight_ref, vectors_ref, small_ref,
    keep_ref, send_ref, grad_rows_ref,
    grad_qkv_ref, grad_ref, sums_ref,
):
    masks, unit, wide_unit = head_masks(), unit_matrix(2 * HEAD_DIM), unit_matrix(PATCHES)

    def pair_step(pair, _):
        at = pl.multiple_of(pair * 2 * HEAD_DIM, 2 * HEAD_DIM)
        columns = pl.ds(at, 2 * HEAD_DIM)
        queries = qkv_ref[:, columns]
        keys_turned = turned(qkv_ref[:, pl.ds(at + D, 2 * HEAD_DIM)], unit)
        values = qkv_ref[:, pl.ds(at + 2 * D, 2 * HEAD_DIM)]
        grads = grad_mixed_ref[:, columns]
        grad_q, grad_k, grad_v = [], [], []
        for head in range(2):
            probs = probs_ref[2 * pair + head]
            grad_probs = product_back(values * masks[head], grads)
            wide = probs.astype(F32)
            inner = jnp.sum(grad_probs * wide, axis=0, keepdims=True)
            grad_scores = (wide * (grad_probs - inner)).astype(BF)
            grad_v.append(product(probs, grads))
            grad_k.append(product(grad_scores, queries) * 0.125)
            part = product(keys_turned[head * HEAD_DIM : (head + 1) * HEAD_DIM], grad_scores)
            grad_q.append((part * 0.125).astype(BF))
        first = low_lanes((PATCHES, 2 * HEAD_DIM))
        grad_qkv_ref[:, columns] = product_back(wide_unit, jnp.concatenate(grad_q)).astype(BF)
        grad_qkv_ref[:, pl.ds(at + D, 2 * HEAD_DIM)] = jnp.where(first, *grad_k).astype(BF)
        grad_qkv_ref[:, pl.ds(at + 2 * D, 2 * HEAD_DIM)] = jnp.where(first, *grad_v).astype(BF)

    lax.fori_loop(0, HEADS // 2, pair_step, None, unroll=PAIRS)
    square = unit_matrix(PLANE)
    for at in range(0, D, PLANE):
        rows = slice(at, at + PLANE)
        left = turned(input_ref[:, rows], square)
        grad_ref[rows, : 3 * D] = product(left, grad_qkv_ref[...]).astype(BF)
        left = turned(attn_ref[:, rows], square)
        grad_ref[rows, 3 * D : 4 * D] = product(left, grad_attn_ref[...]).astype(BF)
    grad = product_back(grad_qkv_ref[...], weight_ref[:, : 3 * D])
    normed, factor = row_norm(rows_ref[...].astype(F32), 1e-06)
    sums_ref[...] = jnp.zeros(sums_ref.shape, F32)
    sums_ref[:16] = small_ref[...]
    sums_ref[0:1] = column_sum(grad * normed)
    sums_ref[1:2] = column_sum(grad)
    sums_ref[2:3] = column_sum(grad_qkv_ref[:, :D].astype(F32))
    sums_ref[3:4] = column_sum(grad_qkv_ref[:, 2 * D :].astype(F32))
    for at in range(0, D, DEC):
        rows = slice(at, at + DEC)
        grad_ref[rows, 4 * D : 4 * D + DEC] = turned(sums_ref[:, rows].astype(BF), unit)
        grad_ref[rows, 4 * D + DEC :] = jnp.zeros((DEC, DEC), BF)
    keep, send = cut_columns(grad_ref, place_ref[0])
    send_ref[...] = grad_ref[:, send]
    keep_ref[...] = grad_ref[:, keep]
    grad = grad_first_ref[...] + row_norm_back(grad * vectors_ref[0:1], normed, factor)
    grad_rows_ref[...] = grad.astype(BF)


def halves(value):
    rows, columns = value.shape
    cut = value.reshape(rows // 16, 2, 8, columns)
    return (cut[:, 0], cut[:, 1])


def join_halves(low, high):
    count, _, columns = low.shape
    return jnp.concatenate(
        [low.reshape(count, 1, 8, columns), high.reshape(count, 1, 8, columns)], axis=1
    ).reshape(count * 16, columns)


def side_steps(low, high):
    place = lax.broadcasted_iota(jnp.int32, low.shape, 1)
    back = jnp.where(place == 0, 0.0, pltpu.roll(high, 1, 1))
    ahead = jnp.where(place == 7, 0.0, pltpu.roll(low, 7, 1))
    return (join_halves(back, low), join_halves(high, ahead))


def put_stack(ref, z, value):
    columns = value.shape[1]
    before, after = side_steps(*halves(value))
    ref[z, :, :columns] = before.astype(BF)
    ref[z, :, columns : 2 * columns] = value.astype(BF)
    ref[z, :, 2 * columns :] = after.astype(BF)


def silu_gate(values):
    return 1.0 / (1.0 + jnp.exp(-values))


UNROLL = 4
PAIRS = 3


def planes(step, carry=None):
    return lax.fori_loop(0, SIDE, step, carry, unroll=UNROLL)


def forward_table(raw_ref, table_ref, first, ins):
    parts, _, rows, _ = raw_ref.shape
    for k in range(9):
        for along in range(3):
            for part in range(parts):
                table_ref[
                    k * DEC + part * rows : k * DEC + (part + 1) * rows,
                    along * ins : (along + 1) * ins,
                ] = raw_ref[part, 3 * k + along, :, first : first + ins]


def backward_table(raw_ref, table_ref, first, ins):
    parts, _, rows, _ = raw_ref.shape
    for k in range(9):
        for along in range(3):
            for part in range(parts):
                table_ref[
                    along * DEC + part * rows : along * DEC + (part + 1) * rows,
                    k * ins : (k + 1) * ins,
                ] = raw_ref[part, 3 * k + 2 - along, :, first : first + ins]


def skip_table(raw_ref):
    return jnp.concatenate([raw_ref[part, 27, :, : 2 * DEC] for part in range(raw_ref.shape[0])])


GROUP = 4


def conv_planes(source, table_ref, total_ref, columns, forward):
    for z in range(SIDE + 2):
        total_ref[z] = jnp.zeros((PLANE, columns), F32)

    def step(group, _):
        start = group * GROUP
        value = jnp.concatenate([source(start + k) for k in range(GROUP)])
        if forward:
            wide = product_back(value, table_ref[...])
        else:
            wide = product(value, table_ref[...])
        none = jnp.zeros((SIDE, columns), F32)
        for plane in range(GROUP):
            for along_d in (-1, 0, 1):
                parts = [
                    wide[plane * PLANE : (plane + 1) * PLANE, k * columns : (k + 1) * columns]
                    for k in range(3 * along_d + 3, 3 * along_d + 6)
                ]
                to = along_d if not forward else -along_d
                early, late = (parts[0], parts[2]) if not forward else (parts[2], parts[0])
                moved = (
                    parts[1]
                    + jnp.concatenate([early[SIDE:], none])
                    + jnp.concatenate([none, late[:-SIDE]])
                )
                at = start + plane + 1 + to
                total_ref[at] = total_ref[at] + moved

    lax.fori_loop(0, SIDE // GROUP, step, None)


def column_sum(value):
    return jnp.sum(value, axis=0, keepdims=True)


def row_sums(value):
    return jnp.sum(value.reshape(-1, 8, value.shape[1]), axis=0)


def map_stats(total_ref, first):
    zero = jnp.zeros((8, total_ref.shape[2]), F32)
    mean = planes(lambda z, run: run + row_sums(total_ref[z + first]), zero)
    mean = column_sum(mean) / VOX

    def spread(z, run):
        center = total_ref[z + first] - mean
        return run + row_sums(center * center)

    return (mean, lax.rsqrt(column_sum(planes(spread, zero)) / VOX + 1e-05))


def sort_matrix():
    here = lax.broadcasted_iota(jnp.int32, (PLANE, PLANE), 0)
    there = lax.broadcasted_iota(jnp.int32, (PLANE, PLANE), 1)
    own = (here & -16) + 2 * (here & 7) + ((here >> 3) & 1)
    return (own == there).astype(F32).astype(BF)


def plane_of(ref, z):
    return ref[lax.shift_right_logical(z, 1), z & 1].reshape(PLANE, ref.shape[-1])


def decoder_forward_kernel(
    block_ref, tap_ref, up_ref, raw_ref, cot_ref,
    joined_ref, hidden_ref, normed_ref, factor_ref, grad_two_ref, grad_skip_ref, section_ref,
    wide_ref, stack_ref, table_one, table_two, total_ref, skip_ref, grad_ref,
):
    forward_table(raw_ref, table_one, 0, 2 * DEC)
    forward_table(raw_ref, table_two, 2 * DEC, DEC)
    for source, rows_ref in enumerate((block_ref, tap_ref)):
        for i in range(2):
            for j in range(2):
                start = source * 8 * DEC + (i * 2 + j) * 2 * DEC
                part = product(rows_ref[...], up_ref[:, start : start + 2 * DEC])
                part = part.astype(BF).astype(F32)
                low = part[:, :DEC].reshape(GRID * GRID, 8, DEC)
                high = part[:, DEC:].reshape(GRID * GRID, 8, DEC)
                before, after = side_steps(low, high)
                for block, value in enumerate((before, join_halves(low, high), after)):
                    at = block * 2 * DEC + source * DEC
                    value = value.astype(BF).reshape(GRID, GRID, SIDE, DEC)
                    wide_ref[:, i, :, j, :, at : at + DEC] = value
                    if block == 1:
                        joined_ref[:, i, :, j, :, source * DEC : (source + 1) * DEC] = value

    conv_planes(lambda z: plane_of(wide_ref, z), table_one, total_ref, DEC, True)
    mean, factor = map_stats(total_ref, 1)
    factor_ref[...] = factor

    def act(z, _):
        normed = (total_ref[z + 1] - mean) * factor
        normed_ref[z] = normed
        value = (normed * silu_gate(normed)).astype(BF)
        hidden_ref[z] = value
        put_stack(stack_ref, z, value.astype(F32))

    planes(act)
    conv_planes(lambda z: stack_ref[z], table_two, total_ref, DEC, True)
    skip = skip_table(raw_ref)

    def skip_step(z, _):
        skip_ref[z] = product_back(plane_of(joined_ref, z), skip)

    planes(skip_step)
    mean_two, factor_two = map_stats(total_ref, 1)
    mean_skip, factor_skip = map_stats(skip_ref, 0)
    sort, unit = sort_matrix(), unit_matrix(DEC)
    zero = jnp.zeros((8, DEC), F32)

    def out_step(z, sums):
        two = (total_ref[z + 1] - mean_two) * factor_two
        side = (skip_ref[z] - mean_skip) * factor_skip
        both = two + side
        gate = silu_gate(both)
        columns = pl.ds(pl.multiple_of(z * PLANE, PLANE), PLANE)
        turned = product_back(unit, (both * gate).astype(BF)).astype(BF)
        section_ref[:, columns] = product(turned, sort).astype(BF)
        grad = product_back(sort, cot_ref[:, columns]) * (gate * (1.0 + both * (1.0 - gate)))
        total_ref[z + 1] = two
        skip_ref[z] = side
        grad_ref[z] = grad
        return (
            sums[0] + row_sums(grad),
            sums[1] + row_sums(grad * two),
            sums[2] + row_sums(grad * side),
        )

    plain, by_two, by_skip = (column_sum(item) for item in planes(out_step, (zero, zero, zero)))

    def back_step(z, _):
        middle = grad_ref[z] - plain / VOX
        grad_two_ref[z] = (factor_two * (middle - total_ref[z + 1] * (by_two / VOX))).astype(BF)
        grad_skip_ref[z] = (factor_skip * (middle - skip_ref[z] * (by_skip / VOX))).astype(BF)

    planes(back_step)


def decoder_backward_kernel(
    grad_two_ref, grad_skip_ref, normed_ref, factor_ref, raw_ref,
    grad_one_ref, rows_block_ref, rows_tap_ref,
    stack_ref, table_one, table_two, total_ref, wide_ref,
):
    backward_table(raw_ref, table_one, 0, 2 * DEC)
    backward_table(raw_ref, table_two, 2 * DEC, DEC)

    def stack_step(z, _):
        put_stack(stack_ref, z, grad_two_ref[z].astype(F32))

    planes(stack_step)
    conv_planes(lambda z: stack_ref[z], table_two, total_ref, DEC, False)
    zero = jnp.zeros((8, DEC), F32)

    def act(z, sums):
        normed = normed_ref[z]
        gate = silu_gate(normed)
        grad = total_ref[z + 1] * (gate * (1.0 + normed * (1.0 - gate)))
        total_ref[z + 1] = grad
        return (sums[0] + row_sums(grad), sums[1] + row_sums(grad * normed))

    plain, by_normed = (column_sum(item) for item in planes(act, (zero, zero)))

    def back_step(z, _):
        middle = total_ref[z + 1] - plain / VOX
        value = (factor_ref[...] * (middle - normed_ref[z] * (by_normed / VOX))).astype(BF)
        grad_one_ref[z] = value
        put_stack(stack_ref, z, value.astype(F32))

    planes(back_step)
    conv_planes(lambda z: stack_ref[z], table_one, wide_ref, 2 * DEC, False)
    skip = skip_table(raw_ref)

    def row_step(a, _):
        rows = pl.ds(pl.multiple_of(a * GRID * GRID, GRID * GRID), GRID * GRID)
        for i in range(2):
            z = 2 * a + i
            value = wide_ref[z + 1] + product(grad_skip_ref[z], skip)
            value = value.reshape(GRID, 2, 2, 8, 2 * DEC)
            for j in range(2):
                for l in range(2):
                    at = ((i * 2 + j) * 2 + l) * DEC
                    part = value[:, j, l].reshape(GRID * GRID, 2 * DEC).astype(BF)
                    rows_block_ref[rows, at : at + DEC] = part[:, :DEC]
                    rows_tap_ref[rows, at : at + DEC] = part[:, DEC:]

    lax.fori_loop(0, GRID, row_step, None)


def turn_stack(source_ref, turned_ref, unit):
    def step(z, _):
        value = source_ref[z].astype(F32)
        before, after = side_steps(*halves(value))
        columns = pl.ds(pl.multiple_of(z * PLANE, PLANE), PLANE)
        for block, item in enumerate((before, value, after)):
            turned_ref[block * DEC : (block + 1) * DEC, columns] = product_back(
                unit, item.astype(BF)
            ).astype(BF)

    planes(step)


def put_shifted(source, shifted_ref):
    columns = shifted_ref.shape[2] // 3
    for z in (0, SIDE + 1):
        shifted_ref[z] = jnp.zeros(shifted_ref.shape[1:], BF)

    def step(z, _):
        value = source(z)
        none = jnp.zeros((SIDE, columns), BF)
        shifted_ref[z + 1, :, :columns] = jnp.concatenate([none, value[:-SIDE]])
        shifted_ref[z + 1, :, columns : 2 * columns] = value
        shifted_ref[z + 1, :, 2 * columns :] = jnp.concatenate([value[SIDE:], none])

    planes(step)


def weight_grad(turned_ref, shifted_ref, out_ref, first, ins):
    parts, _, rows, _ = out_ref.shape
    for along_d in range(3):
        shifted = shifted_ref[along_d : along_d + SIDE].reshape(VOX, 3 * ins)
        table = product(turned_ref[...], shifted).astype(BF)
        for along_h in range(3):
            for block in range(3):
                slot = (along_d * 3 + along_h) * 3 + 2 - block
                for part in range(parts):
                    out_ref[part, slot, :, first : first + ins] = table[
                        block * DEC + part * rows : block * DEC + (part + 1) * rows,
                        along_h * ins : (along_h + 1) * ins,
                    ]


def decoder_weights_kernel(
    grad_two_ref, hidden_ref, grad_one_ref, joined_ref, grad_skip_ref,
    out_ref,
    turned_ref, shifted_ref, narrow_ref,
):
    unit = unit_matrix(DEC)
    turn_stack(grad_two_ref, turned_ref, unit)
    put_shifted(lambda z: hidden_ref[z], narrow_ref)
    weight_grad(turned_ref, narrow_ref, out_ref, 2 * DEC, DEC)
    turn_stack(grad_one_ref, turned_ref, unit)
    put_shifted(lambda z: joined_ref[z], shifted_ref)
    weight_grad(turned_ref, shifted_ref, out_ref, 0, 2 * DEC)

    def step(z, _):
        columns = pl.ds(pl.multiple_of(z * PLANE, PLANE), PLANE)
        turned_ref[:DEC, columns] = product_back(unit, grad_skip_ref[z]).astype(BF)

    planes(step)
    table = product(turned_ref[:DEC], joined_ref[...].reshape(VOX, 2 * DEC)).astype(BF)
    parts, _, rows, columns = out_ref.shape
    for part in range(parts):
        out_ref[part, 27, :, : 2 * DEC] = table[part * rows : (part + 1) * rows]
        out_ref[part, 27, :, 2 * DEC :] = jnp.zeros((rows, columns - 2 * DEC), BF)


def skip_operands(kernel, count, left):
    def run(*refs):
        kernel(*refs[:count], *refs[count + left :])

    return run


def local_call(kernel, outs, scratch, *operands, after=()):
    specs = [
        pl.BlockSpec(memory_space=pltpu.SMEM if item.ndim == 1 else pltpu.VMEM)
        for item in operands
    ]
    specs += [pl.BlockSpec(memory_space=pl.ANY)] * len(after)
    vmem = pl.BlockSpec(memory_space=pltpu.VMEM)
    return pl.pallas_call(
        skip_operands(kernel, len(operands), len(after)),
        out_shape=[jax.ShapeDtypeStruct(shape, dtype) for shape, dtype in outs],
        in_specs=specs,
        out_specs=[vmem] * len(outs),
        scratch_shapes=[pltpu.VMEM(shape, dtype) for shape, dtype in scratch],
        compiler_params=pltpu.CompilerParams(vmem_limit_bytes=VMEM_BYTES),
        cost_estimate=pl.CostEstimate(flops=COST, bytes_accessed=COST, transcendentals=0),
    )(*operands, *after)


MAP = (SIDE, PLANE, DEC)


def decoder_forward(*operands, after=()):
    cube = (GRID, 2, GRID, 2, SIDE)
    return local_call(
        decoder_forward_kernel,
        [
            (cube + (2 * DEC,), BF), (MAP, BF), (MAP, F32), ((1, DEC), F32), (MAP, BF), (MAP, BF),
            ((DEC, VOX), BF),
        ],
        [
            (cube + (6 * DEC,), BF), ((SIDE, PLANE, 3 * DEC), BF), ((9 * DEC, 6 * DEC), BF),
            ((9 * DEC, 3 * DEC), BF), ((SIDE + 2, PLANE, DEC), F32), (MAP, F32), (MAP, F32),
        ],
        *operands, after=after,
    )


def decoder_backward(*operands, after=()):
    return local_call(
        decoder_backward_kernel,
        [(MAP, BF), ((PATCHES, 8 * DEC), BF), ((PATCHES, 8 * DEC), BF)],
        [
            ((SIDE, PLANE, 3 * DEC), BF), ((3 * DEC, 18 * DEC), BF), ((3 * DEC, 9 * DEC), BF),
            ((SIDE + 2, PLANE, DEC), F32), ((SIDE + 2, PLANE, 2 * DEC), F32),
        ],
        *operands, after=after,
    )


def decoder_weights(*operands, shape, after=()):
    return local_call(
        decoder_weights_kernel,
        [(shape, BF)],
        [
            ((3 * DEC, VOX), BF), ((SIDE + 2, PLANE, 6 * DEC), BF),
            ((SIDE + 2, PLANE, 3 * DEC), BF),
        ],
        *operands, after=after,
    )[0]


def attention(rows, weight, after=()):
    flat = (PATCHES, D)
    return local_call(
        attention_kernel,
        [
            (flat, BF), ((PATCHES, 3 * D), BF), ((HEADS, PATCHES, PATCHES), BF), (flat, BF),
            (flat, F32), (flat, BF), ((16, D), F32),
        ],
        [], rows, weight, after=after,
    )


def mlp(rows, first, fc1, fc2, fc1_shift, fc2_shift, after=()):
    return local_call(
        mlp_kernel,
        [((PATCHES, MLP), BF), ((PATCHES, MLP), BF), ((PATCHES, D), BF)],
        [], rows, first, fc1, fc2, fc1_shift, fc2_shift, after=after,
    )


def up_back(grad_block, grad_tap, block_out, tap_rows, up_full, after=()):
    flat = (PATCHES, D)
    return local_call(
        up_back_kernel,
        [((D, 16 * DEC), BF), (flat, BF), (flat, F32), (flat, BF), ((1, D), F32)],
        [], grad_block, grad_tap, block_out, tap_rows, up_full, after=after,
    )


def fc2_back(place, grad_mlp, active, slope, fc2, after=()):
    half = ((MLP, D // 2), BF)
    return local_call(
        fc2_back_kernel,
        [half, half, ((PATCHES, MLP), BF), ((1, MLP), F32)],
        [], place, grad_mlp, active, slope, fc2, after=after,
    )


def fc1_back(place, grad_hidden, input_two, first, grad_second, fc1, weight, vectors, after=()):
    half, flat = ((D, MLP // 2), BF), (PATCHES, D)
    return local_call(
        fc1_back_kernel,
        [half, half, (flat, F32), (flat, BF), (flat, BF), ((8, D), F32)],
        [],
        place, grad_hidden, input_two, first, grad_second, fc1, weight, vectors, after=after,
    )


def attention_back(place, *operands, after=()):
    wide = 4 * D + 2 * DEC
    half = ((D, wide // 2), BF)
    return local_call(
        attention_back_kernel,
        [half, half, ((PATCHES, D), BF)],
        [((PATCHES, 3 * D), BF), ((D, wide), BF), ((DEC, D), F32)],
        place, *operands, after=after,
    )


def make_body(axes):
    names, wa, col = axes.names, axes.wa, axes.col
    both = wa + col

    def body(
        tokens,
        tap,
        ln1_gain,
        ln1_bias,
        qkv_weight,
        query_bias,
        value_bias,
        out_weight,
        out_bias,
        ln2_gain,
        ln2_bias,
        fc1_weight,
        fc1_bias,
        fc2_weight,
        fc2_bias,
        block_up,
        tap_up,
        conv1_weight,
        conv2_weight,
        skip_weight,
        cotangent,
    ):
        rows_here = ln1_gain.shape[0]
        place = lax.axis_index(axes.core).astype(jnp.int32).reshape(1)

        vectors = [
            item.reshape(rows_here, -1)
            for item in (
                ln1_gain, ln1_bias, query_bias, value_bias, out_bias, ln2_gain, ln2_bias,
                fc2_bias, *jnp.split(fc1_bias, MLP // D),
            )
        ]
        vectors = jnp.concatenate(vectors, axis=1)
        extra = vectors.shape[1]
        vectors = jnp.pad(vectors, ((0, 0), (0, 2 * DEC - extra)))
        get_first = RowGather(
            jnp.concatenate([qkv_weight, out_weight, vectors], axis=1), axes.links_a, axes
        )
        get_fc1 = RowGather(fc1_weight, axes.links_b, axes)
        get_fc2 = RowGather(fc2_weight, axes.links_a, axes)
        up_full = lax.all_gather(
            jnp.concatenate([block_up, tap_up], axis=1), both, axis=0, tiled=True
        )
        conv_shard = jnp.concatenate([conv1_weight, conv2_weight], axis=2)
        skip_shard = jnp.pad(skip_weight, ((0, 0), (0, DEC)))
        conv_shard = jnp.concatenate([conv_shard, skip_shard[None]], axis=0)
        raw = lax.all_gather(conv_shard, col, axis=0, tiled=False)
        rows_bf = swap_blocks(tokens.reshape(axes.wa_count, -1, D), wa).reshape(PATCHES, D)
        get_first.link()
        get_fc1.value = wait_for(get_fc1.value, corner(get_first.value))
        get_fc1.link()
        get_first.link()
        get_fc2.value = wait_for(get_fc2.value, corner(get_fc1.value))
        get_fc2.link()
        for item in (get_first, get_fc1, get_fc2):
            while item.left:
                item.link()
        first_weight = get_first.finish(get_first.rows())
        tap = wait_for(tap, corner(get_fc2.value))
        tap_rows = swap_blocks(tap.reshape(axes.wa_count, -1, D), wa).reshape(PATCHES, D)
        cotangent = wait_for(cotangent, corner(get_fc2.value))
        upstream = swap_blocks(cotangent.reshape(axes.col_count, -1, VOX), col).reshape(DEC, VOX)

        input_one, qkv_rows, probs, attn_rows, first, input_two, vectors = attention(
            rows_bf, first_weight
        )
        fc1_full = get_fc1.finish(get_fc1.rows())
        fc2_full = get_fc2.finish(wait_for(get_fc2.rows(), corner(input_two)))
        fc1_shift = vectors[8:extra].reshape(extra - 8, -1, rows_here).transpose(1, 0, 2)
        fc1_shift = fc1_shift.reshape(1, MLP)
        active, slope, block_out = mlp(
            input_two, first, fc1_full, fc2_full, fc1_shift, vectors[7:8],
            after=(tap_rows,),
        )
        joined, hidden_maps, normed_c1, factor_c1, grad_c2, grad_skip, section = decoder_forward(
            block_out, tap_rows, up_full, raw, upstream
        )
        section_out = swap_blocks(section.reshape(axes.col_count, -1, VOX), col)

        grad_c1, grad_up_block, grad_up_tap = decoder_backward(
            grad_c2, grad_skip, normed_c1, factor_c1, raw
        )
        grad_up, grad_tap_rows, grad_second, grad_mlp, fc2_shift_sums = up_back(
            grad_up_block, grad_up_tap, block_out, tap_rows, up_full,
        )
        grad_ups = lax.psum_scatter(grad_up, both, scatter_dimension=0, tiled=True).astype(F32)
        keep, send, grad_hidden, fc1_shift_sums = fc2_back(
            place, grad_mlp, active, slope, fc2_full
        )
        sum_fc2 = RowSum(keep, send, axes.links_a, axes)
        keep, send, grad_first, grad_attn, grad_mixed, sums_two = fc1_back(
            place, grad_hidden, input_two, first, grad_second, fc1_full, first_weight, vectors
        )
        sum_fc1 = RowSum(keep, send, axes.links_b, axes)
        small = jnp.concatenate(
            [
                jnp.zeros((4, D), F32), sums_two[2:3], sums_two[:2], fc2_shift_sums,
                fc1_shift_sums.reshape(-1, extra - 8, rows_here).transpose(1, 0, 2).reshape(-1, D),
                jnp.zeros((16 - extra, D), F32),
            ]
        )
        keep, send, grad_rows = attention_back(
            place, grad_mixed, grad_attn, grad_first, qkv_rows, probs, attn_rows, input_one,
            rows_bf, first_weight, vectors, small, after=(sum_fc2.value,),
        )
        sum_fc2.link()
        sum_first = RowSum(keep, send, axes.links_a, axes)
        conv_grads = decoder_weights(
            grad_c2, hidden_maps, grad_c1, joined.reshape(SIDE, PLANE, 2 * DEC), grad_skip,
            shape=raw.shape, after=(sum_fc1.value, sum_fc2.value),
        )
        sum_fc1.link()
        sum_fc2.link()

        columns = conv_grads.shape[3]
        conv_grads = conv_grads.reshape([lax.axis_size(n) for n in col] + [-1, columns])
        conv_grads = scatter_dims(conv_grads, axes.inside(col)[::-1], names)
        conv_grads = conv_grads.reshape([lax.axis_size(n) for n in wa] + [-1, columns])
        wa_order = axes.inside(wa)
        conv_grads = scatter_dims(conv_grads, wa_order[::-1], names).astype(BF)
        conv_grads = gather_dims(conv_grads, wa_order, names).reshape(28, -1, columns)
        conv_grads = conv_grads.astype(F32)

        home_rows = swap_blocks(grad_rows.reshape(axes.wa_count, -1, D), wa).astype(F32)[None]
        home_tap = swap_blocks(grad_tap_rows.reshape(axes.wa_count, -1, D), wa).astype(F32)[None]
        sums = (sum_fc2, sum_fc1, sum_first)
        for item in sums:
            while item.left:
                item.link()
        grad_fc2, grad_fc1, first_grads = (item.finish() for item in sums)
        small_sums = first_grads[:, 4 * D : 4 * D + extra]
        return (
            section_out[:, None],
            home_rows,
            home_tap,
            small_sums[:, 0],
            small_sums[:, 1],
            first_grads[:, : 3 * D],
            small_sums[:, 2],
            small_sums[:, 3],
            first_grads[:, 3 * D : 4 * D],
            small_sums[:, 4],
            small_sums[:, 5],
            small_sums[:, 6],
            grad_fc1,
            small_sums[:, 8:extra].T.reshape(-1),
            grad_fc2,
            small_sums[:, 7],
            grad_ups[:, : 8 * DEC],
            grad_ups[:, 8 * DEC :],
            conv_grads[:27, :, : 2 * DEC],
            conv_grads[:27, :, 2 * DEC :],
            conv_grads[27, :, : 2 * DEC],
        )

    return body


def solution(mesh):
    axes = Axes(mesh)
    wa, col = axes.wa, axes.col
    both = wa + col
    tall, flat = P(both, None), P(both)
    rows = P(col, None, wa, None)
    maps = P(None, wa, col, None)
    kernel, wide = P(None, col, None), P(col, None)
    in_specs = (
        rows, rows, flat, flat, tall, flat, flat, tall, flat, flat, flat, tall, flat, tall, flat,
        tall, tall, kernel, kernel, wide, maps,
    )
    out_specs = (
        maps, rows, rows, flat, flat, tall, flat, flat, tall, flat, flat, flat, tall, flat, tall,
        flat, tall, tall, kernel, kernel, wide,
    )
    return jax.shard_map(
        make_body(axes), mesh=axes.mesh, in_specs=in_specs, out_specs=out_specs, check_vma=False
    )
```

profile of v0, /device:TPU:0, one launch (start us, length us, event | category | flops | bytes accessed | tf_op | source)
XLA Modules:
  0.0 528.8 jit_solution(14721046998125891459)
XLA Ops:
  13.8 2.0 pad_maximum_fusion.4
  16.0 2.7 collective-permute-start.15
  18.6 2.6 collective-permute-start.16
  24.0 10.9 %collective-permute-done.8 = bf16[2,24,1536]{2,1,0:T(8,128)(2,1)S(1)} collective-permute-done((bf16[2,24,1536]{2,1,0:T(8,128)(2,1)S(1)}, bf16[2,24,1536]{2,1,0:T(8,128)(2,1)S(1)}, u32[]{:S(2)}, u32[]{:S(2)}) %collective-permute-start.8) | collective-permute-done | bytes 147488 | tf_op jit(solution)/shard_map/ppermute | solution.py:76
  36.0 7.5 %collective-permute-start.1 = (bf16[2,24,1664]{2,1,0:T(8,128)(2,1)S(1)}, bf16[2,24,1664]{2,1,0:T(8,128)(2,1)S(1)}, u32[]{:S(2)}, u32[]{:S(2)}) collective-permute-start(bf16[2,24,1664]{2,1,0:T(8,128)(2,1)S(1)} %maximum_select_fusion.15), channel_id=1, source_target_pairs={{0,8},{8,16},{16,24},{24,0},{1,9},{9,17},{17,25},{25,1},{2,10},{10... | collective-permute-start | bytes 479240 | tf_op jit(solution)/shard_map/ppermute | solution.py:76
  43.5 4.0 collective-permute-start.2
  51.7 3.2 collective-permute-done.1
  54.9 5.3 %collective-permute-done.2 = bf16[2,24,1664]{2,1,0:T(8,128)(2,1)S(1)} collective-permute-done((bf16[2,24,1664]{2,1,0:T(8,128)(2,1)S(1)}, bf16[2,24,1664]{2,1,0:T(8,128)(2,1)S(1)}, u32[]{:S(2)}, u32[]{:S(2)}) %collective-permute-start.2) | collective-permute-done | bytes 159776 | tf_op jit(solution)/shard_map/ppermute | solution.py:76
  61.9 3.0 collective-permute-done.18
  65.1 1.6 collective-permute-start.19
  68.9 9.6 %collective-permute-done.4 = bf16[4,2,24,1664]{3,2,1,0:T(8,128)(2,1)S(1)} collective-permute-done((bf16[4,2,24,1664]{3,2,1,0:T(8,128)(2,1)S(1)}, bf16[4,2,24,1664]{3,2,1,0:T(8,128)(2,1)S(1)}, u32[]{:S(2)}, u32[]{:S(2)}) %collective-permute-start.4) | collective-permute-done | bytes 639008 | tf_op jit(solution)/shard_map/ppermute | solution.py:72
  78.7 1.6 collective-permute-start.5
  80.6 13.5 %collective-permute-done.19 = bf16[2,4,2,96,384]{4,3,2,1,0:T(8,128)(2,1)S(1)} collective-permute-done((bf16[2,4,2,96,384]{4,3,2,1,0:T(8,128)(2,1)S(1)}, bf16[2,4,2,96,384]{4,3,2,1,0:T(8,128)(2,1)S(1)}, u32[]{:S(2)}, u32[]{:S(2)}) %collective-permute-start.19) | collective-permute-done | bytes 1179680 | tf_op jit(solution)/shard_map/ppermute | solution.py:72
  94.5 1.8 copy.74
  96.4 5.0 collective-permute-done.12
  101.4 1.8 maximum_select_fusion.4
  103.1 13.3 %collective-permute-done.5 = bf16[2,4,2,24,1664]{4,3,2,0,1:T(8,128)(2,1)S(1)} collective-permute-done((bf16[2,4,2,24,1664]{4,3,2,0,1:T(8,128)(2,1)S(1)}, bf16[2,4,2,24,1664]{4,3,2,0,1:T(8,128)(2,1)S(1)}, u32[]{:S(2)}, u32[]{:S(2)}) %collective-permute-start.5) | collective-permute-done | bytes 1277984 | tf_op jit(solution)/shard_map/ppermute | solution.py:72
  116.8 4.4 all-to-all-start
  122.0 7.7 %maximum_select_fusion.2.refs_3_.refs_4_ = bf16[3072,768]{1,0:T(8,128)(2,1)} fusion(bf16[3072,384]{1,0:T(8,128)(2,1)} %collective-permute-done.20, bf16[3072,384]{1,0:T(8,128)(2,1)} %bitcast.55, pred[]{:T(512)S(6)} %eq.56), kind=kLoop, calls=%fused_computation.3 | loop fusion | flops 21233664 | bytes 9437185 | tf_op jit(solution)/shard_map/jit(_where)/select_n | solution.py:97
  129.7 7.8 %maximum_select_fusion.1.refs_2_.refs_5_ = bf16[768,3072]{1,0:T(8,128)(2,1)} fusion(bf16[768,1536]{1,0:T(8,128)(2,1)} %collective-permute-done.13, bf16[768,1536]{1,0:T(8,128)(2,1)} %bitcast.41, pred[]{:T(512)S(6)} %eq.56), kind=kLoop, calls=%fused_computation.2 | loop fusion | flops 21233664 | bytes 9437185 | tf_op jit(solution)/shard_map/jit(_where)/select_n | solution.py:97
  137.6 6.7 %maximum_select_fusion.refs_1_.refs_6_.refs_9_ = bf16[768,3328]{1,0:T(8,128)(2,1)} fusion(bf16[768,1664]{1,0:T(8,128)(2,1)} %collective-permute-done.6, bf16[768,1664]{1,0:T(8,128)(2,1)S(1)} %bitcast.222, pred[]{:T(512)S(6)} %eq.56), kind=kLoop, calls=%fused_computation | loop fusion | flops 23003136 | bytes 10223617 | tf_op jit(solution)/shard_map/jit(_where)/select_n | solution.py:97
  144.3 6.2 %all-to-all-start.1 = ((bf16[8,64,768]{2,1,0:T(8,128)(2,1)}), bf16[8,64,768]{2,1,0:T(8,128)(2,1)S(1)}, u32[]{:S(2)}, u32[]{:S(2)}) async-start(bf16[8,64,768]{2,1,0:T(8,128)(2,1)} %bitcast.58), calls=%async_computation.1 | async-start | bytes 1572864 | tf_op jit(solution)/shard_map/all_to_all | solution.py:198
  150.5 16.9 %shard_map.364 = (bf16[512,768]{1,0:T(8,128)(2,1)}, bf16[512,2304]{1,0:T(8,128)(2,1)}, bf16[12,512,512]{2,1,0:T(8,128)(2,1)}, bf16[512,768]{1,0:T(8,128)(2,1)}, ...) custom-call(bf16[512,768]{1,0:T(8,128)(2,1)} %bitcast.257, ...), custom_call_target="tpu_custom_call" | custom-call | flops 30000001024 | bytes 30000001024 | tf_op jit(solution)/shard_map/pallas_call | solution.py:771
  170.4 4.6 all-to-all-done.1
  175.0 3.8 all-to-all-start.2
  178.8 14.0 %shard_map.365 = (bf16[512,3072]{1,0:T(8,128)(2,1)}, bf16[512,3072]{1,0:T(8,128)(2,1)}, bf16[512,768]{1,0:T(8,128)(2,1)}) custom-call(bf16[512,768]{1,0:T(8,128)(2,1)} %get-tuple-element.61.refs_0_.refs_2_, f32[512,768]{1,0:T(8,128)} %get-tuple-element.62.refs_1_.refs_3_, bf16[768,3072]{1,0:T(8,128)(2,1)} %maximum_select_fusion.1.refs_2_.refs_5_, ...), custom_call_target="tpu_custom_call" | custom-call | flops 30000001024 | bytes 30000001024 | tf_op jit(solution)/shard_map/pallas_call | solution.py:771
  194.9 43.3 %shard_map.366 = (bf16[8,2,8,2,16,256]{5,4,3,2,1,0:T(8,128)(2,1)}, bf16[16,256,128]{2,1,0:T(8,128)(2,1)}, f32[16,256,128]{2,1,0:T(8,128)}, f32[1,128]{1,0:T(1,12...) custom-call(bf16[512,768]{1,0:T(8,128)(2,1)} %get-tuple-element.65.refs_0_.refs_2_, ...), custom_call_target="tpu_custom_call" | custom-call | flops 30000001024 | bytes 30000001024 | tf_op jit(solution)/shard_map/pallas_call | solution.py:771
  238.2 3.5 all-to-all-start.3
  241.8 25.3 %shard_map.367 = (bf16[16,256,128]{2,1,0:T(8,128)(2,1)}, bf16[512,1024]{1,0:T(8,128)(2,1)}, bf16[512,1024]{1,0:T(8,128)(2,1)}) custom-call(bf16[16,256,128]{2,1,0:T(8,128)(2,1)} %get-tuple-element.68.refs_0_, bf16[16,256,128]{2,1,0:T(8,128)(2,1)} %get-tuple-element.69.refs_1_.refs_4_, f32[16,256,128]{2,1,0:T(8,128)} %get-tuple-element.70.refs_2_, ...), custom_call_target="tpu_custom_call" | custom-call | flops 30000001024 | bytes 30000001024 | tf_op jit(solution)/shard_map/pallas_call | solution.py:771
  267.0 9.1 %shard_map.368 = (bf16[768,2048]{1,0:T(8,128)(2,1)}, bf16[512,768]{1,0:T(8,128)(2,1)}, f32[512,768]{1,0:T(8,128)}, bf16[512,768]{1,0:T(8,128)(2,1)}, f32[1,768]{1,0:T(1,128)}) custom-call(bf16[512,1024]{1,0:T(8,128)(2,1)} %get-tuple-element.72.refs_0_, bf16[512,1024]{1,0:T(8,128)(2,1)} %get-tuple-element.73.refs_1_, ...), custom_call_target="tpu_custom_call" | custom-call | flops 30000001024 | bytes 30000001024 | tf_op jit(solution)/shard_map/pallas_call | solution.py:771
  276.2 13.9 %shard_map.369 = (bf16[3072,384]{1,0:T(8,128)(2,1)}, bf16[3072,384]{1,0:T(8,128)(2,1)}, bf16[512,3072]{1,0:T(8,128)(2,1)}, f32[1,3072]{1,0:T(1,128)}) custom-call(s32[1]{0:T(128)} %bitcast.66.refs_0_, bf16[512,768]{1,0:T(8,128)(2,1)} %get-tuple-element.74.refs_1_, bf16[512,3072]{1,0:T(8,128)(2,1)} %get-tuple-element.75.refs_2_, ...), custom_call_target="tpu_custom_call" | custom-call | flops 30000001024 | bytes 30000001024 | tf_op jit(solution)/shard_map/pallas_call | solution.py:771
  290.6 5.5 %all-to-all-start.5 = ((bf16[8,64,768]{2,1,0:T(8,128)(2,1)}), bf16[8,64,768]{2,1,0:T(8,128)(2,1)S(1)}, u32[]{:S(2)}, u32[]{:S(2)}) async-start(bf16[8,64,768]{2,1,0:T(8,128)(2,1)} %bitcast.71), calls=%async_computation.5 | async-start | bytes 1572864 | tf_op jit(solution)/shard_map/all_to_all | solution.py:198
  296.4 14.6 %shard_map.370 = (bf16[768,1536]{1,0:T(8,128)(2,1)}, bf16[768,1536]{1,0:T(8,128)(2,1)}, f32[512,768]{1,0:T(8,128)}, bf16[512,768]{1,0:T(8,128)(2,1)}, bf16[512,768]{1,0:T(8,128)(2,1)}, /*index=5*/f32[8,768]{1,0:T(8,128)}) custom-call(s32[1]{0:T(128)} %bitcast.66.refs_0_, bf16[512,3072]{1,0:T(8,128)(2,1)} %get-tuple-element.77.refs_1_, ...), custom_call_target="tpu_custom_call" | custom-call | flops 30000001024 | bytes 30000001024 | tf_op jit(solution)/shard_map/pallas_call | solution.py:771
  317.8 2.3 add_convert_fusion.2
  321.2 2.0 collective-permute-start.36
  323.2 2.3 add_convert_fusion.1
  328.6 25.8 %shard_map.371 = (bf16[768,1664]{1,0:T(8,128)(2,1)}, bf16[768,1664]{1,0:T(8,128)(2,1)}, bf16[512,768]{1,0:T(8,128)(2,1)}) custom-call(s32[1]{0:T(128)} %bitcast.66.refs_0_, bf16[512,768]{1,0:T(8,128)(2,1)} %get-tuple-element.79.refs_1_, bf16[512,768]{1,0:T(8,128)(2,1)} %get-tuple-element.80.refs_2_, f32[512,768]{1,0:T(8,128)} %get-tuple-element.81.refs_3_, ...), custom_call_target="tpu_custom_call" | custom-call | flops 30000001024 | bytes 30000001024 | tf_op jit(solution)/shard_map/pallas_call | solution.py:771
  354.4 4.4 all-to-all-start.4
  358.8 1.8 fusion.3
  360.7 1.9 collective-permute-start.31
  362.5 2.6 fusion.2.refs_6_
  365.1 22.5 %shard_map.372 = bf16[4,28,32,384]{3,2,1,0:T(8,128)(2,1)} custom-call(bf16[16,256,128]{2,1,0:T(8,128)(2,1)} %get-tuple-element.68.refs_0_, bf16[16,256,128]{2,1,0:T(8,128)(2,1)} %get-tuple-element.98.refs_1_, bf16[16,256,128]{2,1,0:T(8,128)(2,1)} %get-tuple-element.99.refs_2_, bf16[16,256,256]{2,1,0:T(8,128)(2,1)} %bitcast.280, ...), custom_call_target="tpu_custom_call" | custom-call | flops 30000001024 | bytes 30000001024 | tf_op jit(solution)/shard_map/pallas_call | solution.py:771
  387.7 2.7 dynamic-slice_bitcast_fusion
  390.6 1.8 collective-permute-start.37
  392.4 2.4 bitcast_convert_fusion.1
  398.3 2.4 collective-permute-start.33
  400.6 7.3 %collective-permute-done.37 = bf16[4,2,96,384]{3,2,1,0:T(8,128)(2,1)} collective-permute-done((bf16[4,2,96,384]{3,2,1,0:T(8,128)(2,1)S(1)}, bf16[4,2,96,384]{3,2,1,0:T(8,128)(2,1)}, u32[]{:S(2)}, u32[]{:S(2)}) %collective-permute-start.37) | collective-permute-done | bytes 589856 | tf_op jit(solution)/shard_map/ppermute | solution.py:76
  408.0 3.6 collective-permute-start.34
  412.8 18.2 %reduce-scatter.2.cloned.1.call-done = bf16[24,2048]{1,0:T(8,128)(2,1)} async-done(((bf16[768,2048]{1,0:T(8,128)(2,1)}), bf16[24,2048]{1,0:T(8,128)(2,1)}) %reduce-scatter.2.cloned.1.call-update) | async-done | bytes 98320 | tf_op jit(solution)/shard_map/reduce_scatter | solution.py:974
  434.0 1.6 collective-permute-start.39
  437.1 2.1 fusion
  441.3 3.5 collective-permute-done.39
  444.9 9.2 %collective-permute-done.43 = bf16[896,384]{1,0:T(8,128)(2,1)S(1)} collective-permute-done((bf16[896,384]{1,0:T(8,128)(2,1)S(1)}, bf16[896,384]{1,0:T(8,128)(2,1)S(1)}, u32[]{:S(2)}, u32[]{:S(2)}) %collective-permute-start.43) | collective-permute-done | bytes 688160 | tf_op jit(solution)/shard_map/ppermute | solution.py:76
  455.8 2.4 add_convert_fusion
  463.7 2.5 collective-permute-start.47
  466.3 2.0 collective-permute-done.45
  471.3 2.1 collective-permute-start.49
  473.7 3.4 collective-permute-done.48
  477.1 1.9 collective-permute-done.49
  479.0 5.8 %collective-permute-done.23 = bf16[4,2,2,24,1664]{4,3,2,0,1:T(8,128)(2,1)S(1)} collective-permute-done((bf16[4,2,2,24,1664]{4,3,2,0,1:T(8,128)(2,1)S(1)}, bf16[4,2,2,24,1664]{4,3,2,0,1:T(8,128)(2,1)S(1)}, u32[]{:S(2)}, u32[]{:S(2)}) %collective-permute-start.23) | collective-permute-done | bytes 1277984 | tf_op jit(solution)/shard_map/ppermute | solution.py:76
  488.8 15.3 %collective-permute-done.51 = bf16[4,112,384]{2,1,0:T(8,128)(2,1)S(1)} collective-permute-done((bf16[4,112,384]{2,1,0:T(8,128)(2,1)S(1)}, bf16[4,112,384]{2,1,0:T(8,128)(2,1)S(1)}, u32[]{:S(2)}, u32[]{:S(2)}) %collective-permute-start.51) | collective-permute-done | bytes 344096 | tf_op jit(solution)/shard_map/ppermute | solution.py:72
  508.1 2.2 collective-permute-start.27
  511.0 2.6 collective-permute-done.25
  513.6 3.1 collective-permute-done.26
  (221 shorter events, 73.7 us)
Async XLA Ops:
  7.2 186.8 %all-gather.6.cloned.1.call-start = ((), (), s32[]{:S(2)}) async-start(), calls=%async_computation.9 | async-start | bytes 3440640 | tf_op jit(solution)/shard_map/all_gather | solution.py:935
  8.2 7.7 %collective-permute-start.14 = (bf16[96,384]{1,0:T(8,128)(2,1)S(1)}, bf16[96,384]{1,0:T(8,128)(2,1)S(1)}, u32[]{:S(2)}, u32[]{:S(2)}) collective-permute-start(bf16[96,384]{1,0:T(8,128)(2,1)S(1)} %get-tuple-element.133), channel_id=1, source_target_pairs={{0,1},{1,0},{2,3},{3,2},{4,5},{5,4},{6,7},{7,6},{8,9},{9,8},{10,11... | collective-permute-start | bytes 221192 | tf_op jit(solution)/shard_map/ppermute | solution.py:72
  9.6 12.9 %collective-permute-start.7 = (bf16[24,1536]{1,0:T(8,128)(2,1)S(1)}, bf16[24,1536]{1,0:T(8,128)(2,1)S(1)}, u32[]{:S(2)}, u32[]{:S(2)}) collective-permute-start(bf16[24,1536]{1,0:T(8,128)(2,1)S(1)} %get-tuple-element.135), channel_id=1, source_target_pairs={{0,1},{1,0},{2,3},{3,2},{4,5},{5,4},{6,7},{7,6},{8,9},{9,8},{10,11... | collective-permute-start | bytes 221192 | tf_op jit(solution)/shard_map/ppermute | solution.py:72
  12.5 11.0 %collective-permute-start = (bf16[24,1664]{1,0:T(8,128)(2,1)S(1)}, bf16[24,1664]{1,0:T(8,128)(2,1)S(1)}, u32[]{:S(2)}, u32[]{:S(2)}) collective-permute-start(bf16[24,1664]{1,0:T(8,128)(2,1)S(1)} %get-tuple-element.130), channel_id=1, source_target_pairs={{0,1},{1,0},{2,3},{3,2},{4,5},{5,4},{6,7},{7,6},{8,9},{9,8},{10,11... | collective-permute-start | bytes 239624 | tf_op jit(solution)/shard_map/ppermute | solution.py:72
  16.0 20.0 %collective-permute-start.15 = (bf16[2,96,384]{2,1,0:T(8,128)(2,1)S(1)}, bf16[2,96,384]{2,1,0:T(8,128)(2,1)S(1)}, u32[]{:S(2)}, u32[]{:S(2)}) collective-permute-start(bf16[2,96,384]{2,1,0:T(8,128)(2,1)S(1)} %maximum_select_fusion.17), channel_id=1, source_target_pairs={{0,8},{8,16},{16,24},{24,0},{1,9},{9,17},{17,25},{25,1},{2,10},{10... | collective-permute-start | bytes 442376 | tf_op jit(solution)/shard_map/ppermute | solution.py:76
  18.6 24.9 %collective-permute-start.16 = (bf16[2,96,384]{2,1,0:T(8,128)(2,1)S(1)}, bf16[2,96,384]{2,1,0:T(8,128)(2,1)S(1)}, u32[]{:S(2)}, u32[]{:S(2)}) collective-permute-start(bf16[2,96,384]{2,1,0:T(8,128)(2,1)S(1)} %maximum_select_fusion.17), channel_id=1, source_target_pairs={{0,16},{8,24},{16,0},{24,8},{1,17},{9,25},{17,1},{25,9},{2,18},{10... | collective-permute-start | bytes 442376 | tf_op jit(solution)/shard_map/ppermute | solution.py:76
  21.2 26.3 %collective-permute-start.17 = (bf16[2,96,384]{2,1,0:T(8,128)(2,1)S(1)}, bf16[2,96,384]{2,1,0:T(8,128)(2,1)S(1)}, u32[]{:S(2)}, u32[]{:S(2)}) collective-permute-start(bf16[2,96,384]{2,1,0:T(8,128)(2,1)S(1)} %maximum_select_fusion.17), channel_id=1, source_target_pairs={{0,24},{8,0},{16,8},{24,16},{1,25},{9,1},{17,9},{25,17},{2,26},{10... | collective-permute-start | bytes 442376 | tf_op jit(solution)/shard_map/ppermute | solution.py:76
  22.6 12.4 %collective-permute-start.8 = (bf16[2,24,1536]{2,1,0:T(8,128)(2,1)S(1)}, bf16[2,24,1536]{2,1,0:T(8,128)(2,1)S(1)}, u32[]{:S(2)}, u32[]{:S(2)}) collective-permute-start(bf16[2,24,1536]{2,1,0:T(8,128)(2,1)S(1)} %maximum_select_fusion.16), channel_id=1, source_target_pairs={{0,8},{8,16},{16,24},{24,0},{1,9},{9,17},{17,25},{25,1},{2,10},{10... | collective-permute-start | bytes 442376 | tf_op jit(solution)/shard_map/ppermute | solution.py:76
  23.5 25.0 %collective-permute-start.9 = (bf16[2,24,1536]{2,1,0:T(8,128)(2,1)S(1)}, bf16[2,24,1536]{2,1,0:T(8,128)(2,1)S(1)}, u32[]{:S(2)}, u32[]{:S(2)}) collective-permute-start(bf16[2,24,1536]{2,1,0:T(8,128)(2,1)S(1)} %maximum_select_fusion.16), channel_id=1, source_target_pairs={{0,16},{8,24},{16,0},{24,8},{1,17},{9,25},{17,1},{25,9},{2,18},{10... | collective-permute-start | bytes 442376 | tf_op jit(solution)/shard_map/ppermute | solution.py:76
  35.0 15.1 %collective-permute-start.10 = (bf16[2,24,1536]{2,1,0:T(8,128)(2,1)S(1)}, bf16[2,24,1536]{2,1,0:T(8,128)(2,1)S(1)}, u32[]{:S(2)}, u32[]{:S(2)}) collective-permute-start(bf16[2,24,1536]{2,1,0:T(8,128)(2,1)S(1)} %maximum_select_fusion.16), channel_id=1, source_target_pairs={{0,24},{8,0},{16,8},{24,16},{1,25},{9,1},{17,9},{25,17},{2,26},{10... | collective-permute-start | bytes 442376 | tf_op jit(solution)/shard_map/ppermute | solution.py:76
  36.0 18.9 %collective-permute-start.1 = (bf16[2,24,1664]{2,1,0:T(8,128)(2,1)S(1)}, bf16[2,24,1664]{2,1,0:T(8,128)(2,1)S(1)}, u32[]{:S(2)}, u32[]{:S(2)}) collective-permute-start(bf16[2,24,1664]{2,1,0:T(8,128)(2,1)S(1)} %maximum_select_fusion.15), channel_id=1, source_target_pairs={{0,8},{8,16},{16,24},{24,0},{1,9},{9,17},{17,25},{25,1},{2,10},{10... | collective-permute-start | bytes 479240 | tf_op jit(solution)/shard_map/ppermute | solution.py:76
  43.5 16.8 %collective-permute-start.2 = (bf16[2,24,1664]{2,1,0:T(8,128)(2,1)S(1)}, bf16[2,24,1664]{2,1,0:T(8,128)(2,1)S(1)}, u32[]{:S(2)}, u32[]{:S(2)}) collective-permute-start(bf16[2,24,1664]{2,1,0:T(8,128)(2,1)S(1)} %maximum_select_fusion.15), channel_id=1, source_target_pairs={{0,16},{8,24},{16,0},{24,8},{1,17},{9,25},{17,1},{25,9},{2,18},{10... | collective-permute-start | bytes 479240 | tf_op jit(solution)/shard_map/ppermute | solution.py:76
  47.5 12.8 %collective-permute-start.3 = (bf16[2,24,1664]{2,1,0:T(8,128)(2,1)S(1)}, bf16[2,24,1664]{2,1,0:T(8,128)(2,1)S(1)}, u32[]{:S(2)}, u32[]{:S(2)}) collective-permute-start(bf16[2,24,1664]{2,1,0:T(8,128)(2,1)S(1)} %maximum_select_fusion.15), channel_id=1, source_target_pairs={{0,24},{8,0},{16,8},{24,16},{1,25},{9,1},{17,9},{25,17},{2,26},{10... | collective-permute-start | bytes 479240 | tf_op jit(solution)/shard_map/ppermute | solution.py:76
  48.5 16.3 %collective-permute-start.18 = (bf16[4,2,96,384]{3,2,1,0:T(8,128)(2,1)S(1)}, bf16[4,2,96,384]{3,2,1,0:T(8,128)(2,1)S(1)}, u32[]{:S(2)}, u32[]{:S(2)}) collective-permute-start(bf16[4,2,96,384]{3,2,1,0:T(8,128)(2,1)S(1)} %bitcast_dynamic-update-slice_fusion.3), channel_id=1, source_target_pairs={{0,4},{4,0},{1,5},{5,1},{2,6},{6,2},{3,7},{7,3},{8,12},{12,8},{9,1... | collective-permute-start | bytes 1769480 | tf_op jit(solution)/shard_map/ppermute | solution.py:72
  50.1 16.5 %collective-permute-start.11 = (bf16[4,2,24,1536]{3,2,1,0:T(8,128)(2,1)S(1)}, bf16[4,2,24,1536]{3,2,1,0:T(8,128)(2,1)S(1)}, u32[]{:S(2)}, u32[]{:S(2)}) collective-permute-start(bf16[4,2,24,1536]{3,2,1,0:T(8,128)(2,1)S(1)} %bitcast_dynamic-update-slice_fusion.7), channel_id=1, source_target_pairs={{0,2},{2,0},{1,3},{3,1},{4,6},{6,4},{5,7},{7,5},{8,10},{10,8},{9,1... | collective-permute-start | bytes 1769480 | tf_op jit(solution)/shard_map/ppermute | solution.py:72
  60.3 18.2 %collective-permute-start.4 = (bf16[4,2,24,1664]{3,2,1,0:T(8,128)(2,1)S(1)}, bf16[4,2,24,1664]{3,2,1,0:T(8,128)(2,1)S(1)}, u32[]{:S(2)}, u32[]{:S(2)}) collective-permute-start(bf16[4,2,24,1664]{3,2,1,0:T(8,128)(2,1)S(1)} %bitcast_dynamic-update-slice_fusion), channel_id=1, source_target_pairs={{0,4},{4,0},{1,5},{5,1},{2,6},{6,2},{3,7},{7,3},{8,12},{12,8},{9,1... | collective-permute-start | bytes 1916936 | tf_op jit(solution)/shard_map/ppermute | solution.py:72
  65.1 29.0 %collective-permute-start.19 = (bf16[2,4,2,96,384]{4,3,2,1,0:T(8,128)(2,1)S(1)}, bf16[2,4,2,96,384]{4,3,2,1,0:T(8,128)(2,1)S(1)}, u32[]{:S(2)}, u32[]{:S(2)}) collective-permute-start(bf16[2,4,2,96,384]{4,3,2,1,0:T(8,128)(2,1)S(1)} %maximum_select_fusion.9), channel_id=1, source_target_pairs={{0,2},{2,0},{1,3},{3,1},{4,6},{6,4},{5,7},{7,5},{8,10},{10,8},{9,1... | collective-permute-start | bytes 3538952 | tf_op jit(solution)/shard_map/ppermute | solution.py:72
  66.8 34.6 %collective-permute-start.12 = (bf16[2,4,2,24,1536]{4,3,2,0,1:T(8,128)(2,1)S(1)}, bf16[2,4,2,24,1536]{4,3,2,0,1:T(8,128)(2,1)S(1)}, u32[]{:S(2)}, u32[]{:S(2)}) collective-permute-start(bf16[2,4,2,24,1536]{4,3,2,0,1:T(8,128)(2,1)S(1)} %maximum_select_fusion.7), channel_id=1, source_target_pairs={{0,4},{4,0},{1,5},{5,1},{2,6},{6,2},{3,7},{7,3},{8,12},{12,8},{9,1... | collective-permute-start | bytes 3538952 | tf_op jit(solution)/shard_map/ppermute | solution.py:72
  78.7 37.7 %collective-permute-start.5 = (bf16[2,4,2,24,1664]{4,3,2,0,1:T(8,128)(2,1)S(1)}, bf16[2,4,2,24,1664]{4,3,2,0,1:T(8,128)(2,1)S(1)}, u32[]{:S(2)}, u32[]{:S(2)}) collective-permute-start(bf16[2,4,2,24,1664]{4,3,2,0,1:T(8,128)(2,1)S(1)} %maximum_select_fusion.6), channel_id=1, source_target_pairs={{0,2},{2,0},{1,3},{3,1},{4,6},{6,4},{5,7},{7,5},{8,10},{10,8},{9,1... | collective-permute-start | bytes 3833864 | tf_op jit(solution)/shard_map/ppermute | solution.py:72
  96.2 25.8 %collective-permute-start.20 = (bf16[3072,384]{1,0:T(8,128)(2,1)}, bf16[3072,384]{1,0:T(8,128)(2,1)}, u32[]{:S(2)}, u32[]{:S(2)}) collective-permute-start(bf16[3072,384]{1,0:T(8,128)(2,1)} %bitcast.55), channel_id=1, source_target_pairs={{0,1},{1,0},{2,3},{3,2},{4,5},{5,4},{6,7},{7,6},{8,9},{9,8},{10,11... | collective-permute-start | bytes 7077896 | tf_op jit(solution)/shard_map/ppermute | solution.py:72
  103.1 26.6 %collective-permute-start.13 = (bf16[768,1536]{1,0:T(8,128)(2,1)}, bf16[768,1536]{1,0:T(8,128)(2,1)}, u32[]{:S(2)}, u32[]{:S(2)}) collective-permute-start(bf16[768,1536]{1,0:T(8,128)(2,1)} %bitcast.41), channel_id=1, source_target_pairs={{0,1},{1,0},{2,3},{3,2},{4,5},{5,4},{6,7},{7,6},{8,9},{9,8},{10,11... | collective-permute-start | bytes 7077896 | tf_op jit(solution)/shard_map/ppermute | solution.py:72
  116.8 20.8 %collective-permute-start.6 = (bf16[768,1664]{1,0:T(8,128)(2,1)S(1)}, bf16[768,1664]{1,0:T(8,128)(2,1)}, u32[]{:S(2)}, u32[]{:S(2)}) collective-permute-start(bf16[768,1664]{1,0:T(8,128)(2,1)S(1)} %bitcast.221), channel_id=1, source_target_pairs={{0,1},{1,0},{2,3},{3,2},{4,5},{5,4},{6,7},{7,6},{8,9},{9,8},{10,11... | collective-permute-start | bytes 7667720 | tf_op jit(solution)/shard_map/ppermute | solution.py:72
  116.8 27.4 %all-to-all-start = ((bf16[8,64,768]{2,1,0:T(8,128)(2,1)}), bf16[8,64,768]{2,1,0:T(8,128)(2,1)S(1)}, u32[]{:S(2)}, u32[]{:S(2)}) async-start(bf16[8,64,768]{2,1,0:T(8,128)(2,1)} %bitcast), calls=%async_computation | async-start | bytes 1572864 | tf_op jit(solution)/shard_map/all_to_all | solution.py:198
  121.3 72.7 %all-gather.4.cloned.1.call-start = ((), (), s32[]{:S(2)}) async-start(), calls=%async_computation.7 | async-start | bytes 3244032 | tf_op jit(solution)/shard_map/all_gather | solution.py:929
  144.3 30.7 %all-to-all-start.1 = ((bf16[8,64,768]{2,1,0:T(8,128)(2,1)}), bf16[8,64,768]{2,1,0:T(8,128)(2,1)S(1)}, u32[]{:S(2)}, u32[]{:S(2)}) async-start(bf16[8,64,768]{2,1,0:T(8,128)(2,1)} %bitcast.58), calls=%async_computation.1 | async-start | bytes 1572864 | tf_op jit(solution)/shard_map/all_to_all | solution.py:198
  175.0 19.0 %all-to-all-start.2 = ((bf16[4,32,4096]{2,1,0:T(8,128)(2,1)}), bf16[4,32,4096]{2,1,0:T(8,128)(2,1)S(1)}, u32[]{:S(2)}, u32[]{:S(2)}) async-start(bf16[4,32,4096]{2,1,0:T(8,128)(2,1)} %bitcast.62), calls=%async_computation.2 | async-start | bytes 2097152 | tf_op jit(solution)/shard_map/all_to_all | solution.py:198
  238.2 52.3 %all-to-all-start.3 = ((bf16[4,32,4096]{2,1,0:T(8,128)(2,1)}), bf16[4,32,4096]{2,1,0:T(8,128)(2,1)S(1)}, u32[]{:S(2)}, u32[]{:S(2)}) async-start(bf16[4,32,4096]{2,1,0:T(8,128)(2,1)} %bitcast.255), calls=%async_computation.3 | async-start | bytes 2097152 | tf_op jit(solution)/shard_map/all_to_all | solution.py:198
  290.1 27.7 %collective-permute-start.21 = (bf16[3072,384]{1,0:T(8,128)(2,1)}, bf16[3072,384]{1,0:T(8,128)(2,1)}, u32[]{:S(2)}, u32[]{:S(2)}) collective-permute-start(bf16[3072,384]{1,0:T(8,128)(2,1)} %get-tuple-element.90), channel_id=1, source_target_pairs={{0,1},{1,0},{2,3},{3,2},{4,5},{5,4},{6,7},{7,6},{8,9},{9,8},{10,11... | collective-permute-start | bytes 7077896 | tf_op jit(solution)/shard_map/ppermute | solution.py:72
  290.6 20.4 %copy-start.5 = (bf16[4,32,4096]{2,1,0:T(8,128)(2,1)}, bf16[4,32,4096]{2,1,0:T(8,128)(2,1)S(1)}, u32[]{:S(2)}) copy-start(bf16[4,32,4096]{2,1,0:T(8,128)(2,1)S(1)} %all-to-all-done.3) | copy-start | bytes 3145732
  290.6 25.9 %all-to-all-start.5 = ((bf16[8,64,768]{2,1,0:T(8,128)(2,1)}), bf16[8,64,768]{2,1,0:T(8,128)(2,1)S(1)}, u32[]{:S(2)}, u32[]{:S(2)}) async-start(bf16[8,64,768]{2,1,0:T(8,128)(2,1)} %bitcast.71), calls=%async_computation.5 | async-start | bytes 1572864 | tf_op jit(solution)/shard_map/all_to_all | solution.py:198
  296.1 134.9 %reduce-scatter.2.cloned.1.call-start = ((), (), s32[]{:S(2)}) async-start(), calls=%async_computation.8 | async-start | bytes 3244032 | tf_op jit(solution)/shard_map/reduce_scatter | solution.py:974
  296.4 16.8 %copy-start.15 = (f32[1,3072]{1,0:T(1,128)S(1)}, f32[1,3072]{1,0:T(1,128)}, u32[]{:S(2)}) copy-start(f32[1,3072]{1,0:T(1,128)} %get-tuple-element.88) | copy-start | bytes 36868
  311.0 12.2 %collective-permute-start.29 = (bf16[768,1536]{1,0:T(8,128)(2,1)}, bf16[768,1536]{1,0:T(8,128)(2,1)}, u32[]{:S(2)}, u32[]{:S(2)}) collective-permute-start(bf16[768,1536]{1,0:T(8,128)(2,1)} %get-tuple-element.96), channel_id=1, source_target_pairs={{0,1},{1,0},{2,3},{3,2},{4,5},{5,4},{6,7},{7,6},{8,9},{9,8},{10,11... | collective-permute-start | bytes 7077896 | tf_op jit(solution)/shard_map/ppermute | solution.py:72
  321.2 41.3 %collective-permute-start.36 = (bf16[4,2,2,96,384]{4,3,2,1,0:T(8,128)(2,1)}, bf16[4,2,2,96,384]{4,3,2,1,0:T(8,128)(2,1)}, u32[]{:S(2)}, u32[]{:S(2)}) collective-permute-start(bf16[4,2,2,96,384]{4,3,2,1,0:T(8,128)(2,1)} %dynamic-slice_bitcast_fusion.1), channel_id=1, source_target_pairs={{0,2},{2,0},{1,3},{3,1},{4,6},{6,4},{5,7},{7,5},{8,10},{10,8},{9,1... | collective-permute-start | bytes 3538952 | tf_op jit(solution)/shard_map/ppermute | solution.py:76
  327.1 31.7 %collective-permute-start.30 = (bf16[4,2,2,24,1536]{4,3,2,1,0:T(8,128)(2,1)S(1)}, bf16[4,2,2,24,1536]{4,3,2,1,0:T(8,128)(2,1)}, u32[]{:S(2)}, u32[]{:S(2)}) collective-permute-start(bf16[4,2,2,24,1536]{4,3,2,1,0:T(8,128)(2,1)S(1)} %dynamic-slice_bitcast_fusion.2), channel_id=1, source_target_pairs={{0,4},{4,0},{1,5},{5,1},{2,6},{6,2},{3,7},{7,3},{8,12},{12,8},{9,1... | collective-permute-start | bytes 3538952 | tf_op jit(solution)/shard_map/ppermute | solution.py:76
  328.6 30.2 %copy-start.3 = (bf16[768,1536]{1,0:T(8,128)(2,1)S(1)}, bf16[768,1536]{1,0:T(8,128)(2,1)}, u32[]{:S(2)}) copy-start(bf16[768,1536]{1,0:T(8,128)(2,1)} %copy-done.2) | copy-start | bytes 7077892
  354.4 101.4 %collective-permute-start.22 = (bf16[768,1664]{1,0:T(8,128)(2,1)}, bf16[768,1664]{1,0:T(8,128)(2,1)}, u32[]{:S(2)}, u32[]{:S(2)}) collective-permute-start(bf16[768,1664]{1,0:T(8,128)(2,1)} %get-tuple-element.94), channel_id=1, source_target_pairs={{0,1},{1,0},{2,3},{3,2},{4,5},{5,4},{6,7},{7,6},{8,9},{9,8},{10,11... | collective-permute-start | bytes 7667720 | tf_op jit(solution)/shard_map/ppermute | solution.py:72
  354.4 38.0 %all-to-all-start.4 = ((bf16[8,64,768]{2,1,0:T(8,128)(2,1)}), bf16[8,64,768]{2,1,0:T(8,128)(2,1)}, u32[]{:S(2)}, u32[]{:S(2)}) async-start(bf16[8,64,768]{2,1,0:T(8,128)(2,1)} %bitcast.262), calls=%async_computation.4 | async-start | bytes 1572864 | tf_op jit(solution)/shard_map/all_to_all | solution.py:198
  360.7 34.2 %collective-permute-start.31 = (bf16[4,2,24,1536]{3,2,1,0:T(8,128)(2,1)S(1)}, bf16[4,2,24,1536]{3,2,1,0:T(8,128)(2,1)}, u32[]{:S(2)}, u32[]{:S(2)}) collective-permute-start(bf16[4,2,24,1536]{3,2,1,0:T(8,128)(2,1)S(1)} %dynamic-slice_bitcast_fusion.6), channel_id=1, source_target_pairs={{0,2},{2,0},{1,3},{3,1},{4,6},{6,4},{5,7},{7,5},{8,10},{10,8},{9,1... | collective-permute-start | bytes 1769480 | tf_op jit(solution)/shard_map/ppermute | solution.py:76
  390.3 46.8 %collective-permute-start.42 = (bf16[2,896,384]{2,1,0:T(8,128)(2,1)}, bf16[2,896,384]{2,1,0:T(8,128)(2,1)}, u32[]{:S(2)}, u32[]{:S(2)}) collective-permute-start(bf16[2,896,384]{2,1,0:T(8,128)(2,1)} %dynamic-slice_bitcast_fusion), channel_id=1, source_target_pairs={{0,1},{1,0},{2,3},{3,2},{4,5},{5,4},{6,7},{7,6},{8,9},{9,8},{10,11... | collective-permute-start | bytes 4128776 | tf_op jit(solution)/shard_map/ppermute | solution.py:76
  390.6 17.3 %collective-permute-start.37 = (bf16[4,2,96,384]{3,2,1,0:T(8,128)(2,1)S(1)}, bf16[4,2,96,384]{3,2,1,0:T(8,128)(2,1)}, u32[]{:S(2)}, u32[]{:S(2)}) collective-permute-start(bf16[4,2,96,384]{3,2,1,0:T(8,128)(2,1)S(1)} %dynamic-slice_bitcast_fusion.5), channel_id=1, source_target_pairs={{0,4},{4,0},{1,5},{5,1},{2,6},{6,2},{3,7},{7,3},{8,12},{12,8},{9,1... | collective-permute-start | bytes 1769480 | tf_op jit(solution)/shard_map/ppermute | solution.py:76
  396.8 35.7 %collective-permute-start.32 = (bf16[2,24,1536]{2,1,0:T(8,128)(2,1)}, bf16[2,24,1536]{2,1,0:T(8,128)(2,1)S(1)}, u32[]{:S(2)}, u32[]{:S(2)}) collective-permute-start(bf16[2,24,1536]{2,1,0:T(8,128)(2,1)} %get-tuple-element.123), channel_id=1, source_target_pairs={{0,8},{8,16},{16,24},{24,0},{1,9},{9,17},{17,25},{25,1},{2,10},{10... | collective-permute-start | bytes 442376 | tf_op jit(solution)/shard_map/ppermute | solution.py:76
  398.3 35.7 %collective-permute-start.33 = (bf16[2,24,1536]{2,1,0:T(8,128)(2,1)S(1)}, bf16[2,24,1536]{2,1,0:T(8,128)(2,1)S(1)}, u32[]{:S(2)}, u32[]{:S(2)}) collective-permute-start(bf16[2,24,1536]{2,1,0:T(8,128)(2,1)S(1)} %get-tuple-element.125), channel_id=1, source_target_pairs={{0,16},{8,24},{16,0},{24,8},{1,17},{9,25},{17,1},{25,9},{2,18},{10... | collective-permute-start | bytes 442376 | tf_op jit(solution)/shard_map/ppermute | solution.py:76
  408.0 27.7 %collective-permute-start.34 = (bf16[2,24,1536]{2,1,0:T(8,128)(2,1)S(1)}, bf16[2,24,1536]{2,1,0:T(8,128)(2,1)S(1)}, u32[]{:S(2)}, u32[]{:S(2)}) collective-permute-start(bf16[2,24,1536]{2,1,0:T(8,128)(2,1)S(1)} %get-tuple-element.124), channel_id=1, source_target_pairs={{0,24},{8,0},{16,8},{24,16},{1,25},{9,1},{17,9},{25,17},{2,26},{10... | collective-permute-start | bytes 442376 | tf_op jit(solution)/shard_map/ppermute | solution.py:76
  432.5 8.8 %collective-permute-start.38 = (bf16[2,96,384]{2,1,0:T(8,128)(2,1)S(1)}, bf16[2,96,384]{2,1,0:T(8,128)(2,1)S(1)}, u32[]{:S(2)}, u32[]{:S(2)}) collective-permute-start(bf16[2,96,384]{2,1,0:T(8,128)(2,1)S(1)} %get-tuple-element.120), channel_id=1, source_target_pairs={{0,8},{8,16},{16,24},{24,0},{1,9},{9,17},{17,25},{25,1},{2,10},{10... | collective-permute-start | bytes 442376 | tf_op jit(solution)/shard_map/ppermute | solution.py:76
  434.0 10.8 %collective-permute-start.39 = (bf16[2,96,384]{2,1,0:T(8,128)(2,1)S(1)}, bf16[2,96,384]{2,1,0:T(8,128)(2,1)S(1)}, u32[]{:S(2)}, u32[]{:S(2)}) collective-permute-start(bf16[2,96,384]{2,1,0:T(8,128)(2,1)S(1)} %get-tuple-element.122), channel_id=1, source_target_pairs={{0,16},{8,24},{16,0},{24,8},{1,17},{9,25},{17,1},{25,9},{2,18},{10... | collective-permute-start | bytes 442376 | tf_op jit(solution)/shard_map/ppermute | solution.py:76
  435.6 9.2 %collective-permute-start.40 = (bf16[2,96,384]{2,1,0:T(8,128)(2,1)S(1)}, bf16[2,96,384]{2,1,0:T(8,128)(2,1)S(1)}, u32[]{:S(2)}, u32[]{:S(2)}) collective-permute-start(bf16[2,96,384]{2,1,0:T(8,128)(2,1)S(1)} %get-tuple-element.121), channel_id=1, source_target_pairs={{0,24},{8,0},{16,8},{24,16},{1,25},{9,1},{17,9},{25,17},{2,26},{10... | collective-permute-start | bytes 442376 | tf_op jit(solution)/shard_map/ppermute | solution.py:76
  439.3 14.7 %collective-permute-start.43 = (bf16[896,384]{1,0:T(8,128)(2,1)S(1)}, bf16[896,384]{1,0:T(8,128)(2,1)S(1)}, u32[]{:S(2)}, u32[]{:S(2)}) collective-permute-start(bf16[896,384]{1,0:T(8,128)(2,1)S(1)} %dynamic-slice_bitcast_fusion.3), channel_id=1, source_target_pairs={{0,2},{2,0},{1,3},{3,1},{4,6},{6,4},{5,7},{7,5},{8,10},{10,8},{9,1... | collective-permute-start | bytes 2064392 | tf_op jit(solution)/shard_map/ppermute | solution.py:76
  454.3 7.3 %collective-permute-start.44 = (bf16[4,112,384]{2,1,0:T(8,128)(2,1)S(1)}, bf16[4,112,384]{2,1,0:T(8,128)(2,1)S(1)}, u32[]{:S(2)}, u32[]{:S(2)}) collective-permute-start(bf16[4,112,384]{2,1,0:T(8,128)(2,1)S(1)} %dynamic-slice_bitcast_fusion.7), channel_id=1, source_target_pairs={{0,4},{4,0},{1,5},{5,1},{2,6},{6,2},{3,7},{7,3},{8,12},{12,8},{9,1... | collective-permute-start | bytes 1032200 | tf_op jit(solution)/shard_map/ppermute | solution.py:76
  458.6 26.2 %collective-permute-start.23 = (bf16[4,2,2,24,1664]{4,3,2,0,1:T(8,128)(2,1)S(1)}, bf16[4,2,2,24,1664]{4,3,2,0,1:T(8,128)(2,1)S(1)}, u32[]{:S(2)}, u32[]{:S(2)}) collective-permute-start(bf16[4,2,2,24,1664]{4,3,2,0,1:T(8,128)(2,1)S(1)} %bitcast.252), channel_id=1, source_target_pairs={{0,2},{2,0},{1,3},{3,1},{4,6},{6,4},{5,7},{7,5},{8,10},{10,8},{9,1... | collective-permute-start | bytes 3833864 | tf_op jit(solution)/shard_map/ppermute | solution.py:76
  461.8 6.5 %collective-permute-start.45 = (bf16[112,384]{1,0:T(8,128)(2,1)S(1)}, bf16[112,384]{1,0:T(8,128)(2,1)S(1)}, u32[]{:S(2)}, u32[]{:S(2)}) collective-permute-start(bf16[112,384]{1,0:T(8,128)(2,1)S(1)} %get-tuple-element.126), channel_id=1, source_target_pairs={{0,8},{8,16},{16,24},{24,0},{1,9},{9,17},{17,25},{25,1},{2,10},{10... | collective-permute-start | bytes 258056 | tf_op jit(solution)/shard_map/ppermute | solution.py:76
  462.3 7.2 %collective-permute-start.46 = (bf16[112,384]{1,0:T(8,128)(2,1)S(1)}, bf16[112,384]{1,0:T(8,128)(2,1)S(1)}, u32[]{:S(2)}, u32[]{:S(2)}) collective-permute-start(bf16[112,384]{1,0:T(8,128)(2,1)S(1)} %get-tuple-element.128), channel_id=1, source_target_pairs={{0,16},{8,24},{16,0},{24,8},{1,17},{9,25},{17,1},{25,9},{2,18},{10... | collective-permute-start | bytes 258056 | tf_op jit(solution)/shard_map/ppermute | solution.py:76
  463.7 5.9 %collective-permute-start.47 = (bf16[112,384]{1,0:T(8,128)(2,1)S(1)}, bf16[112,384]{1,0:T(8,128)(2,1)S(1)}, u32[]{:S(2)}, u32[]{:S(2)}) collective-permute-start(bf16[112,384]{1,0:T(8,128)(2,1)S(1)} %get-tuple-element.127), channel_id=1, source_target_pairs={{0,24},{8,0},{16,8},{24,16},{1,25},{9,1},{17,9},{25,17},{2,26},{10... | collective-permute-start | bytes 258056 | tf_op jit(solution)/shard_map/ppermute | solution.py:76
  466.2 5.0 collective-permute-start.41
  468.2 19.8 %collective-permute-start.35 = (bf16[24,1536]{1,0:T(8,128)(2,1)S(1)}, bf16[24,1536]{1,0:T(8,128)(2,1)S(1)}, u32[]{:S(2)}, u32[]{:S(2)}) collective-permute-start(bf16[24,1536]{1,0:T(8,128)(2,1)S(1)} %fusion.23), channel_id=1, source_target_pairs={{0,1},{1,0},{2,3},{3,2},{4,5},{5,4},{6,7},{7,6},{8,9},{9,8},{10,11... | collective-permute-start | bytes 221192 | tf_op jit(solution)/shard_map/ppermute | solution.py:72
  469.7 7.4 %collective-permute-start.48 = (bf16[112,384]{1,0:T(8,128)(2,1)S(1)}, bf16[112,384]{1,0:T(8,128)(2,1)S(1)}, u32[]{:S(2)}, u32[]{:S(2)}) collective-permute-start(bf16[112,384]{1,0:T(8,128)(2,1)S(1)} %get-tuple-element.110), channel_id=1, source_target_pairs={{0,8},{8,16},{16,24},{24,0},{1,9},{9,17},{17,25},{25,1},{2,10},{10... | collective-permute-start | bytes 258056 | tf_op jit(solution)/shard_map/ppermute | solution.py:76
  471.3 7.7 %collective-permute-start.49 = (bf16[112,384]{1,0:T(8,128)(2,1)S(1)}, bf16[112,384]{1,0:T(8,128)(2,1)S(1)}, u32[]{:S(2)}, u32[]{:S(2)}) collective-permute-start(bf16[112,384]{1,0:T(8,128)(2,1)S(1)} %get-tuple-element.110), channel_id=1, source_target_pairs={{0,16},{8,24},{16,0},{24,8},{1,17},{9,25},{17,1},{25,9},{2,18},{10... | collective-permute-start | bytes 258056 | tf_op jit(solution)/shard_map/ppermute | solution.py:76
  473.4 12.3 %collective-permute-start.50 = (bf16[112,384]{1,0:T(8,128)(2,1)S(1)}, bf16[112,384]{1,0:T(8,128)(2,1)S(1)}, u32[]{:S(2)}, u32[]{:S(2)}) collective-permute-start(bf16[112,384]{1,0:T(8,128)(2,1)S(1)} %get-tuple-element.110), channel_id=1, source_target_pairs={{0,24},{8,0},{16,8},{24,16},{1,25},{9,1},{17,9},{25,17},{2,26},{10... | collective-permute-start | bytes 258056 | tf_op jit(solution)/shard_map/ppermute | solution.py:76
  485.2 20.8 %collective-permute-start.24 = (bf16[4,2,24,1664]{3,2,1,0:T(8,128)(2,1)S(1)}, bf16[4,2,24,1664]{3,2,1,0:T(8,128)(2,1)S(1)}, u32[]{:S(2)}, u32[]{:S(2)}) collective-permute-start(bf16[4,2,24,1664]{3,2,1,0:T(8,128)(2,1)S(1)} %dynamic-slice_bitcast_fusion.4), channel_id=1, source_target_pairs={{0,4},{4,0},{1,5},{5,1},{2,6},{6,2},{3,7},{7,3},{8,12},{12,8},{9,1... | collective-permute-start | bytes 1916936 | tf_op jit(solution)/shard_map/ppermute | solution.py:76
  485.8 18.4 %collective-permute-start.51 = (bf16[4,112,384]{2,1,0:T(8,128)(2,1)S(1)}, bf16[4,112,384]{2,1,0:T(8,128)(2,1)S(1)}, u32[]{:S(2)}, u32[]{:S(2)}) collective-permute-start(bf16[4,112,384]{2,1,0:T(8,128)(2,1)S(1)} %bitcast_dynamic-update-slice_fusion.11), channel_id=1, source_target_pairs={{0,4},{4,0},{1,5},{5,1},{2,6},{6,2},{3,7},{7,3},{8,12},{12,8},{9,1... | collective-permute-start | bytes 1032200 | tf_op jit(solution)/shard_map/ppermute | solution.py:72
  506.2 7.3 %collective-permute-start.25 = (bf16[2,24,1664]{2,1,0:T(8,128)(2,1)S(1)}, bf16[2,24,1664]{2,1,0:T(8,128)(2,1)S(1)}, u32[]{:S(2)}, u32[]{:S(2)}) collective-permute-start(bf16[2,24,1664]{2,1,0:T(8,128)(2,1)S(1)} %get-tuple-element.117), channel_id=1, source_target_pairs={{0,8},{8,16},{16,24},{24,0},{1,9},{9,17},{17,25},{25,1},{2,10},{10... | collective-permute-start | bytes 479240 | tf_op jit(solution)/shard_map/ppermute | solution.py:76
  507.0 9.6 %collective-permute-start.26 = (bf16[2,24,1664]{2,1,0:T(8,128)(2,1)S(1)}, bf16[2,24,1664]{2,1,0:T(8,128)(2,1)S(1)}, u32[]{:S(2)}, u32[]{:S(2)}) collective-permute-start(bf16[2,24,1664]{2,1,0:T(8,128)(2,1)S(1)} %get-tuple-element.119), channel_id=1, source_target_pairs={{0,16},{8,24},{16,0},{24,8},{1,17},{9,25},{17,1},{25,9},{2,18},{10... | collective-permute-start | bytes 479240 | tf_op jit(solution)/shard_map/ppermute | solution.py:76
  508.1 8.5 %collective-permute-start.27 = (bf16[2,24,1664]{2,1,0:T(8,128)(2,1)S(1)}, bf16[2,24,1664]{2,1,0:T(8,128)(2,1)S(1)}, u32[]{:S(2)}, u32[]{:S(2)}) collective-permute-start(bf16[2,24,1664]{2,1,0:T(8,128)(2,1)S(1)} %get-tuple-element.118), channel_id=1, source_target_pairs={{0,24},{8,0},{16,8},{24,16},{1,25},{9,1},{17,9},{25,17},{2,26},{10... | collective-permute-start | bytes 479240 | tf_op jit(solution)/shard_map/ppermute | solution.py:76
  516.8 1.3 collective-permute-start.28
  (14 other events, 75.9 us)
Sparse Core Ops, SparseCore 0:
  16.0 28.6 all-gather.5
  125.6 68.2 all-gather.3
  314.2 116.7 reduce-scatter.1
where the time goes:
time: 531 us; the launch traced here: 529 us
  Pallas kernels  186 us (35%)
  waiting for transfers between devices  147 us (28%)
  starting transfers between devices  99.2 us (19%)
  other arithmetic  53 us (10%)
  local copies, waits for them, and re-layouts  28.7 us (5%)
  between operations  14.9 us (3%)
    pallas_call x9, Pallas kernels, local_call(): pl.pallas_call(skip_operands(kernel, len(operands), len(after)), out_shap...  186 us
    ppermute x33, waiting for transfers between devices, turn(): lax.ppermute(value, axis, [(k, (k + step) % size) for k in range(size)])  61.5 us
    ppermute x19, waiting for transfers between devices, swap(): return lax.ppermute(value, axis, [(0, 1), (1, 0)])  60.9 us
    ppermute x33, starting transfers between devices, turn(): lax.ppermute(value, axis, [(k, (k + step) % size) for k in range(size)])  58.1 us
    all_to_all x6, starting transfers between devices, swap_blocks(): return lax.all_to_all(value, axes, 0, 0, tiled=True)  27.9 us
    select_n x9, other arithmetic, keep_order(): jnp.where(place == 0, jnp.concatenate([first, second], axis), jnp.concate...  23.8 us
    reduce_scatter x1, waiting for transfers between devices, body(): lax.psum_scatter(grad_up, both, scatter_dimension=0, tiled=True).astype(F32)  18.2 us
    ppermute x19, starting transfers between devices, swap(): return lax.ppermute(value, axis, [(0, 1), (1, 0)])  12.9 us
  transfers between devices with their start and end apart: 61, of which 26 were waited for; matrix products, arithmetic and copies ran while one was open for 14% of the time, Pallas kernels for 27%

commit v1 on v0

--- a/solution.py
+++ b/solution.py
@@ -822,6 +822,18 @@
     )[0]
 
 
+def gate(value, *after):
+    anywhere = pl.BlockSpec(memory_space=pl.ANY)
+    return pl.pallas_call(
+        lambda *refs: None,
+        out_shape=jax.ShapeDtypeStruct(value.shape, value.dtype),
+        in_specs=[anywhere] * (1 + len(after)),
+        out_specs=anywhere,
+        input_output_aliases={0: 0},
+        cost_estimate=pl.CostEstimate(flops=0, bytes_accessed=0, transcendentals=0),
+    )(value, *after)
+
+
 def attention(rows, weight, after=()):
     flat = (PATCHES, D)
     return local_call(
@@ -971,7 +983,7 @@
         grad_up, grad_tap_rows, grad_second, grad_mlp, fc2_shift_sums = up_back(
             grad_up_block, grad_up_tap, block_out, tap_rows, up_full,
         )
-        grad_ups = lax.psum_scatter(grad_up, both, scatter_dimension=0, tiled=True).astype(F32)
+        grad_ups = lax.psum_scatter(grad_up, both, scatter_dimension=0, tiled=True)
         keep, send, grad_hidden, fc1_shift_sums = fc2_back(
             place, grad_mlp, active, slope, fc2_full
         )
@@ -992,7 +1004,7 @@
             rows_bf, first_weight, vectors, small, after=(sum_fc2.value,),
         )
         sum_fc2.link()
-        sum_first = RowSum(keep, send, axes.links_a, axes)
+        sum_first = RowSum(keep, send, axes.links_b, axes)
         conv_grads = decoder_weights(
             grad_c2, hidden_maps, grad_c1, joined.reshape(SIDE, PLANE, 2 * DEC), grad_skip,
             shape=raw.shape, after=(sum_fc1.value, sum_fc2.value),
@@ -1015,6 +1027,7 @@
         for item in sums:
             while item.left:
                 item.link()
+        grad_ups = gate(grad_ups, sum_first.value).astype(F32)
         grad_fc2, grad_fc1, first_grads = (item.finish() for item in sums)
         small_sums = first_grads[:, 4 * D : 4 * D + extra]
         return (

time: 531 us -> 516 us (0.972)
  waiting for transfers between devices: 147 us -> 128 us
    reduce_scatter x1, waiting for transfers between devices: 18.2 us -> 0.02 us  [body(): grad_ups = lax.psum_scatter(grad_up, both, scatter_dimension=0, tiled=True)]
    ppermute x19, waiting for transfers between devices: 60.9 us -> 48.9 us  [swap(): return lax.ppermute(value, axis, [(0, 1), (1, 0)])]
    ppermute x33, waiting for transfers between devices: 61.5 us -> 72 us  [turn(): lax.ppermute(value, axis, [(k, (k + step) % size) for k in range(size)])]
  transfers between devices with their start and end apart: 61 -> 61, of which waited for: 26 -> 27; matrix products, arithmetic and copies ran while one was open for 14% -> 14% of each run, Pallas kernels for 27% -> 28%
where the time goes in v1:
time: 516 us; the launch traced here: 513 us
  Pallas kernels  186 us (36%)
  waiting for transfers between devices  128 us (25%)
  starting transfers between devices  102 us (20%)
  other arithmetic  52.6 us (10%)
  local copies, waits for them, and re-layouts  29.6 us (6%)
  between operations  15 us (3%)
    pallas_call x9, Pallas kernels, local_call(): pl.pallas_call(skip_operands(kernel, len(operands), len(after)), out_shap...  186 us
    ppermute x33, waiting for transfers between devices, turn(): lax.ppermute(value, axis, [(k, (k + step) % size) for k in range(size)])  72 us
    ppermute x33, starting transfers between devices, turn(): lax.ppermute(value, axis, [(k, (k + step) % size) for k in range(size)])  61.4 us
    ppermute x19, waiting for transfers between devices, swap(): return lax.ppermute(value, axis, [(0, 1), (1, 0)])  48.9 us
    all_to_all x6, starting transfers between devices, swap_blocks(): return lax.all_to_all(value, axes, 0, 0, tiled=True)  27.9 us
    select_n x9, other arithmetic, keep_order(): jnp.where(place == 0, jnp.concatenate([first, second], axis), jnp.concate...  23.9 us
    ppermute x19, starting transfers between devices, swap(): return lax.ppermute(value, axis, [(0, 1), (1, 0)])  12.9 us
  transfers between devices with their start and end apart: 61, of which 27 were waited for; matrix products, arithmetic and copies ran while one was open for 14% of the time, Pallas kernels for 28%

profile of v1, /device:TPU:0, one launch (start us, length us, event | category | flops | bytes accessed | tf_op | source)
XLA Modules:
  0.0 513.1 jit_solution(2022072263559800034)
XLA Ops:
  13.8 2.0 pad_maximum_fusion.4
  16.0 2.7 collective-permute-start.15
  18.6 2.6 collective-permute-start.16
  24.0 10.9 %collective-permute-done.8 = bf16[2,24,1536]{2,1,0:T(8,128)(2,1)S(1)} collective-permute-done((bf16[2,24,1536]{2,1,0:T(8,128)(2,1)S(1)}, bf16[2,24,1536]{2,1,0:T(8,128)(2,1)S(1)}, u32[]{:S(2)}, u32[]{:S(2)}) %collective-permute-start.8) | collective-permute-done | bytes 147488 | tf_op jit(solution)/shard_map/ppermute | solution.py:76
  36.0 7.5 %collective-permute-start.1 = (bf16[2,24,1664]{2,1,0:T(8,128)(2,1)S(1)}, bf16[2,24,1664]{2,1,0:T(8,128)(2,1)S(1)}, u32[]{:S(2)}, u32[]{:S(2)}) collective-permute-start(bf16[2,24,1664]{2,1,0:T(8,128)(2,1)S(1)} %maximum_select_fusion.15), channel_id=1, source_target_pairs={{0,8},{8,16},{16,24},{24,0},{1,9},{9,17},{17,25},{25,1},{2,10},{10... | collective-permute-start | bytes 479240 | tf_op jit(solution)/shard_map/ppermute | solution.py:76
  43.5 4.0 collective-permute-start.2
  51.7 3.2 collective-permute-done.1
  54.9 5.3 %collective-permute-done.2 = bf16[2,24,1664]{2,1,0:T(8,128)(2,1)S(1)} collective-permute-done((bf16[2,24,1664]{2,1,0:T(8,128)(2,1)S(1)}, bf16[2,24,1664]{2,1,0:T(8,128)(2,1)S(1)}, u32[]{:S(2)}, u32[]{:S(2)}) %collective-permute-start.2) | collective-permute-done | bytes 159776 | tf_op jit(solution)/shard_map/ppermute | solution.py:76
  61.9 3.0 collective-permute-done.18
  68.9 9.6 %collective-permute-done.4 = bf16[4,2,24,1664]{3,2,1,0:T(8,128)(2,1)S(1)} collective-permute-done((bf16[4,2,24,1664]{3,2,1,0:T(8,128)(2,1)S(1)}, bf16[4,2,24,1664]{3,2,1,0:T(8,128)(2,1)S(1)}, u32[]{:S(2)}, u32[]{:S(2)}) %collective-permute-start.4) | collective-permute-done | bytes 639008 | tf_op jit(solution)/shard_map/ppermute | solution.py:72
  80.6 13.5 %collective-permute-done.19 = bf16[2,4,2,96,384]{4,3,2,1,0:T(8,128)(2,1)S(1)} collective-permute-done((bf16[2,4,2,96,384]{4,3,2,1,0:T(8,128)(2,1)S(1)}, bf16[2,4,2,96,384]{4,3,2,1,0:T(8,128)(2,1)S(1)}, u32[]{:S(2)}, u32[]{:S(2)}) %collective-permute-start.19) | collective-permute-done | bytes 1179680 | tf_op jit(solution)/shard_map/ppermute | solution.py:72
  94.5 1.7 copy.73
  96.4 5.0 collective-permute-done.12
  101.4 1.8 maximum_select_fusion.4
  103.1 13.3 %collective-permute-done.5 = bf16[2,4,2,24,1664]{4,3,2,0,1:T(8,128)(2,1)S(1)} collective-permute-done((bf16[2,4,2,24,1664]{4,3,2,0,1:T(8,128)(2,1)S(1)}, bf16[2,4,2,24,1664]{4,3,2,0,1:T(8,128)(2,1)S(1)}, u32[]{:S(2)}, u32[]{:S(2)}) %collective-permute-start.5) | collective-permute-done | bytes 1277984 | tf_op jit(solution)/shard_map/ppermute | solution.py:72
  116.8 4.4 all-to-all-start
  122.0 7.8 %maximum_select_fusion.2.refs_3_.refs_4_ = bf16[3072,768]{1,0:T(8,128)(2,1)} fusion(bf16[3072,384]{1,0:T(8,128)(2,1)} %collective-permute-done.20, bf16[3072,384]{1,0:T(8,128)(2,1)} %bitcast.55, pred[]{:T(512)S(6)} %eq.56), kind=kLoop, calls=%fused_computation.3 | loop fusion | flops 21233664 | bytes 9437185 | tf_op jit(solution)/shard_map/jit(_where)/select_n | solution.py:97
  129.8 7.8 %maximum_select_fusion.1.refs_2_.refs_5_ = bf16[768,3072]{1,0:T(8,128)(2,1)} fusion(bf16[768,1536]{1,0:T(8,128)(2,1)} %collective-permute-done.13, bf16[768,1536]{1,0:T(8,128)(2,1)} %bitcast.41, pred[]{:T(512)S(6)} %eq.56), kind=kLoop, calls=%fused_computation.2 | loop fusion | flops 21233664 | bytes 9437185 | tf_op jit(solution)/shard_map/jit(_where)/select_n | solution.py:97
  137.7 6.6 %maximum_select_fusion.refs_1_.refs_6_.refs_9_ = bf16[768,3328]{1,0:T(8,128)(2,1)} fusion(bf16[768,1664]{1,0:T(8,128)(2,1)} %collective-permute-done.6, bf16[768,1664]{1,0:T(8,128)(2,1)S(1)} %bitcast.222, pred[]{:T(512)S(6)} %eq.56), kind=kLoop, calls=%fused_computation | loop fusion | flops 23003136 | bytes 10223617 | tf_op jit(solution)/shard_map/jit(_where)/select_n | solution.py:97
  144.3 6.2 %all-to-all-start.1 = ((bf16[8,64,768]{2,1,0:T(8,128)(2,1)}), bf16[8,64,768]{2,1,0:T(8,128)(2,1)S(1)}, u32[]{:S(2)}, u32[]{:S(2)}) async-start(bf16[8,64,768]{2,1,0:T(8,128)(2,1)} %bitcast.58), calls=%async_computation.1 | async-start | bytes 1572864 | tf_op jit(solution)/shard_map/all_to_all | solution.py:198
  150.6 16.9 %shard_map.364 = (bf16[512,768]{1,0:T(8,128)(2,1)}, bf16[512,2304]{1,0:T(8,128)(2,1)}, bf16[12,512,512]{2,1,0:T(8,128)(2,1)}, bf16[512,768]{1,0:T(8,128)(2,1)}, ...) custom-call(bf16[512,768]{1,0:T(8,128)(2,1)} %bitcast.257, ...), custom_call_target="tpu_custom_call" | custom-call | flops 30000001024 | bytes 30000001024 | tf_op jit(solution)/shard_map/pallas_call | solution.py:771
  170.4 4.6 all-to-all-done.1
  175.0 3.8 all-to-all-start.2
  178.9 14.0 %shard_map.365 = (bf16[512,3072]{1,0:T(8,128)(2,1)}, bf16[512,3072]{1,0:T(8,128)(2,1)}, bf16[512,768]{1,0:T(8,128)(2,1)}) custom-call(bf16[512,768]{1,0:T(8,128)(2,1)} %get-tuple-element.61.refs_0_.refs_2_, f32[512,768]{1,0:T(8,128)} %get-tuple-element.62.refs_1_.refs_3_, bf16[768,3072]{1,0:T(8,128)(2,1)} %maximum_select_fusion.1.refs_2_.refs_5_, ...), custom_call_target="tpu_custom_call" | custom-call | flops 30000001024 | bytes 30000001024 | tf_op jit(solution)/shard_map/pallas_call | solution.py:771
  195.0 43.3 %shard_map.366 = (bf16[8,2,8,2,16,256]{5,4,3,2,1,0:T(8,128)(2,1)}, bf16[16,256,128]{2,1,0:T(8,128)(2,1)}, f32[16,256,128]{2,1,0:T(8,128)}, f32[1,128]{1,0:T(1,12...) custom-call(bf16[512,768]{1,0:T(8,128)(2,1)} %get-tuple-element.65.refs_0_.refs_2_, ...), custom_call_target="tpu_custom_call" | custom-call | flops 30000001024 | bytes 30000001024 | tf_op jit(solution)/shard_map/pallas_call | solution.py:771
  238.3 3.5 all-to-all-start.3
  241.8 25.3 %shard_map.367 = (bf16[16,256,128]{2,1,0:T(8,128)(2,1)}, bf16[512,1024]{1,0:T(8,128)(2,1)}, bf16[512,1024]{1,0:T(8,128)(2,1)}) custom-call(bf16[16,256,128]{2,1,0:T(8,128)(2,1)} %get-tuple-element.68.refs_0_, bf16[16,256,128]{2,1,0:T(8,128)(2,1)} %get-tuple-element.69.refs_1_.refs_4_, f32[16,256,128]{2,1,0:T(8,128)} %get-tuple-element.70.refs_2_, ...), custom_call_target="tpu_custom_call" | custom-call | flops 30000001024 | bytes 30000001024 | tf_op jit(solution)/shard_map/pallas_call | solution.py:771
  267.1 9.1 %shard_map.368 = (bf16[768,2048]{1,0:T(8,128)(2,1)}, bf16[512,768]{1,0:T(8,128)(2,1)}, f32[512,768]{1,0:T(8,128)}, bf16[512,768]{1,0:T(8,128)(2,1)}, f32[1,768]{1,0:T(1,128)}) custom-call(bf16[512,1024]{1,0:T(8,128)(2,1)} %get-tuple-element.72.refs_0_, bf16[512,1024]{1,0:T(8,128)(2,1)} %get-tuple-element.73.refs_1_, ...), custom_call_target="tpu_custom_call" | custom-call | flops 30000001024 | bytes 30000001024 | tf_op jit(solution)/shard_map/pallas_call | solution.py:771
  276.2 13.9 %shard_map.369 = (bf16[3072,384]{1,0:T(8,128)(2,1)}, bf16[3072,384]{1,0:T(8,128)(2,1)}, bf16[512,3072]{1,0:T(8,128)(2,1)}, f32[1,3072]{1,0:T(1,128)}) custom-call(s32[1]{0:T(128)} %bitcast.66.refs_0_, bf16[512,768]{1,0:T(8,128)(2,1)} %get-tuple-element.74.refs_1_, bf16[512,3072]{1,0:T(8,128)(2,1)} %get-tuple-element.75.refs_2_, ...), custom_call_target="tpu_custom_call" | custom-call | flops 30000001024 | bytes 30000001024 | tf_op jit(solution)/shard_map/pallas_call | solution.py:771
  290.6 5.5 %all-to-all-start.5 = ((bf16[8,64,768]{2,1,0:T(8,128)(2,1)}), bf16[8,64,768]{2,1,0:T(8,128)(2,1)S(1)}, u32[]{:S(2)}, u32[]{:S(2)}) async-start(bf16[8,64,768]{2,1,0:T(8,128)(2,1)} %bitcast.71), calls=%async_computation.5 | async-start | bytes 1572864 | tf_op jit(solution)/shard_map/all_to_all | solution.py:198
  296.4 14.6 %shard_map.370 = (bf16[768,1536]{1,0:T(8,128)(2,1)}, bf16[768,1536]{1,0:T(8,128)(2,1)}, f32[512,768]{1,0:T(8,128)}, bf16[512,768]{1,0:T(8,128)(2,1)}, bf16[512,768]{1,0:T(8,128)(2,1)}, /*index=5*/f32[8,768]{1,0:T(8,128)}) custom-call(s32[1]{0:T(128)} %bitcast.66.refs_0_, bf16[512,3072]{1,0:T(8,128)(2,1)} %get-tuple-element.77.refs_1_, ...), custom_call_target="tpu_custom_call" | custom-call | flops 30000001024 | bytes 30000001024 | tf_op jit(solution)/shard_map/pallas_call | solution.py:771
  317.8 2.3 add_convert_fusion.2
  321.3 2.0 collective-permute-start.36
  323.2 2.3 add_convert_fusion.1
  328.6 25.8 %shard_map.371 = (bf16[768,1664]{1,0:T(8,128)(2,1)}, bf16[768,1664]{1,0:T(8,128)(2,1)}, bf16[512,768]{1,0:T(8,128)(2,1)}) custom-call(s32[1]{0:T(128)} %bitcast.66.refs_0_, bf16[512,768]{1,0:T(8,128)(2,1)} %get-tuple-element.79.refs_1_, bf16[512,768]{1,0:T(8,128)(2,1)} %get-tuple-element.80.refs_2_, f32[512,768]{1,0:T(8,128)} %get-tuple-element.81.refs_3_, ...), custom_call_target="tpu_custom_call" | custom-call | flops 30000001024 | bytes 30000001024 | tf_op jit(solution)/shard_map/pallas_call | solution.py:771
  354.5 4.4 all-to-all-start.4
  358.9 1.8 fusion.3
  360.7 1.9 collective-permute-start.31
  362.6 2.6 fusion.2.refs_6_
  365.2 22.5 %shard_map.373 = bf16[4,28,32,384]{3,2,1,0:T(8,128)(2,1)} custom-call(bf16[16,256,128]{2,1,0:T(8,128)(2,1)} %get-tuple-element.68.refs_0_, bf16[16,256,128]{2,1,0:T(8,128)(2,1)} %get-tuple-element.98.refs_1_, bf16[16,256,128]{2,1,0:T(8,128)(2,1)} %get-tuple-element.99.refs_2_, bf16[16,256,256]{2,1,0:T(8,128)(2,1)} %bitcast.280, ...), custom_call_target="tpu_custom_call" | custom-call | flops 30000001024 | bytes 30000001024 | tf_op jit(solution)/shard_map/pallas_call | solution.py:771
  387.7 2.7 dynamic-slice_bitcast_fusion
  390.7 1.8 collective-permute-start.37
  392.5 2.4 bitcast_convert_fusion.1
  397.7 2.4 collective-permute-start.33
  400.1 7.9 %collective-permute-done.37 = bf16[4,2,96,384]{3,2,1,0:T(8,128)(2,1)} collective-permute-done((bf16[4,2,96,384]{3,2,1,0:T(8,128)(2,1)S(1)}, bf16[4,2,96,384]{3,2,1,0:T(8,128)(2,1)}, u32[]{:S(2)}, u32[]{:S(2)}) %collective-permute-start.37) | collective-permute-done | bytes 589856 | tf_op jit(solution)/shard_map/ppermute | solution.py:76
  408.0 3.6 collective-permute-start.34
  414.2 2.1 collective-permute-done.34
  416.3 3.8 collective-permute-start.40
  420.2 1.7 fusion
  422.1 5.6 %collective-permute-done.39 = bf16[2,96,384]{2,1,0:T(8,128)(2,1)S(1)} collective-permute-done((bf16[2,96,384]{2,1,0:T(8,128)(2,1)S(1)}, bf16[2,96,384]{2,1,0:T(8,128)(2,1)S(1)}, u32[]{:S(2)}, u32[]{:S(2)}) %collective-permute-start.39) | collective-permute-done | bytes 147488 | tf_op jit(solution)/shard_map/ppermute | solution.py:76
  428.0 9.0 %collective-permute-done.43 = bf16[896,384]{1,0:T(8,128)(2,1)S(1)} collective-permute-done((bf16[896,384]{1,0:T(8,128)(2,1)S(1)}, bf16[896,384]{1,0:T(8,128)(2,1)S(1)}, u32[]{:S(2)}, u32[]{:S(2)}) %collective-permute-start.43) | collective-permute-done | bytes 688160 | tf_op jit(solution)/shard_map/ppermute | solution.py:76
  438.5 2.4 add_convert_fusion
  442.1 6.2 %collective-permute-done.44 = bf16[4,112,384]{2,1,0:T(8,128)(2,1)S(1)} collective-permute-done((bf16[4,112,384]{2,1,0:T(8,128)(2,1)S(1)}, bf16[4,112,384]{2,1,0:T(8,128)(2,1)S(1)}, u32[]{:S(2)}, u32[]{:S(2)}) %collective-permute-start.44) | collective-permute-done | bytes 344096 | tf_op jit(solution)/shard_map/ppermute | solution.py:76
  449.9 2.6 collective-permute-start.47
  452.7 2.2 collective-permute-done.45
  457.9 1.9 collective-permute-start.49
  460.3 3.3 collective-permute-done.48
  463.7 1.9 collective-permute-done.49
  465.6 5.6 %collective-permute-done.23 = bf16[4,2,2,24,1664]{4,3,2,0,1:T(8,128)(2,1)S(1)} collective-permute-done((bf16[4,2,2,24,1664]{4,3,2,0,1:T(8,128)(2,1)S(1)}, bf16[4,2,2,24,1664]{4,3,2,0,1:T(8,128)(2,1)S(1)}, u32[]{:S(2)}, u32[]{:S(2)}) %collective-permute-start.23) | collective-permute-done | bytes 1277984 | tf_op jit(solution)/shard_map/ppermute | solution.py:76
  475.7 4.2 collective-permute-done.51
  481.8 1.8 collective-permute-done.24
  483.9 5.3 %collective-permute-start.25 = (bf16[2,24,1664]{2,1,0:T(8,128)(2,1)S(1)}, bf16[2,24,1664]{2,1,0:T(8,128)(2,1)S(1)}, u32[]{:S(2)}, u32[]{:S(2)}) collective-permute-start(bf16[2,24,1664]{2,1,0:T(8,128)(2,1)S(1)} %get-tuple-element.117), channel_id=1, source_target_pairs={{0,8},{8,16},{16,24},{24,0},{1,9},{9,17},{17,25},{25,1},{2,10},{10... | collective-permute-start | bytes 479240 | tf_op jit(solution)/shard_map/ppermute | solution.py:76
  490.0 2.8 collective-permute-start.27
  493.5 5.4 %collective-permute-done.26 = bf16[2,24,1664]{2,1,0:T(8,128)(2,1)S(1)} collective-permute-done((bf16[2,24,1664]{2,1,0:T(8,128)(2,1)S(1)}, bf16[2,24,1664]{2,1,0:T(8,128)(2,1)S(1)}, u32[]{:S(2)}, u32[]{:S(2)}) %collective-permute-start.26) | collective-permute-done | bytes 159776 | tf_op jit(solution)/shard_map/ppermute | solution.py:76
  (226 shorter events, 70.4 us)
Async XLA Ops:
  7.2 186.8 %all-gather.6.cloned.1.call-start = ((), (), s32[]{:S(2)}) async-start(), calls=%async_computation.9 | async-start | bytes 3440640 | tf_op jit(solution)/shard_map/all_gather | solution.py:947
  8.2 7.7 %collective-permute-start.14 = (bf16[96,384]{1,0:T(8,128)(2,1)S(1)}, bf16[96,384]{1,0:T(8,128)(2,1)S(1)}, u32[]{:S(2)}, u32[]{:S(2)}) collective-permute-start(bf16[96,384]{1,0:T(8,128)(2,1)S(1)} %get-tuple-element.133), channel_id=1, source_target_pairs={{0,1},{1,0},{2,3},{3,2},{4,5},{5,4},{6,7},{7,6},{8,9},{9,8},{10,11... | collective-permute-start | bytes 221192 | tf_op jit(solution)/shard_map/ppermute | solution.py:72
  9.6 12.9 %collective-permute-start.7 = (bf16[24,1536]{1,0:T(8,128)(2,1)S(1)}, bf16[24,1536]{1,0:T(8,128)(2,1)S(1)}, u32[]{:S(2)}, u32[]{:S(2)}) collective-permute-start(bf16[24,1536]{1,0:T(8,128)(2,1)S(1)} %get-tuple-element.135), channel_id=1, source_target_pairs={{0,1},{1,0},{2,3},{3,2},{4,5},{5,4},{6,7},{7,6},{8,9},{9,8},{10,11... | collective-permute-start | bytes 221192 | tf_op jit(solution)/shard_map/ppermute | solution.py:72
  12.5 11.0 %collective-permute-start = (bf16[24,1664]{1,0:T(8,128)(2,1)S(1)}, bf16[24,1664]{1,0:T(8,128)(2,1)S(1)}, u32[]{:S(2)}, u32[]{:S(2)}) collective-permute-start(bf16[24,1664]{1,0:T(8,128)(2,1)S(1)} %get-tuple-element.130), channel_id=1, source_target_pairs={{0,1},{1,0},{2,3},{3,2},{4,5},{5,4},{6,7},{7,6},{8,9},{9,8},{10,11... | collective-permute-start | bytes 239624 | tf_op jit(solution)/shard_map/ppermute | solution.py:72
  16.0 20.0 %collective-permute-start.15 = (bf16[2,96,384]{2,1,0:T(8,128)(2,1)S(1)}, bf16[2,96,384]{2,1,0:T(8,128)(2,1)S(1)}, u32[]{:S(2)}, u32[]{:S(2)}) collective-permute-start(bf16[2,96,384]{2,1,0:T(8,128)(2,1)S(1)} %maximum_select_fusion.17), channel_id=1, source_target_pairs={{0,8},{8,16},{16,24},{24,0},{1,9},{9,17},{17,25},{25,1},{2,10},{10... | collective-permute-start | bytes 442376 | tf_op jit(solution)/shard_map/ppermute | solution.py:76
  18.6 24.9 %collective-permute-start.16 = (bf16[2,96,384]{2,1,0:T(8,128)(2,1)S(1)}, bf16[2,96,384]{2,1,0:T(8,128)(2,1)S(1)}, u32[]{:S(2)}, u32[]{:S(2)}) collective-permute-start(bf16[2,96,384]{2,1,0:T(8,128)(2,1)S(1)} %maximum_select_fusion.17), channel_id=1, source_target_pairs={{0,16},{8,24},{16,0},{24,8},{1,17},{9,25},{17,1},{25,9},{2,18},{10... | collective-permute-start | bytes 442376 | tf_op jit(solution)/shard_map/ppermute | solution.py:76
  21.2 26.3 %collective-permute-start.17 = (bf16[2,96,384]{2,1,0:T(8,128)(2,1)S(1)}, bf16[2,96,384]{2,1,0:T(8,128)(2,1)S(1)}, u32[]{:S(2)}, u32[]{:S(2)}) collective-permute-start(bf16[2,96,384]{2,1,0:T(8,128)(2,1)S(1)} %maximum_select_fusion.17), channel_id=1, source_target_pairs={{0,24},{8,0},{16,8},{24,16},{1,25},{9,1},{17,9},{25,17},{2,26},{10... | collective-permute-start | bytes 442376 | tf_op jit(solution)/shard_map/ppermute | solution.py:76
  22.6 12.4 %collective-permute-start.8 = (bf16[2,24,1536]{2,1,0:T(8,128)(2,1)S(1)}, bf16[2,24,1536]{2,1,0:T(8,128)(2,1)S(1)}, u32[]{:S(2)}, u32[]{:S(2)}) collective-permute-start(bf16[2,24,1536]{2,1,0:T(8,128)(2,1)S(1)} %maximum_select_fusion.16), channel_id=1, source_target_pairs={{0,8},{8,16},{16,24},{24,0},{1,9},{9,17},{17,25},{25,1},{2,10},{10... | collective-permute-start | bytes 442376 | tf_op jit(solution)/shard_map/ppermute | solution.py:76
  23.5 25.0 %collective-permute-start.9 = (bf16[2,24,1536]{2,1,0:T(8,128)(2,1)S(1)}, bf16[2,24,1536]{2,1,0:T(8,128)(2,1)S(1)}, u32[]{:S(2)}, u32[]{:S(2)}) collective-permute-start(bf16[2,24,1536]{2,1,0:T(8,128)(2,1)S(1)} %maximum_select_fusion.16), channel_id=1, source_target_pairs={{0,16},{8,24},{16,0},{24,8},{1,17},{9,25},{17,1},{25,9},{2,18},{10... | collective-permute-start | bytes 442376 | tf_op jit(solution)/shard_map/ppermute | solution.py:76
  35.0 15.1 %collective-permute-start.10 = (bf16[2,24,1536]{2,1,0:T(8,128)(2,1)S(1)}, bf16[2,24,1536]{2,1,0:T(8,128)(2,1)S(1)}, u32[]{:S(2)}, u32[]{:S(2)}) collective-permute-start(bf16[2,24,1536]{2,1,0:T(8,128)(2,1)S(1)} %maximum_select_fusion.16), channel_id=1, source_target_pairs={{0,24},{8,0},{16,8},{24,16},{1,25},{9,1},{17,9},{25,17},{2,26},{10... | collective-permute-start | bytes 442376 | tf_op jit(solution)/shard_map/ppermute | solution.py:76
  36.0 18.9 %collective-permute-start.1 = (bf16[2,24,1664]{2,1,0:T(8,128)(2,1)S(1)}, bf16[2,24,1664]{2,1,0:T(8,128)(2,1)S(1)}, u32[]{:S(2)}, u32[]{:S(2)}) collective-permute-start(bf16[2,24,1664]{2,1,0:T(8,128)(2,1)S(1)} %maximum_select_fusion.15), channel_id=1, source_target_pairs={{0,8},{8,16},{16,24},{24,0},{1,9},{9,17},{17,25},{25,1},{2,10},{10... | collective-permute-start | bytes 479240 | tf_op jit(solution)/shard_map/ppermute | solution.py:76
  43.5 16.8 %collective-permute-start.2 = (bf16[2,24,1664]{2,1,0:T(8,128)(2,1)S(1)}, bf16[2,24,1664]{2,1,0:T(8,128)(2,1)S(1)}, u32[]{:S(2)}, u32[]{:S(2)}) collective-permute-start(bf16[2,24,1664]{2,1,0:T(8,128)(2,1)S(1)} %maximum_select_fusion.15), channel_id=1, source_target_pairs={{0,16},{8,24},{16,0},{24,8},{1,17},{9,25},{17,1},{25,9},{2,18},{10... | collective-permute-start | bytes 479240 | tf_op jit(solution)/shard_map/ppermute | solution.py:76
  47.5 12.8 %collective-permute-start.3 = (bf16[2,24,1664]{2,1,0:T(8,128)(2,1)S(1)}, bf16[2,24,1664]{2,1,0:T(8,128)(2,1)S(1)}, u32[]{:S(2)}, u32[]{:S(2)}) collective-permute-start(bf16[2,24,1664]{2,1,0:T(8,128)(2,1)S(1)} %maximum_select_fusion.15), channel_id=1, source_target_pairs={{0,24},{8,0},{16,8},{24,16},{1,25},{9,1},{17,9},{25,17},{2,26},{10... | collective-permute-start | bytes 479240 | tf_op jit(solution)/shard_map/ppermute | solution.py:76
  48.5 16.3 %collective-permute-start.18 = (bf16[4,2,96,384]{3,2,1,0:T(8,128)(2,1)S(1)}, bf16[4,2,96,384]{3,2,1,0:T(8,128)(2,1)S(1)}, u32[]{:S(2)}, u32[]{:S(2)}) collective-permute-start(bf16[4,2,96,384]{3,2,1,0:T(8,128)(2,1)S(1)} %bitcast_dynamic-update-slice_fusion.3), channel_id=1, source_target_pairs={{0,4},{4,0},{1,5},{5,1},{2,6},{6,2},{3,7},{7,3},{8,12},{12,8},{9,1... | collective-permute-start | bytes 1769480 | tf_op jit(solution)/shard_map/ppermute | solution.py:72
  50.1 16.5 %collective-permute-start.11 = (bf16[4,2,24,1536]{3,2,1,0:T(8,128)(2,1)S(1)}, bf16[4,2,24,1536]{3,2,1,0:T(8,128)(2,1)S(1)}, u32[]{:S(2)}, u32[]{:S(2)}) collective-permute-start(bf16[4,2,24,1536]{3,2,1,0:T(8,128)(2,1)S(1)} %bitcast_dynamic-update-slice_fusion.7), channel_id=1, source_target_pairs={{0,2},{2,0},{1,3},{3,1},{4,6},{6,4},{5,7},{7,5},{8,10},{10,8},{9,1... | collective-permute-start | bytes 1769480 | tf_op jit(solution)/shard_map/ppermute | solution.py:72
  60.3 18.2 %collective-permute-start.4 = (bf16[4,2,24,1664]{3,2,1,0:T(8,128)(2,1)S(1)}, bf16[4,2,24,1664]{3,2,1,0:T(8,128)(2,1)S(1)}, u32[]{:S(2)}, u32[]{:S(2)}) collective-permute-start(bf16[4,2,24,1664]{3,2,1,0:T(8,128)(2,1)S(1)} %bitcast_dynamic-update-slice_fusion), channel_id=1, source_target_pairs={{0,4},{4,0},{1,5},{5,1},{2,6},{6,2},{3,7},{7,3},{8,12},{12,8},{9,1... | collective-permute-start | bytes 1916936 | tf_op jit(solution)/shard_map/ppermute | solution.py:72
  65.1 29.0 %collective-permute-start.19 = (bf16[2,4,2,96,384]{4,3,2,1,0:T(8,128)(2,1)S(1)}, bf16[2,4,2,96,384]{4,3,2,1,0:T(8,128)(2,1)S(1)}, u32[]{:S(2)}, u32[]{:S(2)}) collective-permute-start(bf16[2,4,2,96,384]{4,3,2,1,0:T(8,128)(2,1)S(1)} %maximum_select_fusion.9), channel_id=1, source_target_pairs={{0,2},{2,0},{1,3},{3,1},{4,6},{6,4},{5,7},{7,5},{8,10},{10,8},{9,1... | collective-permute-start | bytes 3538952 | tf_op jit(solution)/shard_map/ppermute | solution.py:72
  66.8 34.6 %collective-permute-start.12 = (bf16[2,4,2,24,1536]{4,3,2,0,1:T(8,128)(2,1)S(1)}, bf16[2,4,2,24,1536]{4,3,2,0,1:T(8,128)(2,1)S(1)}, u32[]{:S(2)}, u32[]{:S(2)}) collective-permute-start(bf16[2,4,2,24,1536]{4,3,2,0,1:T(8,128)(2,1)S(1)} %maximum_select_fusion.7), channel_id=1, source_target_pairs={{0,4},{4,0},{1,5},{5,1},{2,6},{6,2},{3,7},{7,3},{8,12},{12,8},{9,1... | collective-permute-start | bytes 3538952 | tf_op jit(solution)/shard_map/ppermute | solution.py:72
  78.7 37.7 %collective-permute-start.5 = (bf16[2,4,2,24,1664]{4,3,2,0,1:T(8,128)(2,1)S(1)}, bf16[2,4,2,24,1664]{4,3,2,0,1:T(8,128)(2,1)S(1)}, u32[]{:S(2)}, u32[]{:S(2)}) collective-permute-start(bf16[2,4,2,24,1664]{4,3,2,0,1:T(8,128)(2,1)S(1)} %maximum_select_fusion.6), channel_id=1, source_target_pairs={{0,2},{2,0},{1,3},{3,1},{4,6},{6,4},{5,7},{7,5},{8,10},{10,8},{9,1... | collective-permute-start | bytes 3833864 | tf_op jit(solution)/shard_map/ppermute | solution.py:72
  96.2 25.8 %collective-permute-start.20 = (bf16[3072,384]{1,0:T(8,128)(2,1)}, bf16[3072,384]{1,0:T(8,128)(2,1)}, u32[]{:S(2)}, u32[]{:S(2)}) collective-permute-start(bf16[3072,384]{1,0:T(8,128)(2,1)} %bitcast.55), channel_id=1, source_target_pairs={{0,1},{1,0},{2,3},{3,2},{4,5},{5,4},{6,7},{7,6},{8,9},{9,8},{10,11... | collective-permute-start | bytes 7077896 | tf_op jit(solution)/shard_map/ppermute | solution.py:72
  103.1 26.7 %collective-permute-start.13 = (bf16[768,1536]{1,0:T(8,128)(2,1)}, bf16[768,1536]{1,0:T(8,128)(2,1)}, u32[]{:S(2)}, u32[]{:S(2)}) collective-permute-start(bf16[768,1536]{1,0:T(8,128)(2,1)} %bitcast.41), channel_id=1, source_target_pairs={{0,1},{1,0},{2,3},{3,2},{4,5},{5,4},{6,7},{7,6},{8,9},{9,8},{10,11... | collective-permute-start | bytes 7077896 | tf_op jit(solution)/shard_map/ppermute | solution.py:72
  116.8 20.9 %collective-permute-start.6 = (bf16[768,1664]{1,0:T(8,128)(2,1)S(1)}, bf16[768,1664]{1,0:T(8,128)(2,1)}, u32[]{:S(2)}, u32[]{:S(2)}) collective-permute-start(bf16[768,1664]{1,0:T(8,128)(2,1)S(1)} %bitcast.221), channel_id=1, source_target_pairs={{0,1},{1,0},{2,3},{3,2},{4,5},{5,4},{6,7},{7,6},{8,9},{9,8},{10,11... | collective-permute-start | bytes 7667720 | tf_op jit(solution)/shard_map/ppermute | solution.py:72
  116.8 27.5 %all-to-all-start = ((bf16[8,64,768]{2,1,0:T(8,128)(2,1)}), bf16[8,64,768]{2,1,0:T(8,128)(2,1)S(1)}, u32[]{:S(2)}, u32[]{:S(2)}) async-start(bf16[8,64,768]{2,1,0:T(8,128)(2,1)} %bitcast), calls=%async_computation | async-start | bytes 1572864 | tf_op jit(solution)/shard_map/all_to_all | solution.py:198
  121.3 72.7 %all-gather.4.cloned.1.call-start = ((), (), s32[]{:S(2)}) async-start(), calls=%async_computation.7 | async-start | bytes 3244032 | tf_op jit(solution)/shard_map/all_gather | solution.py:941
  144.3 30.7 %all-to-all-start.1 = ((bf16[8,64,768]{2,1,0:T(8,128)(2,1)}), bf16[8,64,768]{2,1,0:T(8,128)(2,1)S(1)}, u32[]{:S(2)}, u32[]{:S(2)}) async-start(bf16[8,64,768]{2,1,0:T(8,128)(2,1)} %bitcast.58), calls=%async_computation.1 | async-start | bytes 1572864 | tf_op jit(solution)/shard_map/all_to_all | solution.py:198
  175.0 19.0 %all-to-all-start.2 = ((bf16[4,32,4096]{2,1,0:T(8,128)(2,1)}), bf16[4,32,4096]{2,1,0:T(8,128)(2,1)S(1)}, u32[]{:S(2)}, u32[]{:S(2)}) async-start(bf16[4,32,4096]{2,1,0:T(8,128)(2,1)} %bitcast.62), calls=%async_computation.2 | async-start | bytes 2097152 | tf_op jit(solution)/shard_map/all_to_all | solution.py:198
  238.3 52.3 %all-to-all-start.3 = ((bf16[4,32,4096]{2,1,0:T(8,128)(2,1)}), bf16[4,32,4096]{2,1,0:T(8,128)(2,1)S(1)}, u32[]{:S(2)}, u32[]{:S(2)}) async-start(bf16[4,32,4096]{2,1,0:T(8,128)(2,1)} %bitcast.255), calls=%async_computation.3 | async-start | bytes 2097152 | tf_op jit(solution)/shard_map/all_to_all | solution.py:198
  290.2 27.7 %collective-permute-start.21 = (bf16[3072,384]{1,0:T(8,128)(2,1)}, bf16[3072,384]{1,0:T(8,128)(2,1)}, u32[]{:S(2)}, u32[]{:S(2)}) collective-permute-start(bf16[3072,384]{1,0:T(8,128)(2,1)} %get-tuple-element.90), channel_id=1, source_target_pairs={{0,1},{1,0},{2,3},{3,2},{4,5},{5,4},{6,7},{7,6},{8,9},{9,8},{10,11... | collective-permute-start | bytes 7077896 | tf_op jit(solution)/shard_map/ppermute | solution.py:72
  290.6 25.9 %all-to-all-start.5 = ((bf16[8,64,768]{2,1,0:T(8,128)(2,1)}), bf16[8,64,768]{2,1,0:T(8,128)(2,1)S(1)}, u32[]{:S(2)}, u32[]{:S(2)}) async-start(bf16[8,64,768]{2,1,0:T(8,128)(2,1)} %bitcast.71), calls=%async_computation.5 | async-start | bytes 1572864 | tf_op jit(solution)/shard_map/all_to_all | solution.py:198
  296.2 202.8 %reduce-scatter.2.cloned.1.call-start = ((), (), s32[]{:S(2)}) async-start(), calls=%async_computation.8 | async-start | bytes 3244032 | tf_op jit(solution)/shard_map/reduce_scatter | solution.py:986
  311.0 12.2 %collective-permute-start.29 = (bf16[768,1536]{1,0:T(8,128)(2,1)}, bf16[768,1536]{1,0:T(8,128)(2,1)}, u32[]{:S(2)}, u32[]{:S(2)}) collective-permute-start(bf16[768,1536]{1,0:T(8,128)(2,1)} %get-tuple-element.96), channel_id=1, source_target_pairs={{0,1},{1,0},{2,3},{3,2},{4,5},{5,4},{6,7},{7,6},{8,9},{9,8},{10,11... | collective-permute-start | bytes 7077896 | tf_op jit(solution)/shard_map/ppermute | solution.py:72
  321.3 41.3 %collective-permute-start.36 = (bf16[4,2,2,96,384]{4,3,2,1,0:T(8,128)(2,1)}, bf16[4,2,2,96,384]{4,3,2,1,0:T(8,128)(2,1)}, u32[]{:S(2)}, u32[]{:S(2)}) collective-permute-start(bf16[4,2,2,96,384]{4,3,2,1,0:T(8,128)(2,1)} %dynamic-slice_bitcast_fusion.1), channel_id=1, source_target_pairs={{0,2},{2,0},{1,3},{3,1},{4,6},{6,4},{5,7},{7,5},{8,10},{10,8},{9,1... | collective-permute-start | bytes 3538952 | tf_op jit(solution)/shard_map/ppermute | solution.py:76
  327.2 31.7 %collective-permute-start.30 = (bf16[4,2,2,24,1536]{4,3,2,1,0:T(8,128)(2,1)S(1)}, bf16[4,2,2,24,1536]{4,3,2,1,0:T(8,128)(2,1)}, u32[]{:S(2)}, u32[]{:S(2)}) collective-permute-start(bf16[4,2,2,24,1536]{4,3,2,1,0:T(8,128)(2,1)S(1)} %dynamic-slice_bitcast_fusion.2), channel_id=1, source_target_pairs={{0,4},{4,0},{1,5},{5,1},{2,6},{6,2},{3,7},{7,3},{8,12},{12,8},{9,1... | collective-permute-start | bytes 3538952 | tf_op jit(solution)/shard_map/ppermute | solution.py:76
  328.6 30.2 %copy-start.3 = (bf16[768,1536]{1,0:T(8,128)(2,1)S(1)}, bf16[768,1536]{1,0:T(8,128)(2,1)}, u32[]{:S(2)}) copy-start(bf16[768,1536]{1,0:T(8,128)(2,1)} %copy-done.2) | copy-start | bytes 7077892
  354.5 84.0 %collective-permute-start.22 = (bf16[768,1664]{1,0:T(8,128)(2,1)}, bf16[768,1664]{1,0:T(8,128)(2,1)}, u32[]{:S(2)}, u32[]{:S(2)}) collective-permute-start(bf16[768,1664]{1,0:T(8,128)(2,1)} %get-tuple-element.94), channel_id=1, source_target_pairs={{0,1},{1,0},{2,3},{3,2},{4,5},{5,4},{6,7},{7,6},{8,9},{9,8},{10,11... | collective-permute-start | bytes 7667720 | tf_op jit(solution)/shard_map/ppermute | solution.py:72
  354.5 38.0 %all-to-all-start.4 = ((bf16[8,64,768]{2,1,0:T(8,128)(2,1)}), bf16[8,64,768]{2,1,0:T(8,128)(2,1)}, u32[]{:S(2)}, u32[]{:S(2)}) async-start(bf16[8,64,768]{2,1,0:T(8,128)(2,1)} %bitcast.262), calls=%async_computation.4 | async-start | bytes 1572864 | tf_op jit(solution)/shard_map/all_to_all | solution.py:198
  360.7 34.2 %collective-permute-start.31 = (bf16[4,2,24,1536]{3,2,1,0:T(8,128)(2,1)S(1)}, bf16[4,2,24,1536]{3,2,1,0:T(8,128)(2,1)}, u32[]{:S(2)}, u32[]{:S(2)}) collective-permute-start(bf16[4,2,24,1536]{3,2,1,0:T(8,128)(2,1)S(1)} %dynamic-slice_bitcast_fusion.6), channel_id=1, source_target_pairs={{0,2},{2,0},{1,3},{3,1},{4,6},{6,4},{5,7},{7,5},{8,10},{10,8},{9,1... | collective-permute-start | bytes 1769480 | tf_op jit(solution)/shard_map/ppermute | solution.py:76
  390.4 29.8 %collective-permute-start.42 = (bf16[2,896,384]{2,1,0:T(8,128)(2,1)}, bf16[2,896,384]{2,1,0:T(8,128)(2,1)}, u32[]{:S(2)}, u32[]{:S(2)}) collective-permute-start(bf16[2,896,384]{2,1,0:T(8,128)(2,1)} %dynamic-slice_bitcast_fusion), channel_id=1, source_target_pairs={{0,1},{1,0},{2,3},{3,2},{4,5},{5,4},{6,7},{7,6},{8,9},{9,8},{10,11... | collective-permute-start | bytes 4128776 | tf_op jit(solution)/shard_map/ppermute | solution.py:76
  390.7 17.3 %collective-permute-start.37 = (bf16[4,2,96,384]{3,2,1,0:T(8,128)(2,1)S(1)}, bf16[4,2,96,384]{3,2,1,0:T(8,128)(2,1)}, u32[]{:S(2)}, u32[]{:S(2)}) collective-permute-start(bf16[4,2,96,384]{3,2,1,0:T(8,128)(2,1)S(1)} %dynamic-slice_bitcast_fusion.5), channel_id=1, source_target_pairs={{0,4},{4,0},{1,5},{5,1},{2,6},{6,2},{3,7},{7,3},{8,12},{12,8},{9,1... | collective-permute-start | bytes 1769480 | tf_op jit(solution)/shard_map/ppermute | solution.py:76
  396.1 24.1 %copy-start.7 = (bf16[4,28,32,384]{3,2,1,0:T(8,128)(2,1)S(1)}, bf16[4,28,32,384]{3,2,1,0:T(8,128)(2,1)}, u32[]{:S(2)}) copy-start(bf16[4,28,32,384]{3,2,1,0:T(8,128)(2,1)} %shard_map.373) | copy-start | bytes 8257540
  396.2 16.7 %collective-permute-start.32 = (bf16[2,24,1536]{2,1,0:T(8,128)(2,1)S(1)}, bf16[2,24,1536]{2,1,0:T(8,128)(2,1)S(1)}, u32[]{:S(2)}, u32[]{:S(2)}) collective-permute-start(bf16[2,24,1536]{2,1,0:T(8,128)(2,1)S(1)} %get-tuple-element.123), channel_id=1, source_target_pairs={{0,8},{8,16},{16,24},{24,0},{1,9},{9,17},{17,25},{25,1},{2,10},{10... | collective-permute-start | bytes 442376 | tf_op jit(solution)/shard_map/ppermute | solution.py:76
  397.7 15.5 %collective-permute-start.33 = (bf16[2,24,1536]{2,1,0:T(8,128)(2,1)S(1)}, bf16[2,24,1536]{2,1,0:T(8,128)(2,1)S(1)}, u32[]{:S(2)}, u32[]{:S(2)}) collective-permute-start(bf16[2,24,1536]{2,1,0:T(8,128)(2,1)S(1)} %get-tuple-element.125), channel_id=1, source_target_pairs={{0,16},{8,24},{16,0},{24,8},{1,17},{9,25},{17,1},{25,9},{2,18},{10... | collective-permute-start | bytes 442376 | tf_op jit(solution)/shard_map/ppermute | solution.py:76
  408.0 8.3 %collective-permute-start.34 = (bf16[2,24,1536]{2,1,0:T(8,128)(2,1)S(1)}, bf16[2,24,1536]{2,1,0:T(8,128)(2,1)S(1)}, u32[]{:S(2)}, u32[]{:S(2)}) collective-permute-start(bf16[2,24,1536]{2,1,0:T(8,128)(2,1)S(1)} %get-tuple-element.124), channel_id=1, source_target_pairs={{0,24},{8,0},{16,8},{24,16},{1,25},{9,1},{17,9},{25,17},{2,26},{10... | collective-permute-start | bytes 442376 | tf_op jit(solution)/shard_map/ppermute | solution.py:76
  412.8 9.3 %collective-permute-start.38 = (bf16[2,96,384]{2,1,0:T(8,128)(2,1)S(1)}, bf16[2,96,384]{2,1,0:T(8,128)(2,1)S(1)}, u32[]{:S(2)}, u32[]{:S(2)}) collective-permute-start(bf16[2,96,384]{2,1,0:T(8,128)(2,1)S(1)} %get-tuple-element.120), channel_id=1, source_target_pairs={{0,8},{8,16},{16,24},{24,0},{1,9},{9,17},{17,25},{25,1},{2,10},{10... | collective-permute-start | bytes 442376 | tf_op jit(solution)/shard_map/ppermute | solution.py:76
  413.2 14.5 %collective-permute-start.39 = (bf16[2,96,384]{2,1,0:T(8,128)(2,1)S(1)}, bf16[2,96,384]{2,1,0:T(8,128)(2,1)S(1)}, u32[]{:S(2)}, u32[]{:S(2)}) collective-permute-start(bf16[2,96,384]{2,1,0:T(8,128)(2,1)S(1)} %get-tuple-element.122), channel_id=1, source_target_pairs={{0,16},{8,24},{16,0},{24,8},{1,17},{9,25},{17,1},{25,9},{2,18},{10... | collective-permute-start | bytes 442376 | tf_op jit(solution)/shard_map/ppermute | solution.py:76
  416.3 11.6 %collective-permute-start.40 = (bf16[2,96,384]{2,1,0:T(8,128)(2,1)S(1)}, bf16[2,96,384]{2,1,0:T(8,128)(2,1)S(1)}, u32[]{:S(2)}, u32[]{:S(2)}) collective-permute-start(bf16[2,96,384]{2,1,0:T(8,128)(2,1)S(1)} %get-tuple-element.121), channel_id=1, source_target_pairs={{0,24},{8,0},{16,8},{24,16},{1,25},{9,1},{17,9},{25,17},{2,26},{10... | collective-permute-start | bytes 442376 | tf_op jit(solution)/shard_map/ppermute | solution.py:76
  422.0 14.9 %collective-permute-start.43 = (bf16[896,384]{1,0:T(8,128)(2,1)S(1)}, bf16[896,384]{1,0:T(8,128)(2,1)S(1)}, u32[]{:S(2)}, u32[]{:S(2)}) collective-permute-start(bf16[896,384]{1,0:T(8,128)(2,1)S(1)} %dynamic-slice_bitcast_fusion.3), channel_id=1, source_target_pairs={{0,2},{2,0},{1,3},{3,1},{4,6},{6,4},{5,7},{7,5},{8,10},{10,8},{9,1... | collective-permute-start | bytes 2064392 | tf_op jit(solution)/shard_map/ppermute | solution.py:76
  437.2 11.1 %collective-permute-start.44 = (bf16[4,112,384]{2,1,0:T(8,128)(2,1)S(1)}, bf16[4,112,384]{2,1,0:T(8,128)(2,1)S(1)}, u32[]{:S(2)}, u32[]{:S(2)}) collective-permute-start(bf16[4,112,384]{2,1,0:T(8,128)(2,1)S(1)} %dynamic-slice_bitcast_fusion.7), channel_id=1, source_target_pairs={{0,4},{4,0},{1,5},{5,1},{2,6},{6,2},{3,7},{7,3},{8,12},{12,8},{9,1... | collective-permute-start | bytes 1032200 | tf_op jit(solution)/shard_map/ppermute | solution.py:76
  441.2 30.0 %collective-permute-start.23 = (bf16[4,2,2,24,1664]{4,3,2,0,1:T(8,128)(2,1)S(1)}, bf16[4,2,2,24,1664]{4,3,2,0,1:T(8,128)(2,1)S(1)}, u32[]{:S(2)}, u32[]{:S(2)}) collective-permute-start(bf16[4,2,2,24,1664]{4,3,2,0,1:T(8,128)(2,1)S(1)} %bitcast.252), channel_id=1, source_target_pairs={{0,4},{4,0},{1,5},{5,1},{2,6},{6,2},{3,7},{7,3},{8,12},{12,8},{9,1... | collective-permute-start | bytes 3833864 | tf_op jit(solution)/shard_map/ppermute | solution.py:76
  448.4 6.5 %collective-permute-start.45 = (bf16[112,384]{1,0:T(8,128)(2,1)S(1)}, bf16[112,384]{1,0:T(8,128)(2,1)S(1)}, u32[]{:S(2)}, u32[]{:S(2)}) collective-permute-start(bf16[112,384]{1,0:T(8,128)(2,1)S(1)} %get-tuple-element.126), channel_id=1, source_target_pairs={{0,8},{8,16},{16,24},{24,0},{1,9},{9,17},{17,25},{25,1},{2,10},{10... | collective-permute-start | bytes 258056 | tf_op jit(solution)/shard_map/ppermute | solution.py:76
  448.9 7.2 %collective-permute-start.46 = (bf16[112,384]{1,0:T(8,128)(2,1)S(1)}, bf16[112,384]{1,0:T(8,128)(2,1)S(1)}, u32[]{:S(2)}, u32[]{:S(2)}) collective-permute-start(bf16[112,384]{1,0:T(8,128)(2,1)S(1)} %get-tuple-element.128), channel_id=1, source_target_pairs={{0,16},{8,24},{16,0},{24,8},{1,17},{9,25},{17,1},{25,9},{2,18},{10... | collective-permute-start | bytes 258056 | tf_op jit(solution)/shard_map/ppermute | solution.py:76
  449.9 6.2 %collective-permute-start.47 = (bf16[112,384]{1,0:T(8,128)(2,1)S(1)}, bf16[112,384]{1,0:T(8,128)(2,1)S(1)}, u32[]{:S(2)}, u32[]{:S(2)}) collective-permute-start(bf16[112,384]{1,0:T(8,128)(2,1)S(1)} %get-tuple-element.127), channel_id=1, source_target_pairs={{0,24},{8,0},{16,8},{24,16},{1,25},{9,1},{17,9},{25,17},{2,26},{10... | collective-permute-start | bytes 258056 | tf_op jit(solution)/shard_map/ppermute | solution.py:76
  452.6 5.2 %collective-permute-start.41 = (bf16[96,384]{1,0:T(8,128)(2,1)S(1)}, bf16[96,384]{1,0:T(8,128)(2,1)S(1)}, u32[]{:S(2)}, u32[]{:S(2)}) collective-permute-start(bf16[96,384]{1,0:T(8,128)(2,1)S(1)} %fusion.24), channel_id=1, source_target_pairs={{0,1},{1,0},{2,3},{3,2},{4,5},{5,4},{6,7},{7,6},{8,9},{9,8},{10,11... | collective-permute-start | bytes 221192 | tf_op jit(solution)/shard_map/ppermute | solution.py:72
  454.8 20.1 %collective-permute-start.35 = (bf16[24,1536]{1,0:T(8,128)(2,1)S(1)}, bf16[24,1536]{1,0:T(8,128)(2,1)S(1)}, u32[]{:S(2)}, u32[]{:S(2)}) collective-permute-start(bf16[24,1536]{1,0:T(8,128)(2,1)S(1)} %fusion.23), channel_id=1, source_target_pairs={{0,1},{1,0},{2,3},{3,2},{4,5},{5,4},{6,7},{7,6},{8,9},{9,8},{10,11... | collective-permute-start | bytes 221192 | tf_op jit(solution)/shard_map/ppermute | solution.py:72
  456.3 7.4 %collective-permute-start.48 = (bf16[112,384]{1,0:T(8,128)(2,1)S(1)}, bf16[112,384]{1,0:T(8,128)(2,1)S(1)}, u32[]{:S(2)}, u32[]{:S(2)}) collective-permute-start(bf16[112,384]{1,0:T(8,128)(2,1)S(1)} %get-tuple-element.110), channel_id=1, source_target_pairs={{0,8},{8,16},{16,24},{24,0},{1,9},{9,17},{17,25},{25,1},{2,10},{10... | collective-permute-start | bytes 258056 | tf_op jit(solution)/shard_map/ppermute | solution.py:76
  457.9 7.7 %collective-permute-start.49 = (bf16[112,384]{1,0:T(8,128)(2,1)S(1)}, bf16[112,384]{1,0:T(8,128)(2,1)S(1)}, u32[]{:S(2)}, u32[]{:S(2)}) collective-permute-start(bf16[112,384]{1,0:T(8,128)(2,1)S(1)} %get-tuple-element.110), channel_id=1, source_target_pairs={{0,16},{8,24},{16,0},{24,8},{1,17},{9,25},{17,1},{25,9},{2,18},{10... | collective-permute-start | bytes 258056 | tf_op jit(solution)/shard_map/ppermute | solution.py:76
  459.8 12.8 %collective-permute-start.50 = (bf16[112,384]{1,0:T(8,128)(2,1)S(1)}, bf16[112,384]{1,0:T(8,128)(2,1)S(1)}, u32[]{:S(2)}, u32[]{:S(2)}) collective-permute-start(bf16[112,384]{1,0:T(8,128)(2,1)S(1)} %get-tuple-element.110), channel_id=1, source_target_pairs={{0,24},{8,0},{16,8},{24,16},{1,25},{9,1},{17,9},{25,17},{2,26},{10... | collective-permute-start | bytes 258056 | tf_op jit(solution)/shard_map/ppermute | solution.py:76
  471.6 12.0 %collective-permute-start.24 = (bf16[4,2,24,1664]{3,2,1,0:T(8,128)(2,1)S(1)}, bf16[4,2,24,1664]{3,2,1,0:T(8,128)(2,1)S(1)}, u32[]{:S(2)}, u32[]{:S(2)}) collective-permute-start(bf16[4,2,24,1664]{3,2,1,0:T(8,128)(2,1)S(1)} %dynamic-slice_bitcast_fusion.4), channel_id=1, source_target_pairs={{0,2},{2,0},{1,3},{3,1},{4,6},{6,4},{5,7},{7,5},{8,10},{10,8},{9,1... | collective-permute-start | bytes 1916936 | tf_op jit(solution)/shard_map/ppermute | solution.py:76
  472.6 7.3 %collective-permute-start.51 = (bf16[4,112,384]{2,1,0:T(8,128)(2,1)S(1)}, bf16[4,112,384]{2,1,0:T(8,128)(2,1)S(1)}, u32[]{:S(2)}, u32[]{:S(2)}) collective-permute-start(bf16[4,112,384]{2,1,0:T(8,128)(2,1)S(1)} %bitcast_dynamic-update-slice_fusion.11), channel_id=1, source_target_pairs={{0,4},{4,0},{1,5},{5,1},{2,6},{6,2},{3,7},{7,3},{8,12},{12,8},{9,1... | collective-permute-start | bytes 1032200 | tf_op jit(solution)/shard_map/ppermute | solution.py:72
  483.9 21.5 %copy-start.6 = (bf16[4,32,4096]{2,1,0:T(8,128)(2,1)S(1)}, bf16[4,32,4096]{2,1,0:T(8,128)(2,1)}, u32[]{:S(2)}) copy-start(bf16[4,32,4096]{2,1,0:T(8,128)(2,1)} %copy-done.5) | copy-start | bytes 3145732
  483.9 9.6 %collective-permute-start.25 = (bf16[2,24,1664]{2,1,0:T(8,128)(2,1)S(1)}, bf16[2,24,1664]{2,1,0:T(8,128)(2,1)S(1)}, u32[]{:S(2)}, u32[]{:S(2)}) collective-permute-start(bf16[2,24,1664]{2,1,0:T(8,128)(2,1)S(1)} %get-tuple-element.117), channel_id=1, source_target_pairs={{0,8},{8,16},{16,24},{24,0},{1,9},{9,17},{17,25},{25,1},{2,10},{10... | collective-permute-start | bytes 479240 | tf_op jit(solution)/shard_map/ppermute | solution.py:76
  489.1 9.7 %collective-permute-start.26 = (bf16[2,24,1664]{2,1,0:T(8,128)(2,1)S(1)}, bf16[2,24,1664]{2,1,0:T(8,128)(2,1)S(1)}, u32[]{:S(2)}, u32[]{:S(2)}) collective-permute-start(bf16[2,24,1664]{2,1,0:T(8,128)(2,1)S(1)} %get-tuple-element.119), channel_id=1, source_target_pairs={{0,16},{8,24},{16,0},{24,8},{1,17},{9,25},{17,1},{25,9},{2,18},{10... | collective-permute-start | bytes 479240 | tf_op jit(solution)/shard_map/ppermute | solution.py:76
  490.0 8.8 %collective-permute-start.27 = (bf16[2,24,1664]{2,1,0:T(8,128)(2,1)S(1)}, bf16[2,24,1664]{2,1,0:T(8,128)(2,1)S(1)}, u32[]{:S(2)}, u32[]{:S(2)}) collective-permute-start(bf16[2,24,1664]{2,1,0:T(8,128)(2,1)S(1)} %get-tuple-element.118), channel_id=1, source_target_pairs={{0,24},{8,0},{16,8},{24,16},{1,25},{9,1},{17,9},{25,17},{2,26},{10... | collective-permute-start | bytes 479240 | tf_op jit(solution)/shard_map/ppermute | solution.py:76
  501.1 1.3 collective-permute-start.28
  (16 other events, 98.8 us)
Sparse Core Ops, SparseCore 0:
  16.0 28.6 all-gather.5
  125.6 68.3 all-gather.3
  314.3 120.5 reduce-scatter.1

commit v2 on v1

--- a/solution.py
+++ b/solution.py
@@ -462,7 +462,7 @@
     return 1.0 / (1.0 + jnp.exp(-values))
 
 
-UNROLL = 4
+UNROLL = 8
 PAIRS = 3
 
 

time: 516 us -> 509 us (0.986); the launches traced: 513 us -> 500 us
  Pallas kernels: 186 us -> 172 us
    pallas_call x9, Pallas kernels: 186 us -> 172 us  [local_call(): pl.pallas_call(skip_operands(kernel, len(operands), len(after)), out_shap...]
  transfers between devices with their start and end apart: 61 -> 61, of which waited for: 27 -> 28; matrix products, arithmetic and copies ran while one was open for 14% -> 15% of each run, Pallas kernels for 28% -> 28%
where the time goes in v2:
time: 509 us; the launch traced here: 500 us
  Pallas kernels  172 us (34%)
  waiting for transfers between devices  130 us (26%)
  starting transfers between devices  100 us (20%)
  other arithmetic  52.6 us (10%)
  local copies, waits for them, and re-layouts  29.6 us (6%)
  between operations  15 us (3%)
    pallas_call x9, Pallas kernels, local_call(): pl.pallas_call(skip_operands(kernel, len(operands), len(after)), out_shap...  172 us
    ppermute x33, waiting for transfers between devices, turn(): lax.ppermute(value, axis, [(k, (k + step) % size) for k in range(size)])  75.3 us
    ppermute x33, starting transfers between devices, turn(): lax.ppermute(value, axis, [(k, (k + step) % size) for k in range(size)])  58.3 us
    ppermute x19, waiting for transfers between devices, swap(): return lax.ppermute(value, axis, [(0, 1), (1, 0)])  48.7 us
    all_to_all x6, starting transfers between devices, swap_blocks(): return lax.all_to_all(value, axes, 0, 0, tiled=True)  28.2 us
    select_n x9, other arithmetic, keep_order(): jnp.where(place == 0, jnp.concatenate([first, second], axis), jnp.concate...  23.9 us
    ppermute x19, starting transfers between devices, swap(): return lax.ppermute(value, axis, [(0, 1), (1, 0)])  13.1 us
  transfers between devices with their start and end apart: 61, of which 28 were waited for; matrix products, arithmetic and copies ran while one was open for 15% of the time, Pallas kernels for 28%

profile of v2, /device:TPU:0, one launch (start us, length us, event | category | flops | bytes accessed | tf_op | source)
XLA Modules:
  0.0 500.3 jit_solution(4360358421507188124)
XLA Ops:
  13.8 2.0 pad_maximum_fusion.4
  16.0 2.7 collective-permute-start.15
  18.6 2.6 collective-permute-start.16
  24.0 10.9 %collective-permute-done.8 = bf16[2,24,1536]{2,1,0:T(8,128)(2,1)S(1)} collective-permute-done((bf16[2,24,1536]{2,1,0:T(8,128)(2,1)S(1)}, bf16[2,24,1536]{2,1,0:T(8,128)(2,1)S(1)}, u32[]{:S(2)}, u32[]{:S(2)}) %collective-permute-start.8) | collective-permute-done | bytes 147488 | tf_op jit(solution)/shard_map/ppermute | solution.py:76
  36.0 7.5 %collective-permute-start.1 = (bf16[2,24,1664]{2,1,0:T(8,128)(2,1)S(1)}, bf16[2,24,1664]{2,1,0:T(8,128)(2,1)S(1)}, u32[]{:S(2)}, u32[]{:S(2)}) collective-permute-start(bf16[2,24,1664]{2,1,0:T(8,128)(2,1)S(1)} %maximum_select_fusion.15), channel_id=1, source_target_pairs={{0,8},{8,16},{16,24},{24,0},{1,9},{9,17},{17,25},{25,1},{2,10},{10... | collective-permute-start | bytes 479240 | tf_op jit(solution)/shard_map/ppermute | solution.py:76
  43.5 4.0 collective-permute-start.2
  51.7 3.2 collective-permute-done.1
  54.9 5.3 %collective-permute-done.2 = bf16[2,24,1664]{2,1,0:T(8,128)(2,1)S(1)} collective-permute-done((bf16[2,24,1664]{2,1,0:T(8,128)(2,1)S(1)}, bf16[2,24,1664]{2,1,0:T(8,128)(2,1)S(1)}, u32[]{:S(2)}, u32[]{:S(2)}) %collective-permute-start.2) | collective-permute-done | bytes 159776 | tf_op jit(solution)/shard_map/ppermute | solution.py:76
  61.9 3.0 collective-permute-done.18
  68.9 9.6 %collective-permute-done.4 = bf16[4,2,24,1664]{3,2,1,0:T(8,128)(2,1)S(1)} collective-permute-done((bf16[4,2,24,1664]{3,2,1,0:T(8,128)(2,1)S(1)}, bf16[4,2,24,1664]{3,2,1,0:T(8,128)(2,1)S(1)}, u32[]{:S(2)}, u32[]{:S(2)}) %collective-permute-start.4) | collective-permute-done | bytes 639008 | tf_op jit(solution)/shard_map/ppermute | solution.py:72
  80.6 13.5 %collective-permute-done.19 = bf16[2,4,2,96,384]{4,3,2,1,0:T(8,128)(2,1)S(1)} collective-permute-done((bf16[2,4,2,96,384]{4,3,2,1,0:T(8,128)(2,1)S(1)}, bf16[2,4,2,96,384]{4,3,2,1,0:T(8,128)(2,1)S(1)}, u32[]{:S(2)}, u32[]{:S(2)}) %collective-permute-start.19) | collective-permute-done | bytes 1179680 | tf_op jit(solution)/shard_map/ppermute | solution.py:72
  96.4 5.0 collective-permute-done.12
  101.4 1.8 maximum_select_fusion.4
  103.1 13.3 %collective-permute-done.5 = bf16[2,4,2,24,1664]{4,3,2,0,1:T(8,128)(2,1)S(1)} collective-permute-done((bf16[2,4,2,24,1664]{4,3,2,0,1:T(8,128)(2,1)S(1)}, bf16[2,4,2,24,1664]{4,3,2,0,1:T(8,128)(2,1)S(1)}, u32[]{:S(2)}, u32[]{:S(2)}) %collective-permute-start.5) | collective-permute-done | bytes 1277984 | tf_op jit(solution)/shard_map/ppermute | solution.py:72
  116.8 4.4 all-to-all-start
  122.0 7.8 %maximum_select_fusion.2.refs_3_.refs_4_ = bf16[3072,768]{1,0:T(8,128)(2,1)} fusion(bf16[3072,384]{1,0:T(8,128)(2,1)} %collective-permute-done.20, bf16[3072,384]{1,0:T(8,128)(2,1)} %bitcast.55, pred[]{:T(512)S(6)} %eq.56), kind=kLoop, calls=%fused_computation.3 | loop fusion | flops 21233664 | bytes 9437185 | tf_op jit(solution)/shard_map/jit(_where)/select_n | solution.py:97
  129.8 7.8 %maximum_select_fusion.1.refs_2_.refs_5_ = bf16[768,3072]{1,0:T(8,128)(2,1)} fusion(bf16[768,1536]{1,0:T(8,128)(2,1)} %collective-permute-done.13, bf16[768,1536]{1,0:T(8,128)(2,1)} %bitcast.41, pred[]{:T(512)S(6)} %eq.56), kind=kLoop, calls=%fused_computation.2 | loop fusion | flops 21233664 | bytes 9437185 | tf_op jit(solution)/shard_map/jit(_where)/select_n | solution.py:97
  137.7 6.6 %maximum_select_fusion.refs_1_.refs_6_.refs_9_ = bf16[768,3328]{1,0:T(8,128)(2,1)} fusion(bf16[768,1664]{1,0:T(8,128)(2,1)} %collective-permute-done.6, bf16[768,1664]{1,0:T(8,128)(2,1)S(1)} %bitcast.222, pred[]{:T(512)S(6)} %eq.56), kind=kLoop, calls=%fused_computation | loop fusion | flops 23003136 | bytes 10223617 | tf_op jit(solution)/shard_map/jit(_where)/select_n | solution.py:97
  144.3 6.3 %all-to-all-start.1 = ((bf16[8,64,768]{2,1,0:T(8,128)(2,1)}), bf16[8,64,768]{2,1,0:T(8,128)(2,1)S(1)}, u32[]{:S(2)}, u32[]{:S(2)}) async-start(bf16[8,64,768]{2,1,0:T(8,128)(2,1)} %bitcast.58), calls=%async_computation.1 | async-start | bytes 1572864 | tf_op jit(solution)/shard_map/all_to_all | solution.py:198
  150.6 16.9 %shard_map.364 = (bf16[512,768]{1,0:T(8,128)(2,1)}, bf16[512,2304]{1,0:T(8,128)(2,1)}, bf16[12,512,512]{2,1,0:T(8,128)(2,1)}, bf16[512,768]{1,0:T(8,128)(2,1)}, ...) custom-call(bf16[512,768]{1,0:T(8,128)(2,1)} %bitcast.257, ...), custom_call_target="tpu_custom_call" | custom-call | flops 30000001024 | bytes 30000001024 | tf_op jit(solution)/shard_map/pallas_call | solution.py:771
  170.5 4.6 all-to-all-done.1
  175.1 4.0 all-to-all-start.2
  179.1 14.0 %shard_map.365 = (bf16[512,3072]{1,0:T(8,128)(2,1)}, bf16[512,3072]{1,0:T(8,128)(2,1)}, bf16[512,768]{1,0:T(8,128)(2,1)}) custom-call(bf16[512,768]{1,0:T(8,128)(2,1)} %get-tuple-element.61.refs_0_.refs_2_, f32[512,768]{1,0:T(8,128)} %get-tuple-element.62.refs_1_.refs_3_, bf16[768,3072]{1,0:T(8,128)(2,1)} %maximum_select_fusion.1.refs_2_.refs_5_, ...), custom_call_target="tpu_custom_call" | custom-call | flops 30000001024 | bytes 30000001024 | tf_op jit(solution)/shard_map/pallas_call | solution.py:771
  195.0 31.2 %shard_map.366 = (bf16[8,2,8,2,16,256]{5,4,3,2,1,0:T(8,128)(2,1)}, bf16[16,256,128]{2,1,0:T(8,128)(2,1)}, f32[16,256,128]{2,1,0:T(8,128)}, f32[1,128]{1,0:T(1,12...) custom-call(bf16[512,768]{1,0:T(8,128)(2,1)} %get-tuple-element.65.refs_0_.refs_2_, ...), custom_call_target="tpu_custom_call" | custom-call | flops 30000001024 | bytes 30000001024 | tf_op jit(solution)/shard_map/pallas_call | solution.py:771
  226.2 3.5 all-to-all-start.3
  229.7 25.3 %shard_map.367 = (bf16[16,256,128]{2,1,0:T(8,128)(2,1)}, bf16[512,1024]{1,0:T(8,128)(2,1)}, bf16[512,1024]{1,0:T(8,128)(2,1)}) custom-call(bf16[16,256,128]{2,1,0:T(8,128)(2,1)} %get-tuple-element.68.refs_0_, bf16[16,256,128]{2,1,0:T(8,128)(2,1)} %get-tuple-element.69.refs_1_.refs_4_, f32[16,256,128]{2,1,0:T(8,128)} %get-tuple-element.70.refs_2_, ...), custom_call_target="tpu_custom_call" | custom-call | flops 30000001024 | bytes 30000001024 | tf_op jit(solution)/shard_map/pallas_call | solution.py:771
  255.0 9.1 %shard_map.368 = (bf16[768,2048]{1,0:T(8,128)(2,1)}, bf16[512,768]{1,0:T(8,128)(2,1)}, f32[512,768]{1,0:T(8,128)}, bf16[512,768]{1,0:T(8,128)(2,1)}, f32[1,768]{1,0:T(1,128)}) custom-call(bf16[512,1024]{1,0:T(8,128)(2,1)} %get-tuple-element.72.refs_0_, bf16[512,1024]{1,0:T(8,128)(2,1)} %get-tuple-element.73.refs_1_, ...), custom_call_target="tpu_custom_call" | custom-call | flops 30000001024 | bytes 30000001024 | tf_op jit(solution)/shard_map/pallas_call | solution.py:771
  264.1 13.9 %shard_map.369 = (bf16[3072,384]{1,0:T(8,128)(2,1)}, bf16[3072,384]{1,0:T(8,128)(2,1)}, bf16[512,3072]{1,0:T(8,128)(2,1)}, f32[1,3072]{1,0:T(1,128)}) custom-call(s32[1]{0:T(128)} %bitcast.66.refs_0_, bf16[512,768]{1,0:T(8,128)(2,1)} %get-tuple-element.74.refs_1_, bf16[512,3072]{1,0:T(8,128)(2,1)} %get-tuple-element.75.refs_2_, ...), custom_call_target="tpu_custom_call" | custom-call | flops 30000001024 | bytes 30000001024 | tf_op jit(solution)/shard_map/pallas_call | solution.py:771
  278.5 5.5 %all-to-all-start.5 = ((bf16[8,64,768]{2,1,0:T(8,128)(2,1)}), bf16[8,64,768]{2,1,0:T(8,128)(2,1)S(1)}, u32[]{:S(2)}, u32[]{:S(2)}) async-start(bf16[8,64,768]{2,1,0:T(8,128)(2,1)} %bitcast.71), calls=%async_computation.5 | async-start | bytes 1572864 | tf_op jit(solution)/shard_map/all_to_all | solution.py:198
  284.5 14.6 %shard_map.370 = (bf16[768,1536]{1,0:T(8,128)(2,1)}, bf16[768,1536]{1,0:T(8,128)(2,1)}, f32[512,768]{1,0:T(8,128)}, bf16[512,768]{1,0:T(8,128)(2,1)}, bf16[512,768]{1,0:T(8,128)(2,1)}, /*index=5*/f32[8,768]{1,0:T(8,128)}) custom-call(s32[1]{0:T(128)} %bitcast.66.refs_0_, bf16[512,3072]{1,0:T(8,128)(2,1)} %get-tuple-element.77.refs_1_, ...), custom_call_target="tpu_custom_call" | custom-call | flops 30000001024 | bytes 30000001024 | tf_op jit(solution)/shard_map/pallas_call | solution.py:771
  305.7 2.3 add_convert_fusion.2
  309.2 2.0 collective-permute-start.36
  311.2 2.3 add_convert_fusion.1
  316.5 25.6 %shard_map.371 = (bf16[768,1664]{1,0:T(8,128)(2,1)}, bf16[768,1664]{1,0:T(8,128)(2,1)}, bf16[512,768]{1,0:T(8,128)(2,1)}) custom-call(s32[1]{0:T(128)} %bitcast.66.refs_0_, bf16[512,768]{1,0:T(8,128)(2,1)} %get-tuple-element.79.refs_1_, bf16[512,768]{1,0:T(8,128)(2,1)} %get-tuple-element.80.refs_2_, f32[512,768]{1,0:T(8,128)} %get-tuple-element.81.refs_3_, ...), custom_call_target="tpu_custom_call" | custom-call | flops 30000001024 | bytes 30000001024 | tf_op jit(solution)/shard_map/pallas_call | solution.py:771
  342.1 4.4 all-to-all-start.4
  346.6 1.8 fusion.3
  348.4 1.8 collective-permute-start.31
  350.3 2.6 fusion.2.refs_6_
  352.9 21.8 %shard_map.373 = bf16[4,28,32,384]{3,2,1,0:T(8,128)(2,1)} custom-call(bf16[16,256,128]{2,1,0:T(8,128)(2,1)} %get-tuple-element.68.refs_0_, bf16[16,256,128]{2,1,0:T(8,128)(2,1)} %get-tuple-element.98.refs_1_, bf16[16,256,128]{2,1,0:T(8,128)(2,1)} %get-tuple-element.99.refs_2_, bf16[16,256,256]{2,1,0:T(8,128)(2,1)} %bitcast.280, ...), custom_call_target="tpu_custom_call" | custom-call | flops 30000001024 | bytes 30000001024 | tf_op jit(solution)/shard_map/pallas_call | solution.py:771
  374.7 2.7 dynamic-slice_bitcast_fusion
  377.6 1.8 collective-permute-start.37
  379.4 2.4 bitcast_convert_fusion.1
  384.7 2.4 collective-permute-start.33
  387.1 7.8 %collective-permute-done.37 = bf16[4,2,96,384]{3,2,1,0:T(8,128)(2,1)} collective-permute-done((bf16[4,2,96,384]{3,2,1,0:T(8,128)(2,1)S(1)}, bf16[4,2,96,384]{3,2,1,0:T(8,128)(2,1)}, u32[]{:S(2)}, u32[]{:S(2)}) %collective-permute-start.37) | collective-permute-done | bytes 589856 | tf_op jit(solution)/shard_map/ppermute | solution.py:76
  394.9 3.6 collective-permute-start.34
  401.0 2.3 collective-permute-done.34
  403.2 3.8 collective-permute-start.40
  409.1 5.3 %collective-permute-done.39 = bf16[2,96,384]{2,1,0:T(8,128)(2,1)S(1)} collective-permute-done((bf16[2,96,384]{2,1,0:T(8,128)(2,1)S(1)}, bf16[2,96,384]{2,1,0:T(8,128)(2,1)S(1)}, u32[]{:S(2)}, u32[]{:S(2)}) %collective-permute-start.39) | collective-permute-done | bytes 147488 | tf_op jit(solution)/shard_map/ppermute | solution.py:76
  415.0 8.9 %collective-permute-done.43 = bf16[896,384]{1,0:T(8,128)(2,1)S(1)} collective-permute-done((bf16[896,384]{1,0:T(8,128)(2,1)S(1)}, bf16[896,384]{1,0:T(8,128)(2,1)S(1)}, u32[]{:S(2)}, u32[]{:S(2)}) %collective-permute-start.43) | collective-permute-done | bytes 688160 | tf_op jit(solution)/shard_map/ppermute | solution.py:76
  425.5 2.4 add_convert_fusion
  429.0 6.2 %collective-permute-done.44 = bf16[4,112,384]{2,1,0:T(8,128)(2,1)S(1)} collective-permute-done((bf16[4,112,384]{2,1,0:T(8,128)(2,1)S(1)}, bf16[4,112,384]{2,1,0:T(8,128)(2,1)S(1)}, u32[]{:S(2)}, u32[]{:S(2)}) %collective-permute-start.44) | collective-permute-done | bytes 344096 | tf_op jit(solution)/shard_map/ppermute | solution.py:76
  436.9 2.3 collective-permute-start.47
  439.3 2.5 collective-permute-done.45
  447.6 3.0 collective-permute-done.48
  450.7 1.9 collective-permute-done.49
  452.6 5.7 %collective-permute-done.23 = bf16[4,2,2,24,1664]{4,3,2,0,1:T(8,128)(2,1)S(1)} collective-permute-done((bf16[4,2,2,24,1664]{4,3,2,0,1:T(8,128)(2,1)S(1)}, bf16[4,2,2,24,1664]{4,3,2,0,1:T(8,128)(2,1)S(1)}, u32[]{:S(2)}, u32[]{:S(2)}) %collective-permute-start.23) | collective-permute-done | bytes 1277984 | tf_op jit(solution)/shard_map/ppermute | solution.py:76
  458.7 2.0 collective-permute-start.24
  460.7 1.8 collective-permute-start.51
  464.0 4.0 collective-permute-done.51
  469.9 2.5 collective-permute-done.24
  472.6 3.0 collective-permute-start.25
  476.4 1.8 collective-permute-start.27
  478.9 2.5 collective-permute-done.25
  481.3 4.6 collective-permute-done.26
  (226 shorter events, 73.6 us)
Async XLA Ops:
  7.2 186.9 %all-gather.6.cloned.1.call-start = ((), (), s32[]{:S(2)}) async-start(), calls=%async_computation.9 | async-start | bytes 3440640 | tf_op jit(solution)/shard_map/all_gather | solution.py:947
  8.2 7.7 %collective-permute-start.14 = (bf16[96,384]{1,0:T(8,128)(2,1)S(1)}, bf16[96,384]{1,0:T(8,128)(2,1)S(1)}, u32[]{:S(2)}, u32[]{:S(2)}) collective-permute-start(bf16[96,384]{1,0:T(8,128)(2,1)S(1)} %get-tuple-element.133), channel_id=1, source_target_pairs={{0,1},{1,0},{2,3},{3,2},{4,5},{5,4},{6,7},{7,6},{8,9},{9,8},{10,11... | collective-permute-start | bytes 221192 | tf_op jit(solution)/shard_map/ppermute | solution.py:72
  9.6 12.9 %collective-permute-start.7 = (bf16[24,1536]{1,0:T(8,128)(2,1)S(1)}, bf16[24,1536]{1,0:T(8,128)(2,1)S(1)}, u32[]{:S(2)}, u32[]{:S(2)}) collective-permute-start(bf16[24,1536]{1,0:T(8,128)(2,1)S(1)} %get-tuple-element.135), channel_id=1, source_target_pairs={{0,1},{1,0},{2,3},{3,2},{4,5},{5,4},{6,7},{7,6},{8,9},{9,8},{10,11... | collective-permute-start | bytes 221192 | tf_op jit(solution)/shard_map/ppermute | solution.py:72
  12.5 11.0 %collective-permute-start = (bf16[24,1664]{1,0:T(8,128)(2,1)S(1)}, bf16[24,1664]{1,0:T(8,128)(2,1)S(1)}, u32[]{:S(2)}, u32[]{:S(2)}) collective-permute-start(bf16[24,1664]{1,0:T(8,128)(2,1)S(1)} %get-tuple-element.130), channel_id=1, source_target_pairs={{0,1},{1,0},{2,3},{3,2},{4,5},{5,4},{6,7},{7,6},{8,9},{9,8},{10,11... | collective-permute-start | bytes 239624 | tf_op jit(solution)/shard_map/ppermute | solution.py:72
  16.0 20.0 %collective-permute-start.15 = (bf16[2,96,384]{2,1,0:T(8,128)(2,1)S(1)}, bf16[2,96,384]{2,1,0:T(8,128)(2,1)S(1)}, u32[]{:S(2)}, u32[]{:S(2)}) collective-permute-start(bf16[2,96,384]{2,1,0:T(8,128)(2,1)S(1)} %maximum_select_fusion.17), channel_id=1, source_target_pairs={{0,8},{8,16},{16,24},{24,0},{1,9},{9,17},{17,25},{25,1},{2,10},{10... | collective-permute-start | bytes 442376 | tf_op jit(solution)/shard_map/ppermute | solution.py:76
  18.6 24.9 %collective-permute-start.16 = (bf16[2,96,384]{2,1,0:T(8,128)(2,1)S(1)}, bf16[2,96,384]{2,1,0:T(8,128)(2,1)S(1)}, u32[]{:S(2)}, u32[]{:S(2)}) collective-permute-start(bf16[2,96,384]{2,1,0:T(8,128)(2,1)S(1)} %maximum_select_fusion.17), channel_id=1, source_target_pairs={{0,16},{8,24},{16,0},{24,8},{1,17},{9,25},{17,1},{25,9},{2,18},{10... | collective-permute-start | bytes 442376 | tf_op jit(solution)/shard_map/ppermute | solution.py:76
  21.2 26.3 %collective-permute-start.17 = (bf16[2,96,384]{2,1,0:T(8,128)(2,1)S(1)}, bf16[2,96,384]{2,1,0:T(8,128)(2,1)S(1)}, u32[]{:S(2)}, u32[]{:S(2)}) collective-permute-start(bf16[2,96,384]{2,1,0:T(8,128)(2,1)S(1)} %maximum_select_fusion.17), channel_id=1, source_target_pairs={{0,24},{8,0},{16,8},{24,16},{1,25},{9,1},{17,9},{25,17},{2,26},{10... | collective-permute-start | bytes 442376 | tf_op jit(solution)/shard_map/ppermute | solution.py:76
  22.6 12.4 %collective-permute-start.8 = (bf16[2,24,1536]{2,1,0:T(8,128)(2,1)S(1)}, bf16[2,24,1536]{2,1,0:T(8,128)(2,1)S(1)}, u32[]{:S(2)}, u32[]{:S(2)}) collective-permute-start(bf16[2,24,1536]{2,1,0:T(8,128)(2,1)S(1)} %maximum_select_fusion.16), channel_id=1, source_target_pairs={{0,8},{8,16},{16,24},{24,0},{1,9},{9,17},{17,25},{25,1},{2,10},{10... | collective-permute-start | bytes 442376 | tf_op jit(solution)/shard_map/ppermute | solution.py:76
  23.5 25.0 %collective-permute-start.9 = (bf16[2,24,1536]{2,1,0:T(8,128)(2,1)S(1)}, bf16[2,24,1536]{2,1,0:T(8,128)(2,1)S(1)}, u32[]{:S(2)}, u32[]{:S(2)}) collective-permute-start(bf16[2,24,1536]{2,1,0:T(8,128)(2,1)S(1)} %maximum_select_fusion.16), channel_id=1, source_target_pairs={{0,16},{8,24},{16,0},{24,8},{1,17},{9,25},{17,1},{25,9},{2,18},{10... | collective-permute-start | bytes 442376 | tf_op jit(solution)/shard_map/ppermute | solution.py:76
  35.0 15.1 %collective-permute-start.10 = (bf16[2,24,1536]{2,1,0:T(8,128)(2,1)S(1)}, bf16[2,24,1536]{2,1,0:T(8,128)(2,1)S(1)}, u32[]{:S(2)}, u32[]{:S(2)}) collective-permute-start(bf16[2,24,1536]{2,1,0:T(8,128)(2,1)S(1)} %maximum_select_fusion.16), channel_id=1, source_target_pairs={{0,24},{8,0},{16,8},{24,16},{1,25},{9,1},{17,9},{25,17},{2,26},{10... | collective-permute-start | bytes 442376 | tf_op jit(solution)/shard_map/ppermute | solution.py:76
  36.0 18.9 %collective-permute-start.1 = (bf16[2,24,1664]{2,1,0:T(8,128)(2,1)S(1)}, bf16[2,24,1664]{2,1,0:T(8,128)(2,1)S(1)}, u32[]{:S(2)}, u32[]{:S(2)}) collective-permute-start(bf16[2,24,1664]{2,1,0:T(8,128)(2,1)S(1)} %maximum_select_fusion.15), channel_id=1, source_target_pairs={{0,8},{8,16},{16,24},{24,0},{1,9},{9,17},{17,25},{25,1},{2,10},{10... | collective-permute-start | bytes 479240 | tf_op jit(solution)/shard_map/ppermute | solution.py:76
  43.5 16.8 %collective-permute-start.2 = (bf16[2,24,1664]{2,1,0:T(8,128)(2,1)S(1)}, bf16[2,24,1664]{2,1,0:T(8,128)(2,1)S(1)}, u32[]{:S(2)}, u32[]{:S(2)}) collective-permute-start(bf16[2,24,1664]{2,1,0:T(8,128)(2,1)S(1)} %maximum_select_fusion.15), channel_id=1, source_target_pairs={{0,16},{8,24},{16,0},{24,8},{1,17},{9,25},{17,1},{25,9},{2,18},{10... | collective-permute-start | bytes 479240 | tf_op jit(solution)/shard_map/ppermute | solution.py:76
  47.5 12.8 %collective-permute-start.3 = (bf16[2,24,1664]{2,1,0:T(8,128)(2,1)S(1)}, bf16[2,24,1664]{2,1,0:T(8,128)(2,1)S(1)}, u32[]{:S(2)}, u32[]{:S(2)}) collective-permute-start(bf16[2,24,1664]{2,1,0:T(8,128)(2,1)S(1)} %maximum_select_fusion.15), channel_id=1, source_target_pairs={{0,24},{8,0},{16,8},{24,16},{1,25},{9,1},{17,9},{25,17},{2,26},{10... | collective-permute-start | bytes 479240 | tf_op jit(solution)/shard_map/ppermute | solution.py:76
  48.5 16.3 %collective-permute-start.18 = (bf16[4,2,96,384]{3,2,1,0:T(8,128)(2,1)S(1)}, bf16[4,2,96,384]{3,2,1,0:T(8,128)(2,1)S(1)}, u32[]{:S(2)}, u32[]{:S(2)}) collective-permute-start(bf16[4,2,96,384]{3,2,1,0:T(8,128)(2,1)S(1)} %bitcast_dynamic-update-slice_fusion.3), channel_id=1, source_target_pairs={{0,4},{4,0},{1,5},{5,1},{2,6},{6,2},{3,7},{7,3},{8,12},{12,8},{9,1... | collective-permute-start | bytes 1769480 | tf_op jit(solution)/shard_map/ppermute | solution.py:72
  50.1 16.5 %collective-permute-start.11 = (bf16[4,2,24,1536]{3,2,1,0:T(8,128)(2,1)S(1)}, bf16[4,2,24,1536]{3,2,1,0:T(8,128)(2,1)S(1)}, u32[]{:S(2)}, u32[]{:S(2)}) collective-permute-start(bf16[4,2,24,1536]{3,2,1,0:T(8,128)(2,1)S(1)} %bitcast_dynamic-update-slice_fusion.7), channel_id=1, source_target_pairs={{0,2},{2,0},{1,3},{3,1},{4,6},{6,4},{5,7},{7,5},{8,10},{10,8},{9,1... | collective-permute-start | bytes 1769480 | tf_op jit(solution)/shard_map/ppermute | solution.py:72
  60.3 18.2 %collective-permute-start.4 = (bf16[4,2,24,1664]{3,2,1,0:T(8,128)(2,1)S(1)}, bf16[4,2,24,1664]{3,2,1,0:T(8,128)(2,1)S(1)}, u32[]{:S(2)}, u32[]{:S(2)}) collective-permute-start(bf16[4,2,24,1664]{3,2,1,0:T(8,128)(2,1)S(1)} %bitcast_dynamic-update-slice_fusion), channel_id=1, source_target_pairs={{0,4},{4,0},{1,5},{5,1},{2,6},{6,2},{3,7},{7,3},{8,12},{12,8},{9,1... | collective-permute-start | bytes 1916936 | tf_op jit(solution)/shard_map/ppermute | solution.py:72
  65.1 29.0 %collective-permute-start.19 = (bf16[2,4,2,96,384]{4,3,2,1,0:T(8,128)(2,1)S(1)}, bf16[2,4,2,96,384]{4,3,2,1,0:T(8,128)(2,1)S(1)}, u32[]{:S(2)}, u32[]{:S(2)}) collective-permute-start(bf16[2,4,2,96,384]{4,3,2,1,0:T(8,128)(2,1)S(1)} %maximum_select_fusion.9), channel_id=1, source_target_pairs={{0,2},{2,0},{1,3},{3,1},{4,6},{6,4},{5,7},{7,5},{8,10},{10,8},{9,1... | collective-permute-start | bytes 3538952 | tf_op jit(solution)/shard_map/ppermute | solution.py:72
  66.8 34.6 %collective-permute-start.12 = (bf16[2,4,2,24,1536]{4,3,2,0,1:T(8,128)(2,1)S(1)}, bf16[2,4,2,24,1536]{4,3,2,0,1:T(8,128)(2,1)S(1)}, u32[]{:S(2)}, u32[]{:S(2)}) collective-permute-start(bf16[2,4,2,24,1536]{4,3,2,0,1:T(8,128)(2,1)S(1)} %maximum_select_fusion.7), channel_id=1, source_target_pairs={{0,4},{4,0},{1,5},{5,1},{2,6},{6,2},{3,7},{7,3},{8,12},{12,8},{9,1... | collective-permute-start | bytes 3538952 | tf_op jit(solution)/shard_map/ppermute | solution.py:72
  78.7 37.7 %collective-permute-start.5 = (bf16[2,4,2,24,1664]{4,3,2,0,1:T(8,128)(2,1)S(1)}, bf16[2,4,2,24,1664]{4,3,2,0,1:T(8,128)(2,1)S(1)}, u32[]{:S(2)}, u32[]{:S(2)}) collective-permute-start(bf16[2,4,2,24,1664]{4,3,2,0,1:T(8,128)(2,1)S(1)} %maximum_select_fusion.6), channel_id=1, source_target_pairs={{0,2},{2,0},{1,3},{3,1},{4,6},{6,4},{5,7},{7,5},{8,10},{10,8},{9,1... | collective-permute-start | bytes 3833864 | tf_op jit(solution)/shard_map/ppermute | solution.py:72
  96.2 25.8 %collective-permute-start.20 = (bf16[3072,384]{1,0:T(8,128)(2,1)}, bf16[3072,384]{1,0:T(8,128)(2,1)}, u32[]{:S(2)}, u32[]{:S(2)}) collective-permute-start(bf16[3072,384]{1,0:T(8,128)(2,1)} %bitcast.55), channel_id=1, source_target_pairs={{0,1},{1,0},{2,3},{3,2},{4,5},{5,4},{6,7},{7,6},{8,9},{9,8},{10,11... | collective-permute-start | bytes 7077896 | tf_op jit(solution)/shard_map/ppermute | solution.py:72
  103.1 26.7 %collective-permute-start.13 = (bf16[768,1536]{1,0:T(8,128)(2,1)}, bf16[768,1536]{1,0:T(8,128)(2,1)}, u32[]{:S(2)}, u32[]{:S(2)}) collective-permute-start(bf16[768,1536]{1,0:T(8,128)(2,1)} %bitcast.41), channel_id=1, source_target_pairs={{0,1},{1,0},{2,3},{3,2},{4,5},{5,4},{6,7},{7,6},{8,9},{9,8},{10,11... | collective-permute-start | bytes 7077896 | tf_op jit(solution)/shard_map/ppermute | solution.py:72
  116.8 20.9 %collective-permute-start.6 = (bf16[768,1664]{1,0:T(8,128)(2,1)S(1)}, bf16[768,1664]{1,0:T(8,128)(2,1)}, u32[]{:S(2)}, u32[]{:S(2)}) collective-permute-start(bf16[768,1664]{1,0:T(8,128)(2,1)S(1)} %bitcast.221), channel_id=1, source_target_pairs={{0,1},{1,0},{2,3},{3,2},{4,5},{5,4},{6,7},{7,6},{8,9},{9,8},{10,11... | collective-permute-start | bytes 7667720 | tf_op jit(solution)/shard_map/ppermute | solution.py:72
  116.8 27.5 %all-to-all-start = ((bf16[8,64,768]{2,1,0:T(8,128)(2,1)}), bf16[8,64,768]{2,1,0:T(8,128)(2,1)S(1)}, u32[]{:S(2)}, u32[]{:S(2)}) async-start(bf16[8,64,768]{2,1,0:T(8,128)(2,1)} %bitcast), calls=%async_computation | async-start | bytes 1572864 | tf_op jit(solution)/shard_map/all_to_all | solution.py:198
  121.3 72.8 %all-gather.4.cloned.1.call-start = ((), (), s32[]{:S(2)}) async-start(), calls=%async_computation.7 | async-start | bytes 3244032 | tf_op jit(solution)/shard_map/all_gather | solution.py:941
  144.3 30.8 %all-to-all-start.1 = ((bf16[8,64,768]{2,1,0:T(8,128)(2,1)}), bf16[8,64,768]{2,1,0:T(8,128)(2,1)S(1)}, u32[]{:S(2)}, u32[]{:S(2)}) async-start(bf16[8,64,768]{2,1,0:T(8,128)(2,1)} %bitcast.58), calls=%async_computation.1 | async-start | bytes 1572864 | tf_op jit(solution)/shard_map/all_to_all | solution.py:198
  175.1 19.0 %all-to-all-start.2 = ((bf16[4,32,4096]{2,1,0:T(8,128)(2,1)}), bf16[4,32,4096]{2,1,0:T(8,128)(2,1)S(1)}, u32[]{:S(2)}, u32[]{:S(2)}) async-start(bf16[4,32,4096]{2,1,0:T(8,128)(2,1)} %bitcast.62), calls=%async_computation.2 | async-start | bytes 2097152 | tf_op jit(solution)/shard_map/all_to_all | solution.py:198
  226.2 52.3 %all-to-all-start.3 = ((bf16[4,32,4096]{2,1,0:T(8,128)(2,1)}), bf16[4,32,4096]{2,1,0:T(8,128)(2,1)S(1)}, u32[]{:S(2)}, u32[]{:S(2)}) async-start(bf16[4,32,4096]{2,1,0:T(8,128)(2,1)} %bitcast.255), calls=%async_computation.3 | async-start | bytes 2097152 | tf_op jit(solution)/shard_map/all_to_all | solution.py:198
  278.1 27.7 %collective-permute-start.21 = (bf16[3072,384]{1,0:T(8,128)(2,1)}, bf16[3072,384]{1,0:T(8,128)(2,1)}, u32[]{:S(2)}, u32[]{:S(2)}) collective-permute-start(bf16[3072,384]{1,0:T(8,128)(2,1)} %get-tuple-element.90), channel_id=1, source_target_pairs={{0,1},{1,0},{2,3},{3,2},{4,5},{5,4},{6,7},{7,6},{8,9},{9,8},{10,11... | collective-permute-start | bytes 7077896 | tf_op jit(solution)/shard_map/ppermute | solution.py:72
  278.5 20.6 %copy-start.5 = (bf16[4,32,4096]{2,1,0:T(8,128)(2,1)}, bf16[4,32,4096]{2,1,0:T(8,128)(2,1)S(1)}, u32[]{:S(2)}) copy-start(bf16[4,32,4096]{2,1,0:T(8,128)(2,1)S(1)} %all-to-all-done.3) | copy-start | bytes 3145732
  278.5 25.9 %all-to-all-start.5 = ((bf16[8,64,768]{2,1,0:T(8,128)(2,1)}), bf16[8,64,768]{2,1,0:T(8,128)(2,1)S(1)}, u32[]{:S(2)}, u32[]{:S(2)}) async-start(bf16[8,64,768]{2,1,0:T(8,128)(2,1)} %bitcast.71), calls=%async_computation.5 | async-start | bytes 1572864 | tf_op jit(solution)/shard_map/all_to_all | solution.py:198
  284.1 202.1 %reduce-scatter.2.cloned.1.call-start = ((), (), s32[]{:S(2)}) async-start(), calls=%async_computation.8 | async-start | bytes 3244032 | tf_op jit(solution)/shard_map/reduce_scatter | solution.py:986
  299.1 12.0 %collective-permute-start.29 = (bf16[768,1536]{1,0:T(8,128)(2,1)}, bf16[768,1536]{1,0:T(8,128)(2,1)}, u32[]{:S(2)}, u32[]{:S(2)}) collective-permute-start(bf16[768,1536]{1,0:T(8,128)(2,1)} %get-tuple-element.96), channel_id=1, source_target_pairs={{0,1},{1,0},{2,3},{3,2},{4,5},{5,4},{6,7},{7,6},{8,9},{9,8},{10,11... | collective-permute-start | bytes 7077896 | tf_op jit(solution)/shard_map/ppermute | solution.py:72
  309.2 41.1 %collective-permute-start.36 = (bf16[4,2,2,96,384]{4,3,2,1,0:T(8,128)(2,1)}, bf16[4,2,2,96,384]{4,3,2,1,0:T(8,128)(2,1)}, u32[]{:S(2)}, u32[]{:S(2)}) collective-permute-start(bf16[4,2,2,96,384]{4,3,2,1,0:T(8,128)(2,1)} %dynamic-slice_bitcast_fusion.1), channel_id=1, source_target_pairs={{0,2},{2,0},{1,3},{3,1},{4,6},{6,4},{5,7},{7,5},{8,10},{10,8},{9,1... | collective-permute-start | bytes 3538952 | tf_op jit(solution)/shard_map/ppermute | solution.py:76
  315.0 31.5 %collective-permute-start.30 = (bf16[4,2,2,24,1536]{4,3,2,1,0:T(8,128)(2,1)S(1)}, bf16[4,2,2,24,1536]{4,3,2,1,0:T(8,128)(2,1)}, u32[]{:S(2)}, u32[]{:S(2)}) collective-permute-start(bf16[4,2,2,24,1536]{4,3,2,1,0:T(8,128)(2,1)S(1)} %dynamic-slice_bitcast_fusion.2), channel_id=1, source_target_pairs={{0,4},{4,0},{1,5},{5,1},{2,6},{6,2},{3,7},{7,3},{8,12},{12,8},{9,1... | collective-permute-start | bytes 3538952 | tf_op jit(solution)/shard_map/ppermute | solution.py:76
  316.5 30.1 %copy-start.3 = (bf16[768,1536]{1,0:T(8,128)(2,1)S(1)}, bf16[768,1536]{1,0:T(8,128)(2,1)}, u32[]{:S(2)}) copy-start(bf16[768,1536]{1,0:T(8,128)(2,1)} %copy-done.2) | copy-start | bytes 7077892
  342.1 83.3 %collective-permute-start.22 = (bf16[768,1664]{1,0:T(8,128)(2,1)}, bf16[768,1664]{1,0:T(8,128)(2,1)}, u32[]{:S(2)}, u32[]{:S(2)}) collective-permute-start(bf16[768,1664]{1,0:T(8,128)(2,1)} %get-tuple-element.94), channel_id=1, source_target_pairs={{0,1},{1,0},{2,3},{3,2},{4,5},{5,4},{6,7},{7,6},{8,9},{9,8},{10,11... | collective-permute-start | bytes 7667720 | tf_op jit(solution)/shard_map/ppermute | solution.py:72
  342.1 37.3 %all-to-all-start.4 = ((bf16[8,64,768]{2,1,0:T(8,128)(2,1)}), bf16[8,64,768]{2,1,0:T(8,128)(2,1)}, u32[]{:S(2)}, u32[]{:S(2)}) async-start(bf16[8,64,768]{2,1,0:T(8,128)(2,1)} %bitcast.262), calls=%async_computation.4 | async-start | bytes 1572864 | tf_op jit(solution)/shard_map/all_to_all | solution.py:198
  348.4 33.4 %collective-permute-start.31 = (bf16[4,2,24,1536]{3,2,1,0:T(8,128)(2,1)S(1)}, bf16[4,2,24,1536]{3,2,1,0:T(8,128)(2,1)}, u32[]{:S(2)}, u32[]{:S(2)}) collective-permute-start(bf16[4,2,24,1536]{3,2,1,0:T(8,128)(2,1)S(1)} %dynamic-slice_bitcast_fusion.6), channel_id=1, source_target_pairs={{0,2},{2,0},{1,3},{3,1},{4,6},{6,4},{5,7},{7,5},{8,10},{10,8},{9,1... | collective-permute-start | bytes 1769480 | tf_op jit(solution)/shard_map/ppermute | solution.py:76
  377.3 29.8 %collective-permute-start.42 = (bf16[2,896,384]{2,1,0:T(8,128)(2,1)}, bf16[2,896,384]{2,1,0:T(8,128)(2,1)}, u32[]{:S(2)}, u32[]{:S(2)}) collective-permute-start(bf16[2,896,384]{2,1,0:T(8,128)(2,1)} %dynamic-slice_bitcast_fusion), channel_id=1, source_target_pairs={{0,1},{1,0},{2,3},{3,2},{4,5},{5,4},{6,7},{7,6},{8,9},{9,8},{10,11... | collective-permute-start | bytes 4128776 | tf_op jit(solution)/shard_map/ppermute | solution.py:76
  377.6 17.3 %collective-permute-start.37 = (bf16[4,2,96,384]{3,2,1,0:T(8,128)(2,1)S(1)}, bf16[4,2,96,384]{3,2,1,0:T(8,128)(2,1)}, u32[]{:S(2)}, u32[]{:S(2)}) collective-permute-start(bf16[4,2,96,384]{3,2,1,0:T(8,128)(2,1)S(1)} %dynamic-slice_bitcast_fusion.5), channel_id=1, source_target_pairs={{0,4},{4,0},{1,5},{5,1},{2,6},{6,2},{3,7},{7,3},{8,12},{12,8},{9,1... | collective-permute-start | bytes 1769480 | tf_op jit(solution)/shard_map/ppermute | solution.py:76
  383.1 24.1 %copy-start.7 = (bf16[4,28,32,384]{3,2,1,0:T(8,128)(2,1)S(1)}, bf16[4,28,32,384]{3,2,1,0:T(8,128)(2,1)}, u32[]{:S(2)}) copy-start(bf16[4,28,32,384]{3,2,1,0:T(8,128)(2,1)} %shard_map.373) | copy-start | bytes 8257540
  383.1 16.7 %collective-permute-start.32 = (bf16[2,24,1536]{2,1,0:T(8,128)(2,1)S(1)}, bf16[2,24,1536]{2,1,0:T(8,128)(2,1)S(1)}, u32[]{:S(2)}, u32[]{:S(2)}) collective-permute-start(bf16[2,24,1536]{2,1,0:T(8,128)(2,1)S(1)} %get-tuple-element.123), channel_id=1, source_target_pairs={{0,8},{8,16},{16,24},{24,0},{1,9},{9,17},{17,25},{25,1},{2,10},{10... | collective-permute-start | bytes 442376 | tf_op jit(solution)/shard_map/ppermute | solution.py:76
  384.7 15.5 %collective-permute-start.33 = (bf16[2,24,1536]{2,1,0:T(8,128)(2,1)S(1)}, bf16[2,24,1536]{2,1,0:T(8,128)(2,1)S(1)}, u32[]{:S(2)}, u32[]{:S(2)}) collective-permute-start(bf16[2,24,1536]{2,1,0:T(8,128)(2,1)S(1)} %get-tuple-element.125), channel_id=1, source_target_pairs={{0,16},{8,24},{16,0},{24,8},{1,17},{9,25},{17,1},{25,9},{2,18},{10... | collective-permute-start | bytes 442376 | tf_op jit(solution)/shard_map/ppermute | solution.py:76
  394.9 8.3 %collective-permute-start.34 = (bf16[2,24,1536]{2,1,0:T(8,128)(2,1)S(1)}, bf16[2,24,1536]{2,1,0:T(8,128)(2,1)S(1)}, u32[]{:S(2)}, u32[]{:S(2)}) collective-permute-start(bf16[2,24,1536]{2,1,0:T(8,128)(2,1)S(1)} %get-tuple-element.124), channel_id=1, source_target_pairs={{0,24},{8,0},{16,8},{24,16},{1,25},{9,1},{17,9},{25,17},{2,26},{10... | collective-permute-start | bytes 442376 | tf_op jit(solution)/shard_map/ppermute | solution.py:76
  399.8 9.3 %collective-permute-start.38 = (bf16[2,96,384]{2,1,0:T(8,128)(2,1)S(1)}, bf16[2,96,384]{2,1,0:T(8,128)(2,1)S(1)}, u32[]{:S(2)}, u32[]{:S(2)}) collective-permute-start(bf16[2,96,384]{2,1,0:T(8,128)(2,1)S(1)} %get-tuple-element.120), channel_id=1, source_target_pairs={{0,8},{8,16},{16,24},{24,0},{1,9},{9,17},{17,25},{25,1},{2,10},{10... | collective-permute-start | bytes 442376 | tf_op jit(solution)/shard_map/ppermute | solution.py:76
  400.2 14.1 %collective-permute-start.39 = (bf16[2,96,384]{2,1,0:T(8,128)(2,1)S(1)}, bf16[2,96,384]{2,1,0:T(8,128)(2,1)S(1)}, u32[]{:S(2)}, u32[]{:S(2)}) collective-permute-start(bf16[2,96,384]{2,1,0:T(8,128)(2,1)S(1)} %get-tuple-element.122), channel_id=1, source_target_pairs={{0,16},{8,24},{16,0},{24,8},{1,17},{9,25},{17,1},{25,9},{2,18},{10... | collective-permute-start | bytes 442376 | tf_op jit(solution)/shard_map/ppermute | solution.py:76
  403.2 11.7 %collective-permute-start.40 = (bf16[2,96,384]{2,1,0:T(8,128)(2,1)S(1)}, bf16[2,96,384]{2,1,0:T(8,128)(2,1)S(1)}, u32[]{:S(2)}, u32[]{:S(2)}) collective-permute-start(bf16[2,96,384]{2,1,0:T(8,128)(2,1)S(1)} %get-tuple-element.121), channel_id=1, source_target_pairs={{0,24},{8,0},{16,8},{24,16},{1,25},{9,1},{17,9},{25,17},{2,26},{10... | collective-permute-start | bytes 442376 | tf_op jit(solution)/shard_map/ppermute | solution.py:76
  408.9 15.0 %collective-permute-start.43 = (bf16[896,384]{1,0:T(8,128)(2,1)S(1)}, bf16[896,384]{1,0:T(8,128)(2,1)S(1)}, u32[]{:S(2)}, u32[]{:S(2)}) collective-permute-start(bf16[896,384]{1,0:T(8,128)(2,1)S(1)} %dynamic-slice_bitcast_fusion.3), channel_id=1, source_target_pairs={{0,2},{2,0},{1,3},{3,1},{4,6},{6,4},{5,7},{7,5},{8,10},{10,8},{9,1... | collective-permute-start | bytes 2064392 | tf_op jit(solution)/shard_map/ppermute | solution.py:76
  424.1 11.1 %collective-permute-start.44 = (bf16[4,112,384]{2,1,0:T(8,128)(2,1)S(1)}, bf16[4,112,384]{2,1,0:T(8,128)(2,1)S(1)}, u32[]{:S(2)}, u32[]{:S(2)}) collective-permute-start(bf16[4,112,384]{2,1,0:T(8,128)(2,1)S(1)} %dynamic-slice_bitcast_fusion.7), channel_id=1, source_target_pairs={{0,4},{4,0},{1,5},{5,1},{2,6},{6,2},{3,7},{7,3},{8,12},{12,8},{9,1... | collective-permute-start | bytes 1032200 | tf_op jit(solution)/shard_map/ppermute | solution.py:76
  428.2 30.1 %collective-permute-start.23 = (bf16[4,2,2,24,1664]{4,3,2,0,1:T(8,128)(2,1)S(1)}, bf16[4,2,2,24,1664]{4,3,2,0,1:T(8,128)(2,1)S(1)}, u32[]{:S(2)}, u32[]{:S(2)}) collective-permute-start(bf16[4,2,2,24,1664]{4,3,2,0,1:T(8,128)(2,1)S(1)} %bitcast.252), channel_id=1, source_target_pairs={{0,4},{4,0},{1,5},{5,1},{2,6},{6,2},{3,7},{7,3},{8,12},{12,8},{9,1... | collective-permute-start | bytes 3833864 | tf_op jit(solution)/shard_map/ppermute | solution.py:76
  435.3 6.5 %collective-permute-start.45 = (bf16[112,384]{1,0:T(8,128)(2,1)S(1)}, bf16[112,384]{1,0:T(8,128)(2,1)S(1)}, u32[]{:S(2)}, u32[]{:S(2)}) collective-permute-start(bf16[112,384]{1,0:T(8,128)(2,1)S(1)} %get-tuple-element.126), channel_id=1, source_target_pairs={{0,8},{8,16},{16,24},{24,0},{1,9},{9,17},{17,25},{25,1},{2,10},{10... | collective-permute-start | bytes 258056 | tf_op jit(solution)/shard_map/ppermute | solution.py:76
  436.2 7.2 %collective-permute-start.46 = (bf16[112,384]{1,0:T(8,128)(2,1)S(1)}, bf16[112,384]{1,0:T(8,128)(2,1)S(1)}, u32[]{:S(2)}, u32[]{:S(2)}) collective-permute-start(bf16[112,384]{1,0:T(8,128)(2,1)S(1)} %get-tuple-element.128), channel_id=1, source_target_pairs={{0,16},{8,24},{16,0},{24,8},{1,17},{9,25},{17,1},{25,9},{2,18},{10... | collective-permute-start | bytes 258056 | tf_op jit(solution)/shard_map/ppermute | solution.py:76
  436.9 6.5 %collective-permute-start.47 = (bf16[112,384]{1,0:T(8,128)(2,1)S(1)}, bf16[112,384]{1,0:T(8,128)(2,1)S(1)}, u32[]{:S(2)}, u32[]{:S(2)}) collective-permute-start(bf16[112,384]{1,0:T(8,128)(2,1)S(1)} %get-tuple-element.127), channel_id=1, source_target_pairs={{0,24},{8,0},{16,8},{24,16},{1,25},{9,1},{17,9},{25,17},{2,26},{10... | collective-permute-start | bytes 258056 | tf_op jit(solution)/shard_map/ppermute | solution.py:76
  439.2 5.9 %collective-permute-start.41 = (bf16[96,384]{1,0:T(8,128)(2,1)S(1)}, bf16[96,384]{1,0:T(8,128)(2,1)S(1)}, u32[]{:S(2)}, u32[]{:S(2)}) collective-permute-start(bf16[96,384]{1,0:T(8,128)(2,1)S(1)} %fusion.24), channel_id=1, source_target_pairs={{0,1},{1,0},{2,3},{3,2},{4,5},{5,4},{6,7},{7,6},{8,9},{9,8},{10,11... | collective-permute-start | bytes 221192 | tf_op jit(solution)/shard_map/ppermute | solution.py:72
  441.8 21.4 %collective-permute-start.35 = (bf16[24,1536]{1,0:T(8,128)(2,1)S(1)}, bf16[24,1536]{1,0:T(8,128)(2,1)S(1)}, u32[]{:S(2)}, u32[]{:S(2)}) collective-permute-start(bf16[24,1536]{1,0:T(8,128)(2,1)S(1)} %fusion.23), channel_id=1, source_target_pairs={{0,1},{1,0},{2,3},{3,2},{4,5},{5,4},{6,7},{7,6},{8,9},{9,8},{10,11... | collective-permute-start | bytes 221192 | tf_op jit(solution)/shard_map/ppermute | solution.py:72
  443.6 7.1 %collective-permute-start.48 = (bf16[112,384]{1,0:T(8,128)(2,1)S(1)}, bf16[112,384]{1,0:T(8,128)(2,1)S(1)}, u32[]{:S(2)}, u32[]{:S(2)}) collective-permute-start(bf16[112,384]{1,0:T(8,128)(2,1)S(1)} %get-tuple-element.110), channel_id=1, source_target_pairs={{0,8},{8,16},{16,24},{24,0},{1,9},{9,17},{17,25},{25,1},{2,10},{10... | collective-permute-start | bytes 258056 | tf_op jit(solution)/shard_map/ppermute | solution.py:76
  445.1 7.4 %collective-permute-start.49 = (bf16[112,384]{1,0:T(8,128)(2,1)S(1)}, bf16[112,384]{1,0:T(8,128)(2,1)S(1)}, u32[]{:S(2)}, u32[]{:S(2)}) collective-permute-start(bf16[112,384]{1,0:T(8,128)(2,1)S(1)} %get-tuple-element.110), channel_id=1, source_target_pairs={{0,16},{8,24},{16,0},{24,8},{1,17},{9,25},{17,1},{25,9},{2,18},{10... | collective-permute-start | bytes 258056 | tf_op jit(solution)/shard_map/ppermute | solution.py:76
  446.4 14.2 %collective-permute-start.50 = (bf16[112,384]{1,0:T(8,128)(2,1)S(1)}, bf16[112,384]{1,0:T(8,128)(2,1)S(1)}, u32[]{:S(2)}, u32[]{:S(2)}) collective-permute-start(bf16[112,384]{1,0:T(8,128)(2,1)S(1)} %get-tuple-element.110), channel_id=1, source_target_pairs={{0,24},{8,0},{16,8},{24,16},{1,25},{9,1},{17,9},{25,17},{2,26},{10... | collective-permute-start | bytes 258056 | tf_op jit(solution)/shard_map/ppermute | solution.py:76
  458.7 13.7 %collective-permute-start.24 = (bf16[4,2,24,1664]{3,2,1,0:T(8,128)(2,1)S(1)}, bf16[4,2,24,1664]{3,2,1,0:T(8,128)(2,1)S(1)}, u32[]{:S(2)}, u32[]{:S(2)}) collective-permute-start(bf16[4,2,24,1664]{3,2,1,0:T(8,128)(2,1)S(1)} %dynamic-slice_bitcast_fusion.4), channel_id=1, source_target_pairs={{0,2},{2,0},{1,3},{3,1},{4,6},{6,4},{5,7},{7,5},{8,10},{10,8},{9,1... | collective-permute-start | bytes 1916936 | tf_op jit(solution)/shard_map/ppermute | solution.py:76
  460.7 7.3 %collective-permute-start.51 = (bf16[4,112,384]{2,1,0:T(8,128)(2,1)S(1)}, bf16[4,112,384]{2,1,0:T(8,128)(2,1)S(1)}, u32[]{:S(2)}, u32[]{:S(2)}) collective-permute-start(bf16[4,112,384]{2,1,0:T(8,128)(2,1)S(1)} %bitcast_dynamic-update-slice_fusion.11), channel_id=1, source_target_pairs={{0,4},{4,0},{1,5},{5,1},{2,6},{6,2},{3,7},{7,3},{8,12},{12,8},{9,1... | collective-permute-start | bytes 1032200 | tf_op jit(solution)/shard_map/ppermute | solution.py:72
  472.6 8.7 %collective-permute-start.25 = (bf16[2,24,1664]{2,1,0:T(8,128)(2,1)S(1)}, bf16[2,24,1664]{2,1,0:T(8,128)(2,1)S(1)}, u32[]{:S(2)}, u32[]{:S(2)}) collective-permute-start(bf16[2,24,1664]{2,1,0:T(8,128)(2,1)S(1)} %get-tuple-element.117), channel_id=1, source_target_pairs={{0,8},{8,16},{16,24},{24,0},{1,9},{9,17},{17,25},{25,1},{2,10},{10... | collective-permute-start | bytes 479240 | tf_op jit(solution)/shard_map/ppermute | solution.py:76
  475.6 10.4 %collective-permute-start.26 = (bf16[2,24,1664]{2,1,0:T(8,128)(2,1)S(1)}, bf16[2,24,1664]{2,1,0:T(8,128)(2,1)S(1)}, u32[]{:S(2)}, u32[]{:S(2)}) collective-permute-start(bf16[2,24,1664]{2,1,0:T(8,128)(2,1)S(1)} %get-tuple-element.119), channel_id=1, source_target_pairs={{0,16},{8,24},{16,0},{24,8},{1,17},{9,25},{17,1},{25,9},{2,18},{10... | collective-permute-start | bytes 479240 | tf_op jit(solution)/shard_map/ppermute | solution.py:76
  476.4 9.5 %collective-permute-start.27 = (bf16[2,24,1664]{2,1,0:T(8,128)(2,1)S(1)}, bf16[2,24,1664]{2,1,0:T(8,128)(2,1)S(1)}, u32[]{:S(2)}, u32[]{:S(2)}) collective-permute-start(bf16[2,24,1664]{2,1,0:T(8,128)(2,1)S(1)} %get-tuple-element.118), channel_id=1, source_target_pairs={{0,24},{8,0},{16,8},{24,16},{1,25},{9,1},{17,9},{25,17},{2,26},{10... | collective-permute-start | bytes 479240 | tf_op jit(solution)/shard_map/ppermute | solution.py:76
  488.3 1.3 collective-permute-start.28
  (16 other events, 98.5 us)
Sparse Core Ops, SparseCore 0:
  16.0 28.6 all-gather.5
  125.6 68.1 all-gather.3
  302.3 120.0 reduce-scatter.1
